TPU v7x, 32 devices: a whole 2x2x4 slice. The times are simulated.
32 devices in a mesh: dp: 16 (over z, y, core), tensor: 2 (over x).
Axes of the slice: x: 2, y: 2, z: 4, core: 2. Of those that a mesh axis runs over, the one named last changes fastest.
Arguments:
- activations: bfloat16 [512, 16384], P('dp', 'tensor'), may hold values from -6 to 6
- weight: bfloat16 [16384, 16384], P('tensor', 'dp'), may hold values from -0.046875 to 0.046875
- out_grad: bfloat16 [512, 16384], P('tensor', 'dp'), may hold values from -6 to 6
Outputs:
- outputs: bfloat16 [512, 16384], P('tensor', 'dp')
- in_grad: bfloat16 [512, 16384], P('dp', 'tensor')
- weight_grad: float32 [16384, 16384], P('tensor', 'dp')
All inputs are finite; a program needn't handle non-finite values.
Results may differ from a plain program's by a relative error of at most 0.0049.
Values may be sent and summed in bfloat16 or wider, within the bound.
No kernel may reach another device: no remote copies, remote signals or barrier semaphores. Data moves between devices by JAX's collectives and lax.ppermute only.
A program may use at most 128 MiB of HBM per device.

v0:
```python
import math

import jax
import jax.numpy as jnp
from jax import lax
from jax.sharding import PartitionSpec as P


def from_partner(shard, axis, apart):
    return lax.ppermute(shard, axis, [(i, i ^ 1 << apart) for i in range(lax.axis_size(axis))])


def signs_table(width):
    position = jnp.arange(width, dtype=jnp.int32)
    joined = jnp.bitwise_and(position[:, None], position[None, :])
    parity = jnp.zeros_like(joined)
    for bit_number in range(width.bit_length() - 1):
        parity = parity + jnp.bitwise_and(jnp.right_shift(joined, bit_number), 1)
    return jnp.where(parity % 2 == 1, -1.0, 1.0).astype(jnp.float32)


def transform(values, width):
    bit_count = width.bit_length() - 1
    first_size = 2 ** (bit_count // 2)
    second = width // first_size
    shaped = values.reshape(values.shape[0], first_size, second)
    result = jnp.einsum(
        "rab,ac->rcb", shaped, signs_table(first_size), precision=lax.Precision.HIGHEST
    )
    result = jnp.einsum("rcb,bd->rcd", result, signs_table(second), precision=lax.Precision.HIGHEST)
    return result.reshape(values.shape[0], width)


def rotate_pairs(values, width):
    result = transform(values, width)
    position = lax.axis_index("tensor")
    for bit_number in range(lax.axis_size("tensor").bit_length() - 1):
        other = from_partner(result, "tensor", bit_number)
        upper = jnp.bitwise_and(jnp.right_shift(position, bit_number), 1) == 1
        result = jnp.where(upper, other - result, result + other)
    return result


def per_device(activations, weight, out_grad):
    tensor_size = lax.axis_size("tensor")
    local_width = activations.shape[1]
    full_width = local_width * tensor_size
    factor = 1.0 / math.sqrt(full_width)
    grad_count = out_grad.shape[0]
    token_total = grad_count * tensor_size
    rotated = (rotate_pairs(activations.astype(jnp.float32), local_width) * factor).astype(
        jnp.bfloat16
    )
    grad_all = lax.all_gather(out_grad, "tensor", axis=0, tiled=True)
    rows_all = lax.all_gather(rotated, "dp", axis=0, tiled=True)
    weight_grad = lax.dot_general(
        rows_all, grad_all, (((0,), (0,)), ((), ())), preferred_element_type=jnp.float32
    )
    outputs = lax.psum_scatter(
        jnp.dot(rows_all, weight, preferred_element_type=jnp.float32),
        "tensor",
        scatter_dimension=0,
        tiled=True,
    ).astype(jnp.bfloat16)
    weight_grad = weight_grad * (1.0 / math.sqrt(token_total))
    rotated_grad = lax.psum_scatter(
        lax.dot_general(
            grad_all, weight, (((1,), (1,)), ((), ())), preferred_element_type=jnp.float32
        ),
        "dp",
        scatter_dimension=0,
        tiled=True,
    )
    in_grad = (rotate_pairs(rotated_grad, local_width) * factor).astype(jnp.bfloat16)
    return (outputs, in_grad, weight_grad)


def solution(mesh):
    return jax.shard_map(
        per_device,
        mesh=mesh,
        in_specs=(P("dp", "tensor"), P("tensor", "dp"), P("tensor", "dp")),
        out_specs=(P("tensor", "dp"), P("dp", "tensor"), P("tensor", "dp")),
        check_vma=False,
    )
```

profile of v0, /device:TPU:0, one launch (start us, length us, event | category | flops | bytes accessed | tf_op | source)
XLA Modules:
  0.0 370.8 jit_solution(5138069714917787311)
XLA Ops:
  7.2 0.0 all-gather.5.cloned.1.call-start
  7.2 1.2 copy.6
  8.4 0.7 convolution_bitcast_fusion
  9.0 1.0 fusion.4
  10.1 0.6 copy.17
  10.7 3.0 collective-permute-start
  13.7 0.0 all-gather.5.cloned.1.call-update
  13.7 0.0 all-gather.3.cloned.1.call-start
  13.8 34.3 %collective-permute-done = f32[32,8192]{1,0:T(8,128)S(1)} collective-permute-done((f32[32,8192]{1,0:T(8,128)S(1)}, f32[32,8192]{1,0:T(8,128)S(1)}, u32[]{:S(2)}, u32[]{:S(2)}) %collective-permute-start) | collective-permute-done | bytes 1048608 | tf_op jit(solution)/shard_map/ppermute | solution.py:10
  48.1 1.5 multiply_convert_fusion.1
  49.5 0.0 all-gather.3.cloned.1.call-update
  49.6 0.0 reduce-scatter.5.cloned.1.call-start
  49.6 0.0 all-gather.5.cloned.1.call-done
  49.6 16.1 %fusion.61 = f32[512,8192]{1,0:T(8,128)} fusion(bf16[512,1024]{1,0:T(8,128)(2,1)} %all-gather.5.cloned.1.call-done, bf16[8192,1024]{1,0:T(8,128)(2,1)} %param.4), kind=kOutput, calls=%fused_computation.70 | convolution fusion | flops 8589934592 | bytes 34603008 | tf_op jit(solution)/shard_map/dot_general | solution.py:67
  65.8 0.0 reduce-scatter.5.cloned.1.call-update
  65.8 0.2 reduce-scatter.3.cloned.1.call-start
  66.0 60.1 %all-gather.3.cloned.1.call-done = bf16[512,8192]{1,0:T(8,128)(2,1)} async-done(((bf16[32,8192]{1,0:T(8,128)(2,1)}), bf16[512,8192]{1,0:T(8,128)(2,1)}) %all-gather.3.cloned.1.call-update) | async-done | bytes 8388624 | tf_op jit(solution)/shard_map/all_gather | solution.py:55
  126.1 16.0 %fusion.60 = f32[512,1024]{1,0:T(8,128)} fusion(bf16[512,8192]{1,0:T(8,128)(2,1)} %all-gather.3.cloned.1.call-done, bf16[8192,1024]{1,0:T(8,128)(2,1)} %param.4), kind=kOutput, calls=%fused_computation.69 | convolution fusion | flops 8589934592 | bytes 27262976 | tf_op jit(solution)/shard_map/dot_general | solution.py:60
  142.1 0.0 reduce-scatter.3.cloned.1.call-update
  142.1 165.6 %reduce-scatter.5.cloned.1.call-done = f32[32,8192]{1,0:T(8,128)} async-done(((f32[512,8192]{1,0:T(8,128)}), f32[32,8192]{1,0:T(8,128)}) %reduce-scatter.5.cloned.1.call-update) | async-done | bytes 1048592 | tf_op jit(solution)/shard_map/reduce_scatter | solution.py:66
  307.7 1.4 copy.8
  309.1 1.1 convolution_bitcast_fusion.1
  310.2 1.0 fusion.2
  311.2 0.6 copy.16
  311.8 1.5 collective-permute-start.1
  313.4 19.5 %broadcast_multiply_fusion = f32[8192,1024]{1,0:T(8,128)} fusion(bf16[512,8192]{1,0:T(8,128)(2,1)} %all-gather.3.cloned.1.call-done, bf16[512,1024]{1,0:T(8,128)(2,1)} %all-gather.5.cloned.1.call-done), kind=kOutput, calls=%fused_computation | convolution fusion | flops 8598323200 | bytes 42991616 | tf_op jit(solution)/shard_map/dot_general | solution.py:56
  332.9 27.9 %reduce-scatter.3.cloned.1.call-done = f32[256,1024]{1,0:T(8,128)} async-done(((f32[512,1024]{1,0:T(8,128)}), f32[256,1024]{1,0:T(8,128)}) %reduce-scatter.3.cloned.1.call-update) | async-done | bytes 1048592 | tf_op jit(solution)/shard_map/reduce_scatter | solution.py:59
  360.7 2.1 convert_element_type.11
  362.8 0.0 collective-permute-done.1
  362.8 1.5 multiply_convert_fusion
Async XLA Ops:
  7.2 42.5 %all-gather.5.cloned.1.call-start = ((), (), s32[]{:S(2)}) async-start(), calls=%async_computation.4 | async-start | bytes 1572864 | tf_op jit(solution)/shard_map/all_gather | solution.py:54
  10.7 37.4 %collective-permute-start = (f32[32,8192]{1,0:T(8,128)S(1)}, f32[32,8192]{1,0:T(8,128)S(1)}, u32[]{:S(2)}, u32[]{:S(2)}) collective-permute-start(f32[32,8192]{1,0:T(8,128)S(1)} %bitcast.46), channel_id=1, source_target_pairs={{0,1},{1,0},{2,3},{3,2},{4,5},{5,4},{6,7},{7,6},{8,9},{9,8},{10,11... | collective-permute-start | bytes 3145736 | tf_op jit(solution)/shard_map/ppermute | solution.py:10
  13.7 112.4 %all-gather.3.cloned.1.call-start = ((), (), s32[]{:S(2)}) async-start(), calls=%async_computation.2 | async-start | bytes 8912896 | tf_op jit(solution)/shard_map/all_gather | solution.py:55
  49.6 258.1 %reduce-scatter.5.cloned.1.call-start = ((), (), s32[]{:S(2)}) async-start(), calls=%async_computation.5 | async-start | bytes 17825792 | tf_op jit(solution)/shard_map/reduce_scatter | solution.py:66
  65.8 295.0 %reduce-scatter.3.cloned.1.call-start = ((), (), s32[]{:S(2)}) async-start(), calls=%async_computation.3 | async-start | bytes 3145728 | tf_op jit(solution)/shard_map/reduce_scatter | solution.py:59
  311.8 51.0 %collective-permute-start.1 = (f32[32,8192]{1,0:T(8,128)S(1)}, f32[32,8192]{1,0:T(8,128)S(1)}, u32[]{:S(2)}, u32[]{:S(2)}) collective-permute-start(f32[32,8192]{1,0:T(8,128)S(1)} %bitcast.48), channel_id=1, source_target_pairs={{0,1},{1,0},{2,3},{3,2},{4,5},{5,4},{6,7},{7,6},{8,9},{9,8},{10,11... | collective-permute-start | bytes 3145736 | tf_op jit(solution)/shard_map/ppermute | solution.py:10
Sparse Core Ops, SparseCore 0:
  13.8 32.9 all-gather.4
  49.7 76.3 all-gather.2
  130.8 176.8 reduce-scatter.4
  309.8 50.9 reduce-scatter.2
where the time goes:
time: 371 us
  waiting for transfers between devices  288 us (78%)
  matrix products  55.4 us (15%)
  between operations  13.8 us (4%)
  other arithmetic  5 us (1%)
  starting transfers between devices  4.88 us (1%)
  local copies, waits for them, and re-layouts  3.79 us (1%)
    reduce_scatter x1, waiting for transfers between devices, per_device(): lax.psum_scatter(lax.dot_general(grad_all, weight, (((1,), (1,)), ((), ()...  166 us
    all_gather x1, waiting for transfers between devices, per_device(): rows_all = lax.all_gather(rotated, 'dp', axis=0, tiled=True)  60.1 us
    ppermute x2, waiting for transfers between devices, from_partner(): lax.ppermute(shard, axis, [(i, i ^ 1 << apart) for i in range(lax.axis_si...  34.3 us
    reduce_scatter x1, waiting for transfers between devices, per_device(): lax.psum_scatter(jnp.dot(rows_all, weight, preferred_element_type=jnp.flo...  27.9 us
    dot_general x1, matrix products, per_device(): lax.dot_general(rows_all, grad_all, (((0,), (0,)), ((), ())), preferred_e...  19.5 us
    dot_general x1, matrix products, per_device(): lax.dot_general(grad_all, weight, (((1,), (1,)), ((), ())), preferred_ele...  16.1 us
    dot_general x1, matrix products, per_device(): jnp.dot(rows_all, weight, preferred_element_type=jnp.float32)  16 us
  transfers between devices with their start and end apart: 6, of which 4 were waited for; matrix products, arithmetic and copies ran while one was open for 16% of the time, Pallas kernels for 0%

commit v1 on v0

v1 whole, which is shorter than its diff:
```python
import functools
import math

import jax
import jax.numpy as jnp
from jax import lax
from jax.experimental import pallas as pl
from jax.experimental.pallas import tpu as pltpu
from jax.sharding import PartitionSpec as P

BF16 = jnp.bfloat16
F32 = jnp.float32
VMEM_LIMIT = 48 * 1024 * 1024


def swap(values, axis, mask):
    return lax.ppermute(values, axis, [(i, i ^ mask) for i in range(lax.axis_size(axis))])


def bit(number, place):
    return jnp.bitwise_and(jnp.right_shift(number, place), 1) == 1


def signs_table(width):
    position = jnp.arange(width, dtype=jnp.int32)
    joined = jnp.bitwise_and(position[:, None], position[None, :])
    parity = jnp.zeros_like(joined)
    for bit_number in range(width.bit_length() - 1):
        parity = parity + jnp.bitwise_and(jnp.right_shift(joined, bit_number), 1)
    return jnp.where(parity % 2 == 1, -1.0, 1.0).astype(F32)


def transform(values, width):
    bit_count = width.bit_length() - 1
    first_size = 2 ** (bit_count // 2)
    second = width // first_size
    shaped = values.reshape(values.shape[0], first_size, second)
    result = jnp.einsum(
        "rab,ac->rcb", shaped, signs_table(first_size), precision=lax.Precision.HIGHEST
    )
    result = jnp.einsum("rcb,bd->rcd", result, signs_table(second), precision=lax.Precision.HIGHEST)
    return result.reshape(values.shape[0], width)


def butterfly(values):
    position = lax.axis_index("tensor")
    result = values.astype(F32)
    for place in range(lax.axis_size("tensor").bit_length() - 1):
        other = swap(values.astype(BF16) if place == 0 else result, "tensor", 1 << place)
        other = other.astype(F32)
        result = jnp.where(bit(position, place), other - result, result + other)
    return result


def product_kernel(with_grad, with_out, has_sum, scale, *refs):
    refs = list(refs)
    even, odd = refs.pop(0), refs.pop(0)
    half = even.shape[0]
    if with_grad:
        cotangent = refs.pop(0)
    if with_out:
        weight = refs.pop(0)
    if has_sum:
        before = refs.pop(0)
    if with_grad:
        grad = refs[-2] if with_out else refs[-1]
        over_rows = (((0,), (0,)), ((), ()))
        total = lax.dot_general(
            even[...], cotangent[:half, :], over_rows, preferred_element_type=F32
        ) + lax.dot_general(odd[...], cotangent[half:, :], over_rows, preferred_element_type=F32)
        grad[...] = total * scale
    if with_out:
        out = refs[-1]

        @pl.when(pl.program_id(0) == 0)
        def _():
            out[...] = before[...] if has_sum else jnp.zeros_like(out)

        out[:half, :] += jnp.dot(even[...], weight[...], preferred_element_type=F32)
        out[half:, :] += jnp.dot(odd[...], weight[...], preferred_element_type=F32)


def product(even, odd, cotangent, weight, chunk, chunks, grad_before, sum_before, grad, out, scale):
    half, width = even.shape
    features, columns = weight.shape
    tile = min(512, width)
    steps = width // tile
    first = chunk * steps
    whole = lambda rows: pl.BlockSpec((rows, columns), lambda i: (0, 0))
    tall = pl.BlockSpec((tile, columns), lambda i: (first + i, 0))
    args, specs = [even, odd], [pl.BlockSpec((half, tile), lambda i: (0, i))] * 2
    aliases = {}
    if grad:
        args.append(cotangent)
        specs.append(whole(2 * half))
    if out:
        args.append(weight)
        specs.append(tall)
    if out and sum_before is not None:
        args.append(sum_before)
        specs.append(whole(2 * half))
    outs, out_specs = [], []
    if grad:
        if grad_before is not None:
            aliases[len(args)] = 0
            args.append(grad_before)
            specs.append(pl.BlockSpec(memory_space=pl.ANY))
        outs.append(jax.ShapeDtypeStruct((features, columns), F32))
        out_specs.append(tall)
    if out:
        outs.append(jax.ShapeDtypeStruct((2 * half, columns), F32))
        out_specs.append(whole(2 * half))
    kinds = int(grad) + int(out)
    return pl.pallas_call(
        functools.partial(product_kernel, grad, out, out and sum_before is not None, scale),
        grid=(steps,),
        in_specs=specs,
        out_specs=out_specs,
        out_shape=outs,
        input_output_aliases=aliases,
        compiler_params=pltpu.CompilerParams(vmem_limit_bytes=VMEM_LIMIT),
        cost_estimate=pl.CostEstimate(
            flops=kinds * 4 * half * width * columns,
            bytes_accessed=4 * half * width
            + (4 * width * columns if grad else 0)
            + (2 * width * columns if out else 0),
            transcendentals=0,
        ),
    )(*args)


def per_device(activations, weight, out_grad):
    dp, tensor = lax.axis_size("dp"), lax.axis_size("tensor")
    dp_bits, top_bits = dp.bit_length() - 1, tensor.bit_length() - 1
    low_bits = dp_bits - top_bits
    rows, width = activations.shape
    columns = weight.shape[1]
    me, mine = lax.axis_index("dp"), lax.axis_index("tensor")
    low_me = jnp.bitwise_and(me, (1 << low_bits) - 1)
    apart = jnp.bitwise_xor(jnp.right_shift(me, low_bits), mine)
    factor = 1.0 / math.sqrt(width * tensor)
    blocks = 1 << low_bits

    def reversed_bits(number):
        return sum((number >> b & 1) << (low_bits - 1 - b) for b in range(low_bits))

    def low_order(values, inverse=False):
        pieces = []
        for position in range(blocks):
            if inverse:
                source = sum(
                    jnp.bitwise_and(jnp.right_shift(jnp.bitwise_xor(low_me, position), b), 1)
                    << (low_bits - 1 - b)
                    for b in range(low_bits)
                )
            else:
                source = jnp.bitwise_xor(low_me, reversed_bits(position))
            pieces.append(lax.dynamic_slice_in_dim(values, source * rows, rows, 0))
        return jnp.concatenate(pieces, axis=0)

    def exchange_order(parts):
        for b in range(top_bits):
            flip = bit(apart, b)
            parts = [jnp.where(flip, parts[q ^ 1 << b], parts[q]) for q in range(tensor)]
        return parts

    rotated = (transform(butterfly(activations), width) * factor).astype(BF16)

    grads = [low_order(out_grad)]
    grads += [swap(grads[0], "tensor", q) for q in range(1, tensor)]

    sums = []
    for grad in grads:
        part = lax.dot_general(
            grad, weight, (((1,), (1,)), ((), ())), preferred_element_type=F32
        ).astype(BF16)
        part = part.reshape((2,) * low_bits + (rows, width))
        for place in range(low_bits):
            got = swap(part[1], "dp", 1 << place)
            part = part[0].astype(F32) + got.astype(F32)
            if place + 1 < low_bits:
                part = part.astype(BF16)
        sums.append(part)
    sums = exchange_order(sums)
    for place in reversed(range(top_bits)):
        count = 1 << place
        sums = [
            sums[j].astype(F32)
            + swap(sums[j + count].astype(BF16), "dp", count << low_bits).astype(F32)
            for j in range(count)
        ]
    rotated_grad = sums[0]

    ordered = exchange_order(grads)
    half = blocks * rows // 2
    cotangent = jnp.concatenate(
        [g[:half] for g in ordered] + [g[half:] for g in ordered], axis=0
    )
    chunks = 2
    chunk_width = width // chunks
    axes = [place for place in reversed(range(low_bits, dp_bits))] + list(range(1, low_bits))
    down = list(reversed(range(1, dp_bits)))
    up = list(reversed(range(low_bits, dp_bits))) + list(range(1, low_bits))
    grad_full, out_sum = None, None
    token_total = out_grad.shape[0] * tensor
    scale = 1.0 / math.sqrt(token_total)
    for chunk in range(chunks):
        got = rotated[:, chunk * chunk_width : (chunk + 1) * chunk_width]
        got = got.reshape((1,) * len(axes) + (rows, chunk_width))
        for place in down if chunk % 2 == 0 else up:
            got = jnp.concatenate([got, swap(got, "dp", 1 << place)], axis=axes.index(place))
        even = got.reshape(dp // 2 * rows, chunk_width)
        odd = swap(even, "dp", 1)
        call = functools.partial(
            product, even, odd, cotangent, weight, chunk, chunks, grad_full, out_sum, scale=scale
        )
        if chunk + 1 < chunks:
            grad_full, out_sum = call(grad=True, out=True)
        else:
            (out_sum,) = call(grad=False, out=True)
            (grad_full,) = call(grad=True, out=False)

    per_top = half
    parts = [
        jnp.concatenate(
            [
                out_sum[j * per_top : (j + 1) * per_top],
                out_sum[(tensor + j) * per_top : (tensor + j + 1) * per_top],
            ],
            axis=0,
        )
        for j in range(tensor)
    ]
    parts = exchange_order(parts)
    total = parts[0]
    for q in range(1, tensor):
        total = total + swap(parts[q].astype(BF16), "tensor", q).astype(F32)
    outputs = low_order(total.astype(BF16), inverse=True)

    in_grad = (transform(butterfly(rotated_grad), width) * factor).astype(BF16)
    return (outputs, in_grad, grad_full)


def solution(mesh):
    return jax.shard_map(
        per_device,
        mesh=mesh,
        in_specs=(P("dp", "tensor"), P("tensor", "dp"), P("tensor", "dp")),
        out_specs=(P("tensor", "dp"), P("dp", "tensor"), P("tensor", "dp")),
        check_vma=False,
    )
```

time: 371 us -> 204 us (0.55)
  waiting for transfers between devices: 288 us -> 101 us
  matrix products: 55.4 us -> 20.9 us
  Pallas kernels: 0 us -> 33.3 us
  starting transfers between devices: 4.88 us -> 25 us
  between operations: 13.8 us -> 1 us
  local copies, waits for them, and re-layouts: 3.79 us -> 14.1 us
    reduce_scatter x2 -> x0, waiting for transfers between devices: 193 us -> none  [the longest x1 166 us: per_device(): lax.psum_scatter(lax.dot_general(grad_all, weight, (((1,), (1,)), ((), ()...]
    ppermute x2 -> x19, waiting for transfers between devices: 34.3 us -> 101 us  [swap(): lax.ppermute(values, axis, [(i, i ^ mask) for i in range(lax.axis_size(ax...]
    all_gather x2 -> x0, waiting for transfers between devices: 60.1 us -> none  [the longest x1 60.1 us: per_device(): rows_all = lax.all_gather(rotated, 'dp', axis=0, tiled=True)]
    dot_general x3 -> x2, matrix products: 51.6 us -> 16.6 us  [per_device(): lax.dot_general(grad, weight, (((1,), (1,)), ((), ())), preferred_element...]
    pallas_call x0 -> x3, Pallas kernels: none -> 33.3 us  [product(): pl.pallas_call(functools.partial(product_kernel, grad, out, out and sum_b...]
    ppermute x2 -> x19, starting transfers between devices: 4.54 us -> 25 us  [swap(): lax.ppermute(values, axis, [(i, i ^ mask) for i in range(lax.axis_size(ax...]
    unnamed x4 -> x28, local copies, waits for them, and re-layouts: 3.79 us -> 10.5 us
  transfers between devices with their start and end apart: 6 -> 19, of which waited for: 4 -> 8; matrix products, arithmetic and copies ran while one was open for 16% -> 18% of each run, Pallas kernels for 0% -> 16%
where the time goes in v1:
time: 204 us; the launch traced here: 203 us
  waiting for transfers between devices  101 us (50%)
  Pallas kernels  33.3 us (16%)
  starting transfers between devices  25 us (12%)
  matrix products  20.9 us (10%)
  local copies, waits for them, and re-layouts  14.1 us (7%)
  other arithmetic  7.63 us (4%)
    ppermute x19, waiting for transfers between devices, swap(): lax.ppermute(values, axis, [(i, i ^ mask) for i in range(lax.axis_size(ax...  101 us
    pallas_call x3, Pallas kernels, product(): pl.pallas_call(functools.partial(product_kernel, grad, out, out and sum_b...  33.3 us
    ppermute x19, starting transfers between devices, swap(): lax.ppermute(values, axis, [(i, i ^ mask) for i in range(lax.axis_size(ax...  25 us
    dot_general x2, matrix products, per_device(): lax.dot_general(grad, weight, (((1,), (1,)), ((), ())), preferred_element...  16.6 us
    unnamed x28, local copies, waits for them, and re-layouts  10.5 us
  transfers between devices with their start and end apart: 19, of which 8 were waited for; matrix products, arithmetic and copies ran while one was open for 18% of the time, Pallas kernels for 16%

profile of v1, /device:TPU:0, one launch (start us, length us, event | category | flops | bytes accessed | tf_op | source)
XLA Modules:
  0.0 203.0 jit_solution(59241207942108059)
XLA Ops:
  0.6 3.0 %collective-permute-start = (bf16[32,8192]{1,0:T(8,128)(2,1)}, bf16[32,8192]{1,0:T(8,128)(2,1)}, u32[]{:S(2)}, u32[]{:S(2)}) collective-permute-start(bf16[32,8192]{1,0:T(8,128)(2,1)} %param.3), channel_id=1, source_target_pairs={{0,1},{1,0},{2,3},{3,2},{4,5},{5,4},{6,7},{7,6},{8,9},{9,8},{10,11... | collective-permute-start | bytes 1572872 | tf_op jit(solution)/shard_map/ppermute | solution.py:17
  10.5 8.2 %convolution_convert_fusion = bf16[256,8192]{1,0:T(8,128)(2,1)S(1)} fusion(bf16[256,1024]{1,0:T(8,128)(2,1)S(1)} %dynamic-slice_dynamic-update-slice_fusion.8, bf16[8192,1024]{1,0:T(8,128)(2,1)} %refs_2_.1), kind=kOutput, calls=%fused_computation | convolution fusion | flops 4297064448 | bytes 21495808 | tf_op jit(solution)/shard_map/dot_general | solution.py:174
  18.6 1.7 fusion.69
  20.3 1.2 fusion.7
  21.7 1.1 convolution_bitcast_fusion.1
  22.8 1.0 fusion.4
  24.3 3.1 %collective-permute-start.1 = (bf16[1,1,1,32,4096]{4,3,2,1,0:T(8,128)(2,1)S(1)}, bf16[1,1,1,32,4096]{4,3,2,1,0:T(8,128)(2,1)S(1)}, u32[]{:S(2)}, u32[]{:S(2)}) collective-permute-start(bf16[1,1,1,32,4096]{4,3,2,1,0:T(8,128)(2,1)S(1)} %get-tuple-element.22), channel_id=1, source_target_pairs={{0,16},{2,18},{4,20},{6,22},{8,24},{10,26},{12,28},{14,30},{16,0},... | collective-permute-start | bytes 786440 | tf_op jit(solution)/shard_map/ppermute | solution.py:17
  27.5 8.5 %convolution_convert_fusion.1 = bf16[256,8192]{1,0:T(8,128)(2,1)S(1)} fusion(bf16[256,1024]{1,0:T(8,128)(2,1)} %collective-permute-done.9, bf16[8192,1024]{1,0:T(8,128)(2,1)} %refs_2_.1), kind=kOutput, calls=%fused_computation.1 | convolution fusion | flops 4297064448 | bytes 21495808 | tf_op jit(solution)/shard_map/dot_general | solution.py:174
  36.7 1.1 broadcast_select_fusion.1
  37.9 7.9 %collective-permute-done.1 = bf16[1,1,1,32,4096]{4,3,2,1,0:T(8,128)(2,1)S(1)} collective-permute-done((bf16[1,1,1,32,4096]{4,3,2,1,0:T(8,128)(2,1)S(1)}, bf16[1,1,1,32,4096]{4,3,2,1,0:T(8,128)(2,1)S(1)}, u32[]{:S(2)}, u32[]{:S(2)}) %collective-permute-start.1) | collective-permute-done | bytes 262176 | tf_op jit(solution)/shard_map/ppermute | solution.py:17
  45.8 1.8 collective-permute-start.2
  47.7 3.5 %collective-permute-done.5 = bf16[1,1,1,32,4096]{4,3,2,1,0:T(8,128)(2,1)S(1)} collective-permute-done((bf16[1,1,1,32,4096]{4,3,2,1,0:T(8,128)(2,1)S(1)}, bf16[1,1,1,32,4096]{4,3,2,1,0:T(8,128)(2,1)S(1)}, u32[]{:S(2)}, u32[]{:S(2)}) %collective-permute-start.5) | collective-permute-done | bytes 262176 | tf_op jit(solution)/shard_map/ppermute | solution.py:17
  52.2 7.3 %collective-permute-done.2 = bf16[2,1,1,32,4096]{4,3,2,1,0:T(8,128)(2,1)S(1)} collective-permute-done((bf16[2,1,1,32,4096]{4,3,2,1,0:T(8,128)(2,1)S(1)}, bf16[2,1,1,32,4096]{4,3,2,1,0:T(8,128)(2,1)S(1)}, u32[]{:S(2)}, u32[]{:S(2)}) %collective-permute-start.2) | collective-permute-done | bytes 524320 | tf_op jit(solution)/shard_map/ppermute | solution.py:17
  60.5 5.6 %collective-permute-done.6 = bf16[2,1,1,32,4096]{4,3,2,1,0:T(8,128)(2,1)S(1)} collective-permute-done((bf16[2,1,1,32,4096]{4,3,2,1,0:T(8,128)(2,1)S(1)}, bf16[2,1,1,32,4096]{4,3,2,1,0:T(8,128)(2,1)S(1)}, u32[]{:S(2)}, u32[]{:S(2)}) %collective-permute-start.6) | collective-permute-done | bytes 524320 | tf_op jit(solution)/shard_map/ppermute | solution.py:17
  66.2 1.7 collective-permute-start.7
  67.9 2.1 %fusion = bf16[2,2,32,8192]{3,2,1,0:T(8,128)(2,1)S(1)} fusion(bf16[2,2,32,8192]{3,2,1,0:T(8,128)(2,1)S(1)} %bitcast.93, bf16[2,2,32,8192]{3,2,1,0:T(8,128)(2,1)} %collective-permute-done.14), kind=kLoop, calls=%fused_computation.3 | loop fusion | flops 4194304 | bytes 6291456 | tf_op jit(solution)/shard_map/convert_element_type | solution.py:182
  71.1 1.7 collective-permute-start.12
  72.8 42.1 %collective-permute-done.15 = bf16[2,32,8192]{2,1,0:T(8,128)(2,1)S(1)} collective-permute-done((bf16[2,32,8192]{2,1,0:T(8,128)(2,1)S(1)}, bf16[2,32,8192]{2,1,0:T(8,128)(2,1)S(1)}, u32[]{:S(2)}, u32[]{:S(2)}) %collective-permute-start.15) | collective-permute-done | bytes 1048608 | tf_op jit(solution)/shard_map/ppermute | solution.py:17
  116.0 18.4 %collective-permute-done.12 = bf16[2,32,8192]{2,1,0:T(8,128)(2,1)S(1)} collective-permute-done((bf16[2,32,8192]{2,1,0:T(8,128)(2,1)S(1)}, bf16[2,32,8192]{2,1,0:T(8,128)(2,1)S(1)}, u32[]{:S(2)}, u32[]{:S(2)}) %collective-permute-start.12) | collective-permute-done | bytes 1048608 | tf_op jit(solution)/shard_map/ppermute | solution.py:17
  134.6 1.1 collective-permute-start.13
  136.8 8.8 %collective-permute-done.13 = bf16[32,8192]{1,0:T(8,128)(2,1)S(1)} collective-permute-done((bf16[32,8192]{1,0:T(8,128)(2,1)S(1)}, bf16[32,8192]{1,0:T(8,128)(2,1)S(1)}, u32[]{:S(2)}, u32[]{:S(2)}) %collective-permute-start.13) | collective-permute-done | bytes 524320 | tf_op jit(solution)/shard_map/ppermute | solution.py:17
  145.9 5.5 %collective-permute-start.17 = (bf16[32,8192]{1,0:T(8,128)(2,1)S(1)}, bf16[32,8192]{1,0:T(8,128)(2,1)S(1)}, u32[]{:S(2)}, u32[]{:S(2)}) collective-permute-start(bf16[32,8192]{1,0:T(8,128)(2,1)S(1)} %select_convert_fusion), channel_id=1, source_target_pairs={{0,16},{2,18},{4,20},{6,22},{8,24},{10,26},{12,28},{14,30},{16,0},... | collective-permute-start | bytes 1572872 | tf_op jit(solution)/shard_map/ppermute | solution.py:17
  151.4 14.0 %shard_map.58 = (f32[8192,1024]{1,0:T(8,128)}, f32[512,1024]{1,0:T(8,128)S(1)}) custom-call(bf16[256,4096]{1,0:T(8,128)(2,1)S(1)} %bitcast.92, bf16[256,4096]{1,0:T(8,128)(2,1)} %collective-permute-done.8.refs_1_, bf16[512,1024]{1,0:T(8,128)(2,1)S(1)} %pad_maximum_fusion.4.refs_2_, bf16[8192,1024]{1,0:T(8,128)(2,1)} %refs_2_.1), custom_call_target="tpu_custom_call" | custom-call | flops 8589934592 | bytes 29360128 | tf_op jit(solution)/shard_map/pallas_call | solution.py:114
  165.3 1.3 copy-done.2
  166.6 1.4 copy-done
  168.0 10.1 %shard_map.59 = f32[512,1024]{1,0:T(8,128)S(1)} custom-call(bf16[256,4096]{1,0:T(8,128)(2,1)S(1)} %bitcast.89, bf16[256,4096]{1,0:T(8,128)(2,1)} %copy-done, bf16[8192,1024]{1,0:T(8,128)(2,1)} %refs_2_.1, f32[512,1024]{1,0:T(8,128)} %copy-done.2), custom_call_target="tpu_custom_call" | custom-call | flops 4294967296 | bytes 12582912 | tf_op jit(solution)/shard_map/pallas_call | solution.py:114
  178.6 1.5 collective-permute-start.10
  180.1 9.2 %shard_map.60 = f32[8192,1024]{1,0:T(8,128)} custom-call(bf16[256,4096]{1,0:T(8,128)(2,1)S(1)} %bitcast.90, bf16[256,4096]{1,0:T(8,128)(2,1)S(1)} %copy-done.1, bf16[512,1024]{1,0:T(8,128)(2,1)S(1)} %pad_maximum_fusion.4.refs_2_, f32[8192,1024]{1,0:T(8,128)} %get-tuple-element.6.refs_3_), custom_call_target="tpu_custom_call", output_to_operand_aliasing={{}: (3, {})} | custom-call | flops 4294967296 | bytes 20971520 | tf_op jit(solution)/shard_map/pallas_call | solution.py:114
  189.6 1.4 collective-permute-start.18
  191.5 7.6 %collective-permute-done.18 = bf16[32,8192]{1,0:T(8,128)(2,1)S(1)} collective-permute-done((bf16[32,8192]{1,0:T(8,128)(2,1)S(1)}, bf16[32,8192]{1,0:T(8,128)(2,1)S(1)}, u32[]{:S(2)}, u32[]{:S(2)}) %collective-permute-start.18) | collective-permute-done | bytes 524320 | tf_op jit(solution)/shard_map/ppermute | solution.py:17
  199.8 1.1 convolution_bitcast_fusion
  201.9 1.1 copy.13
  (72 shorter events, 17.0 us)
Async XLA Ops:
  0.6 19.7 %collective-permute-start = (bf16[32,8192]{1,0:T(8,128)(2,1)}, bf16[32,8192]{1,0:T(8,128)(2,1)}, u32[]{:S(2)}, u32[]{:S(2)}) collective-permute-start(bf16[32,8192]{1,0:T(8,128)(2,1)} %param.3), channel_id=1, source_target_pairs={{0,1},{1,0},{2,3},{3,2},{4,5},{5,4},{6,7},{7,6},{8,9},{9,8},{10,11... | collective-permute-start | bytes 1572872 | tf_op jit(solution)/shard_map/ppermute | solution.py:17
  10.4 17.1 %collective-permute-start.9 = (bf16[256,1024]{1,0:T(8,128)(2,1)S(1)}, bf16[256,1024]{1,0:T(8,128)(2,1)}, u32[]{:S(2)}, u32[]{:S(2)}) collective-permute-start(bf16[256,1024]{1,0:T(8,128)(2,1)S(1)} %dynamic-slice_dynamic-update-slice_fusion.8), channel_id=1, source_target_pairs={{0,1},{1,0},{2,3},{3,2},{4,5},{5,4},{6,7},{7,6},{8,9},{9,8},{10,11... | collective-permute-start | bytes 1572872 | tf_op jit(solution)/shard_map/ppermute | solution.py:17
  18.6 1.7 copy-start.3
  20.3 47.6 %collective-permute-start.14 = (bf16[2,2,32,8192]{3,2,1,0:T(8,128)(2,1)}, bf16[2,2,32,8192]{3,2,1,0:T(8,128)(2,1)}, u32[]{:S(2)}, u32[]{:S(2)}) collective-permute-start(bf16[2,2,32,8192]{3,2,1,0:T(8,128)(2,1)} %bitcast.14), channel_id=1, source_target_pairs={{0,2},{2,0},{4,6},{6,4},{8,10},{10,8},{12,14},{14,12},{16,18},{18,... | collective-permute-start | bytes 6291464 | tf_op jit(solution)/shard_map/ppermute | solution.py:17
  24.3 21.5 %collective-permute-start.1 = (bf16[1,1,1,32,4096]{4,3,2,1,0:T(8,128)(2,1)S(1)}, bf16[1,1,1,32,4096]{4,3,2,1,0:T(8,128)(2,1)S(1)}, u32[]{:S(2)}, u32[]{:S(2)}) collective-permute-start(bf16[1,1,1,32,4096]{4,3,2,1,0:T(8,128)(2,1)S(1)} %get-tuple-element.22), channel_id=1, source_target_pairs={{0,16},{2,18},{4,20},{6,22},{8,24},{10,26},{12,28},{14,30},{16,0},... | collective-permute-start | bytes 786440 | tf_op jit(solution)/shard_map/ppermute | solution.py:17
  27.4 23.8 %collective-permute-start.5 = (bf16[1,1,1,32,4096]{4,3,2,1,0:T(8,128)(2,1)S(1)}, bf16[1,1,1,32,4096]{4,3,2,1,0:T(8,128)(2,1)S(1)}, u32[]{:S(2)}, u32[]{:S(2)}) collective-permute-start(bf16[1,1,1,32,4096]{4,3,2,1,0:T(8,128)(2,1)S(1)} %get-tuple-element.21), channel_id=1, source_target_pairs={{0,16},{2,18},{4,20},{6,22},{8,24},{10,26},{12,28},{14,30},{16,0},... | collective-permute-start | bytes 786440 | tf_op jit(solution)/shard_map/ppermute | solution.py:17
  36.4 34.2 %collective-permute-start.11 = (bf16[2,2,32,8192]{3,2,1,0:T(8,128)(2,1)S(1)}, bf16[2,2,32,8192]{3,2,1,0:T(8,128)(2,1)S(1)}, u32[]{:S(2)}, u32[]{:S(2)}) collective-permute-start(bf16[2,2,32,8192]{3,2,1,0:T(8,128)(2,1)S(1)} %bitcast.100), channel_id=1, source_target_pairs={{0,2},{2,0},{4,6},{6,4},{8,10},{10,8},{12,14},{14,12},{16,18},{18,... | collective-permute-start | bytes 6291464 | tf_op jit(solution)/shard_map/ppermute | solution.py:17
  45.8 13.6 %collective-permute-start.2 = (bf16[2,1,1,32,4096]{4,3,2,1,0:T(8,128)(2,1)S(1)}, bf16[2,1,1,32,4096]{4,3,2,1,0:T(8,128)(2,1)S(1)}, u32[]{:S(2)}, u32[]{:S(2)}) collective-permute-start(bf16[2,1,1,32,4096]{4,3,2,1,0:T(8,128)(2,1)S(1)} %pad_maximum_fusion.7), channel_id=1, source_target_pairs={{0,4},{2,6},{4,0},{6,2},{8,12},{10,14},{12,8},{14,10},{16,20},{18,... | collective-permute-start | bytes 1572872 | tf_op jit(solution)/shard_map/ppermute | solution.py:17
  51.3 14.9 %collective-permute-start.6 = (bf16[2,1,1,32,4096]{4,3,2,1,0:T(8,128)(2,1)S(1)}, bf16[2,1,1,32,4096]{4,3,2,1,0:T(8,128)(2,1)S(1)}, u32[]{:S(2)}, u32[]{:S(2)}) collective-permute-start(bf16[2,1,1,32,4096]{4,3,2,1,0:T(8,128)(2,1)S(1)} %pad_maximum_fusion.8), channel_id=1, source_target_pairs={{0,8},{2,10},{4,12},{6,14},{8,0},{10,2},{12,4},{14,6},{16,24},{18,... | collective-permute-start | bytes 1572872 | tf_op jit(solution)/shard_map/ppermute | solution.py:17
  59.6 76.4 %collective-permute-start.3 = (bf16[2,2,1,32,4096]{4,3,2,1,0:T(8,128)(2,1)S(1)}, bf16[2,2,1,32,4096]{4,3,2,1,0:T(8,128)(2,1)S(1)}, u32[]{:S(2)}, u32[]{:S(2)}) collective-permute-start(bf16[2,2,1,32,4096]{4,3,2,1,0:T(8,128)(2,1)S(1)} %pad_maximum_fusion.2), channel_id=1, source_target_pairs={{0,8},{2,10},{4,12},{6,14},{8,0},{10,2},{12,4},{14,6},{16,24},{18,... | collective-permute-start | bytes 3145736 | tf_op jit(solution)/shard_map/ppermute | solution.py:17
  66.2 69.5 %collective-permute-start.7 = (bf16[2,1,2,32,4096]{4,3,2,1,0:T(8,128)(2,1)S(1)}, bf16[2,1,2,32,4096]{4,3,2,1,0:T(8,128)(2,1)S(1)}, u32[]{:S(2)}, u32[]{:S(2)}) collective-permute-start(bf16[2,1,2,32,4096]{4,3,2,1,0:T(8,128)(2,1)S(1)} %pad_maximum_fusion.3), channel_id=1, source_target_pairs={{0,4},{2,6},{4,0},{6,2},{8,12},{10,14},{12,8},{14,10},{16,20},{18,... | collective-permute-start | bytes 3145736 | tf_op jit(solution)/shard_map/ppermute | solution.py:17
  70.1 44.8 %collective-permute-start.15 = (bf16[2,32,8192]{2,1,0:T(8,128)(2,1)S(1)}, bf16[2,32,8192]{2,1,0:T(8,128)(2,1)S(1)}, u32[]{:S(2)}, u32[]{:S(2)}) collective-permute-start(bf16[2,32,8192]{2,1,0:T(8,128)(2,1)S(1)} %slice_bitcast_fusion), channel_id=1, source_target_pairs={{0,4},{2,6},{4,0},{6,2},{8,12},{10,14},{12,8},{14,10},{16,20},{18,... | collective-permute-start | bytes 3145736 | tf_op jit(solution)/shard_map/ppermute | solution.py:17
  71.1 63.2 %collective-permute-start.12 = (bf16[2,32,8192]{2,1,0:T(8,128)(2,1)S(1)}, bf16[2,32,8192]{2,1,0:T(8,128)(2,1)S(1)}, u32[]{:S(2)}, u32[]{:S(2)}) collective-permute-start(bf16[2,32,8192]{2,1,0:T(8,128)(2,1)S(1)} %slice_bitcast_fusion.2), channel_id=1, source_target_pairs={{0,4},{2,6},{4,0},{6,2},{8,12},{10,14},{12,8},{14,10},{16,20},{18,... | collective-permute-start | bytes 3145736 | tf_op jit(solution)/shard_map/ppermute | solution.py:17
  115.1 21.6 %collective-permute-start.16 = (bf16[32,8192]{1,0:T(8,128)(2,1)S(1)}, bf16[32,8192]{1,0:T(8,128)(2,1)S(1)}, u32[]{:S(2)}, u32[]{:S(2)}) collective-permute-start(bf16[32,8192]{1,0:T(8,128)(2,1)S(1)} %slice_bitcast_fusion.4), channel_id=1, source_target_pairs={{0,8},{2,10},{4,12},{6,14},{8,0},{10,2},{12,4},{14,6},{16,24},{18,... | collective-permute-start | bytes 1572872 | tf_op jit(solution)/shard_map/ppermute | solution.py:17
  134.6 11.0 %collective-permute-start.13 = (bf16[32,8192]{1,0:T(8,128)(2,1)S(1)}, bf16[32,8192]{1,0:T(8,128)(2,1)S(1)}, u32[]{:S(2)}, u32[]{:S(2)}) collective-permute-start(bf16[32,8192]{1,0:T(8,128)(2,1)S(1)} %slice_bitcast_fusion.6), channel_id=1, source_target_pairs={{0,8},{2,10},{4,12},{6,14},{8,0},{10,2},{12,4},{14,6},{16,24},{18,... | collective-permute-start | bytes 1572872 | tf_op jit(solution)/shard_map/ppermute | solution.py:17
  135.9 15.5 %collective-permute-start.8 = (bf16[256,4096]{1,0:T(8,128)(2,1)S(1)}, bf16[256,4096]{1,0:T(8,128)(2,1)}, u32[]{:S(2)}, u32[]{:S(2)}) collective-permute-start(bf16[256,4096]{1,0:T(8,128)(2,1)S(1)} %bitcast.91), channel_id=1, source_target_pairs={{0,2},{2,0},{4,6},{6,4},{8,10},{10,8},{12,14},{14,12},{16,18},{18,... | collective-permute-start | bytes 6291464 | tf_op jit(solution)/shard_map/ppermute | solution.py:17
  136.2 30.4 %collective-permute-start.4 = (bf16[256,4096]{1,0:T(8,128)(2,1)S(1)}, bf16[256,4096]{1,0:T(8,128)(2,1)S(1)}, u32[]{:S(2)}, u32[]{:S(2)}) collective-permute-start(bf16[256,4096]{1,0:T(8,128)(2,1)S(1)} %bitcast.88), channel_id=1, source_target_pairs={{0,2},{2,0},{4,6},{6,4},{8,10},{10,8},{12,14},{14,12},{16,18},{18,... | collective-permute-start | bytes 6291464 | tf_op jit(solution)/shard_map/ppermute | solution.py:17
  145.9 43.4 %collective-permute-start.17 = (bf16[32,8192]{1,0:T(8,128)(2,1)S(1)}, bf16[32,8192]{1,0:T(8,128)(2,1)S(1)}, u32[]{:S(2)}, u32[]{:S(2)}) collective-permute-start(bf16[32,8192]{1,0:T(8,128)(2,1)S(1)} %select_convert_fusion), channel_id=1, source_target_pairs={{0,16},{2,18},{4,20},{6,22},{8,24},{10,26},{12,28},{14,30},{16,0},... | collective-permute-start | bytes 1572872 | tf_op jit(solution)/shard_map/ppermute | solution.py:17
  165.3 1.3 copy-start.2
  166.6 1.4 copy-start
  178.4 1.7 copy-start.1
  178.6 12.5 %collective-permute-start.10 = (bf16[256,1024]{1,0:T(8,128)(2,1)S(1)}, bf16[256,1024]{1,0:T(8,128)(2,1)S(1)}, u32[]{:S(2)}, u32[]{:S(2)}) collective-permute-start(bf16[256,1024]{1,0:T(8,128)(2,1)S(1)} %select_convert_fusion.1), channel_id=1, source_target_pairs={{0,1},{1,0},{2,3},{3,2},{4,5},{5,4},{6,7},{7,6},{8,9},{9,8},{10,11... | collective-permute-start | bytes 1572872 | tf_op jit(solution)/shard_map/ppermute | solution.py:17
  189.6 9.5 %collective-permute-start.18 = (bf16[32,8192]{1,0:T(8,128)(2,1)S(1)}, bf16[32,8192]{1,0:T(8,128)(2,1)S(1)}, u32[]{:S(2)}, u32[]{:S(2)}) collective-permute-start(bf16[32,8192]{1,0:T(8,128)(2,1)S(1)} %fusion.68), channel_id=1, source_target_pairs={{0,1},{1,0},{2,3},{3,2},{4,5},{5,4},{6,7},{7,6},{8,9},{9,8},{10,11... | collective-permute-start | bytes 1572872 | tf_op jit(solution)/shard_map/ppermute | solution.py:17
  191.5 8.1 %copy-start.4 = (bf16[256,1024]{1,0:T(8,128)(2,1)}, bf16[256,1024]{1,0:T(8,128)(2,1)S(1)}, u32[]{:S(2)}) copy-start(bf16[256,1024]{1,0:T(8,128)(2,1)S(1)} %dynamic-slice_dynamic-update-slice_fusion) | copy-start | bytes 1572868

commit v2 on v0

v2 whole, which is shorter than its diff:
```python
import functools
import math

import jax
import jax.numpy as jnp
from jax import lax
from jax.experimental import pallas as pl
from jax.experimental.pallas import tpu as pltpu
from jax.sharding import PartitionSpec as P

BF16 = jnp.bfloat16
F32 = jnp.float32
VMEM_LIMIT = 60 * 1024 * 1024
VMEM_MOST = 63 * 1024 * 1024
LANES = 128


def swap(values, axis, mask):
    return lax.ppermute(values, axis, [(i, i ^ mask) for i in range(lax.axis_size(axis))])


def bit(number, place):
    return jnp.bitwise_and(jnp.right_shift(number, place), 1) == 1


def reversed_bits(number, count):
    return sum((number >> b & 1) << (count - 1 - b) for b in range(count))


def exchange_order(parts, apart):
    for b in range(len(parts).bit_length() - 1):
        flip = bit(apart, b)
        parts = [jnp.where(flip, parts[q ^ 1 << b], parts[q]) for q in range(len(parts))]
    return parts


class Chain:
    def __init__(self, place):
        self.place = place
        self.last = []

    def __call__(
        self,
        body,
        inputs,
        in_specs,
        outs,
        out_specs,
        steps=1,
        scratch=(),
        aliases=None,
        flops=0,
        limit=VMEM_LIMIT,
        late=(),
    ):
        count, extra = len(inputs), len(self.last)

        late = list(late)
        made = len(outs)
        skipped = count + len(late) + extra

        def kernel(place, *refs):
            body(
                place,
                *refs[:count],
                *refs[skipped : skipped + made],
                *refs[skipped + made + len(late) :],
            )

        moved = sum(math.prod(v.shape) * v.dtype.itemsize for v in list(inputs) + list(outs))
        result = pl.pallas_call(
            kernel,
            grid=(steps,),
            in_specs=[pl.BlockSpec(memory_space=pltpu.SMEM)]
            + list(in_specs)
            + [pl.BlockSpec(memory_space=pl.ANY)] * (len(late) + extra),
            out_specs=list(out_specs) + [pl.BlockSpec(memory_space=pl.ANY)] * len(late),
            scratch_shapes=list(scratch),
            out_shape=list(outs) + [jax.ShapeDtypeStruct(v.shape, v.dtype) for v in late],
            input_output_aliases={1 + k: v for k, v in (aliases or {}).items()}
            | {1 + count + k: made + k for k in range(len(late))},
            compiler_params=pltpu.CompilerParams(vmem_limit_bytes=limit),
            cost_estimate=pl.CostEstimate(flops=flops, bytes_accessed=moved, transcendentals=0),
        )(self.place, *inputs, *late, *self.last)
        self.last = [result[made - 1]]
        return result

    def gate(self, values, after):
        count = len(values)

        def body(*refs):
            del refs

        return pl.pallas_call(
            body,
            in_specs=[pl.BlockSpec(memory_space=pl.ANY)] * (count + len(after)),
            out_specs=[pl.BlockSpec(memory_space=pl.ANY)] * count,
            out_shape=[jax.ShapeDtypeStruct(v.shape, v.dtype) for v in values],
            input_output_aliases={k: k for k in range(count)},
        )(*values, *after)

    def follow(self, *values):
        self.last.extend(values)


def whole(shape):
    return pl.BlockSpec(shape, lambda i: (0,) * len(shape))


def across(rows, tile):
    return pl.BlockSpec((rows, tile), lambda i: (0, i))


def array(rows, columns, kind=BF16):
    return jax.ShapeDtypeStruct((rows, columns), kind)


def cotangent_product(chain, grad, weight, rows, low_bits, reorder, cuts=1, late=()):
    tokens, columns = grad.shape
    width = weight.shape[0]
    tile = min(2048, width)
    blocks = 1 << low_bits

    def body(place, grad, weight, *outs):
        if reorder:
            ordered = outs[-1]

            @pl.when(pl.program_id(0) == 0)
            def _():
                for position in range(blocks):
                    source = place[0] ^ reversed_bits(position, low_bits)
                    start = pl.multiple_of(source * rows, rows)
                    ordered[position * rows : (position + 1) * rows, :] = grad[
                        pl.ds(start, rows), :
                    ]

            grad = ordered
        result = lax.dot_general(
            grad[...], weight[...], (((1,), (1,)), ((), ())), preferred_element_type=F32
        ).astype(BF16)
        for position in range(plain):
            outs[position][...] = result[position * rows : (position + 1) * rows]
        for position in range(plain, blocks):
            for piece in range(cuts):
                out = outs[plain + (position - plain) * cuts + piece]

                @pl.when(pl.program_id(0) // each == piece)
                def _(out=out, position=position):
                    out[...] = result[position * rows : (position + 1) * rows]

    steps = width // tile
    cuts = min(cuts, steps)
    each = steps // cuts
    plain = blocks - blocks // 4
    count = plain + (blocks - plain) * cuts
    piece_specs = [
        pl.BlockSpec((rows, tile), lambda i, k=k: (0, jnp.clip(i - k * each, 0, each - 1)))
        for k in range(cuts)
    ]
    made = chain(
        body,
        [grad, weight],
        [whole((tokens, columns)), pl.BlockSpec((tile, columns), lambda i: (i, 0))],
        [array(rows, width)] * plain
        + [array(rows, width // cuts)] * (count - plain)
        + [array(tokens, columns)] * reorder,
        [across(rows, tile)] * plain
        + piece_specs * (blocks - plain)
        + [whole((tokens, columns))] * reorder,
        steps,
        flops=2 * tokens * width * columns,
        late=late,
    )
    pieces = [list(made[k : k + cuts]) for k in range(plain, count, cuts)]
    return list(made[:plain]) + pieces, list(made[count:])


def add(first, *others):
    total = first.astype(F32)
    for other in others:
        total = total + other.astype(F32)
    return total


def exchange_last(values):
    position = lax.axis_index("tensor")
    places = lax.axis_size("tensor").bit_length() - 1
    for place in range(places):
        sent = values.astype(BF16) if place == 0 else values
        other = swap(sent, "tensor", 1 << place)
        if place + 1 < places:
            own, other = values.astype(F32), other.astype(F32)
            values = jnp.where(bit(position, place), other - own, own + other)
    return values, other


def rotate(chain, pairs, places, factor, copies=1, sums=()):
    rows = pairs[0][0].shape[0]
    widths = [own.shape[1] for own, _ in pairs]
    width = sum(widths)
    blocks = width // LANES

    def body(place, *refs):
        ins, outs = refs[: 2 * len(pairs)], refs[len(flat) :]
        terms = list(refs[2 * len(pairs) : len(flat)])
        for k, (_, others) in enumerate(sums):
            own, start = terms.pop(0), 0
            for _ in others:
                other = terms.pop(0)
                there = slice(start, start + other.shape[1])
                total = own[:, there].astype(F32) + other[...].astype(F32)
                outs[-1][k * rows : (k + 1) * rows, there] = total.astype(BF16)
                start += other.shape[1]
        upper = bit(place[2], places - 1)
        columns = []
        for k in range(len(pairs)):
            own, other = ins[2 * k], ins[2 * k + 1]
            for start in range(0, widths[k], LANES):
                here = slice(start, start + LANES)
                a, b = own[:, here].astype(F32), other[:, here].astype(F32)
                columns.append(jnp.where(upper, b - a, a + b))
        values = jnp.concatenate(columns, axis=0)
        i = lax.broadcasted_iota(jnp.int32, (LANES, LANES), 0)
        j = lax.broadcasted_iota(jnp.int32, (LANES, LANES), 1)
        parity = i & j
        for shift in (4, 2, 1):
            parity = parity ^ (parity >> shift)
        signs = jnp.where(parity & 1 == 1, -1.0, 1.0).astype(BF16)
        high = values.astype(BF16)
        rest = values - high.astype(F32)
        middle = rest.astype(BF16)
        low = (rest - middle.astype(F32)).astype(BF16)
        result = (
            jnp.dot(low, signs, preferred_element_type=F32)
            + jnp.dot(middle, signs, preferred_element_type=F32)
        ) + jnp.dot(high, signs, preferred_element_type=F32)
        apart = 1
        while apart < blocks:
            shaped = result.reshape(blocks // (2 * apart), 2, apart * rows, LANES)
            a, b = shaped[:, 0], shaped[:, 1]
            result = jnp.stack([a + b, a - b], axis=1).reshape(blocks * rows, LANES)
            apart *= 2
        result = (result * factor).astype(BF16)
        for block in range(blocks):
            for copy in range(copies):
                outs[copy][:, block * LANES : (block + 1) * LANES] = result[
                    block * rows : (block + 1) * rows
                ]

    flat = [v for pair in pairs for v in pair]
    flat += [v for own, others in sums for v in [own] + list(others)]
    shapes = [(rows, width)] * copies + [(len(sums) * rows, width)] * (len(sums) > 0)
    return chain(
        body,
        flat,
        [whole(v.shape) for v in flat],
        [array(*shape) for shape in shapes],
        [whole(shape) for shape in shapes],
        flops=6 * rows * width * LANES,
    )


def product(
    chain,
    gathered,
    grads,
    weight,
    columns_from,
    width,
    inner,
    before=None,
    into=None,
    grad=False,
    out=0,
    last=False,
    late=(),
):
    features, columns = weight.shape
    tile = min(1024, width)
    steps = width // tile
    first = columns_from // tile
    count = len(grads)
    held = count * inner
    groups = len(gathered)
    flat = [v for group in gathered for v in group]
    tall = pl.BlockSpec((tile, columns), lambda i: (first + i, 0))
    share = whole((out * inner, columns))
    inputs = list(flat)
    specs = [
        across(v.shape[0], tile)
        if v.shape[1] == width
        else pl.BlockSpec((v.shape[0], tile), lambda i: (0, first + i))
        for v in flat
    ]
    outs, out_specs, scratch, aliases = [], [], [], {}
    if grad:
        inputs += grads
        specs += [whole(v.shape) for v in grads]
        outs.append(array(features, columns, F32))
        out_specs.append(tall)
        scratch.append(pltpu.VMEM((groups * held, columns), BF16))
    if out:
        square = whole((out * held, columns))
        inputs.append(weight)
        specs.append(tall)
        if before is not None:
            inputs.append(before)
            specs.append(square)
        if last:
            outs += [array(out * inner, columns, F32)] + [array(out * inner, columns)] * (count - 1)
            out_specs += [share] * count
            scratch.append(pltpu.VMEM((out * held, columns), F32))
        else:
            outs.append(array(out * held, columns, F32))
            out_specs.append(square)
    if into is not None:
        aliases[len(inputs)] = 0
        inputs.append(into)
        specs.append(pl.BlockSpec(memory_space=pl.ANY))

    def body(place, *refs):
        refs = list(refs)
        step = pl.program_id(0)
        held_rows = [refs.pop(0) for _ in flat]
        shares = [refs.pop(0) for _ in range(count)] if grad else []
        if out:
            weight = refs.pop(0)
            earlier = refs.pop(0) if before is not None else None
        if aliases:
            refs.pop(0)
        rotated = jnp.concatenate([v[...] for v in held_rows], axis=0)
        if grad:
            result = refs.pop(0)
            cotangent = refs.pop(-2 if out and last else -1)

            @pl.when(step == 0)
            def _():
                parts = exchange_order([s[...] for s in shares], place[1])
                for group in range(groups):
                    start = (group % 2 * 2 + group // 2) * inner
                    for j, part in enumerate(parts):
                        to = group * held + j * inner
                        cotangent[to : to + inner, :] = part[start : start + inner]

            result[...] = (
                lax.dot_general(
                    rotated, cotangent[...], (((0,), (0,)), ((), ())), preferred_element_type=F32
                )
                * chain.scale
            )
        if out:
            total = refs.pop(-1)

            @pl.when(step == 0)
            def _():
                total[...] = jnp.zeros_like(total) if earlier is None else earlier[...]

            total[...] += jnp.dot(
                rotated[(groups - out) * held :], weight[...], preferred_element_type=F32
            )
            if last:

                @pl.when(step == steps - 1)
                def _():
                    for side in range(out):
                        start = side * held
                        parts = [
                            total[start + j * inner : start + (j + 1) * inner, :]
                            for j in range(count)
                        ]
                        for ref, part in zip(refs, exchange_order(parts, place[1])):
                            ref[side * inner : (side + 1) * inner, :] = part.astype(ref.dtype)

    return chain(
        body,
        inputs,
        specs,
        outs,
        out_specs,
        steps,
        scratch,
        aliases,
        flops=2 * width * columns * held * (groups * grad + out),
        limit=VMEM_MOST,
        late=late,
    )


def finish(chain, shares, rows, low_bits):
    rest = 1 << (low_bits - 2)

    def body(place, *refs):
        *shares, out = refs
        for position in range(1 << low_bits):
            side, middle = position // (2 * rest), position // rest % 2
            start = ((middle * 2 + side) * rest + position % rest) * rows
            here = slice(start, start + rows)
            total = shares[0][here, :]
            for other in shares[1:]:
                total = total + other[here, :].astype(F32)
            target = place[0] ^ reversed_bits(position, low_bits)
            out[pl.ds(pl.multiple_of(target * rows, rows), rows), :] = total.astype(BF16)

    shape = shares[0].shape
    (out,) = chain(
        body, shares, [whole(shape)] * len(shares), [array(*shape)], [whole(shape)]
    )
    return out


def per_device(activations, weight, out_grad):
    dp, tensor = lax.axis_size("dp"), lax.axis_size("tensor")
    dp_bits, top_bits = dp.bit_length() - 1, tensor.bit_length() - 1
    low_bits = dp_bits - top_bits
    rows, width = activations.shape
    me, mine = lax.axis_index("dp"), lax.axis_index("tensor")
    low_me = jnp.bitwise_and(me, (1 << low_bits) - 1)
    apart = jnp.bitwise_xor(jnp.right_shift(me, low_bits), mine)
    chain = Chain(jnp.stack([low_me, apart, mine]).astype(jnp.int32))
    chain.scale = 1.0 / math.sqrt(out_grad.shape[0] * tensor)
    factor = 1.0 / math.sqrt(width * tensor)
    rest = 1 << (low_bits - 2)
    inner = rest * rows

    def near(values, p):
        return swap(values, "dp", 1 << p)

    def core_send(blocks):
        half = len(blocks) // 2
        return [
            [kept, [near(v, 0) for v in went] if isinstance(went, list) else near(went, 0)]
            for kept, went in zip(blocks[:half], blocks[half:])
        ]

    def split_send(terms, p, *more):
        half = len(terms) // 2
        message = jnp.concatenate([add(*t).astype(BF16) for t in terms[half:]] + list(more), axis=0)
        came = near(message, p)
        pieces = [came[k * rows : (k + 1) * rows] for k in range(half + len(more))]
        kept = [t + [piece] for t, piece in zip(terms[:half], pieces)]
        return kept, pieces[half:], message

    rotation = exchange_last(activations)
    own, (ordered,) = cotangent_product(
        chain, out_grad, weight, rows, low_bits, True, 2
    )
    own = core_send(own)
    far = [swap(ordered, "tensor", q) for q in range(1, tensor)]
    half = len(own) // 2
    sent, rotated, message = rotate(chain, [rotation], top_bits, factor, 2, own[half:])
    came = near(message, 1)
    own = [terms + [came[k * rows : (k + 1) * rows]] for k, terms in enumerate(own[:half])]

    wide = list(range(2, dp_bits))
    gathered = {0: sent}
    for p in reversed(wide):
        for j in list(gathered):
            if p > 2 or j == 0:
                gathered[j | 1 << p] = near(gathered[j], p)
    gathered[0] = rotated

    others = []
    for q, grad in enumerate(far):
        late = [terms[0] for terms in own] if q == 0 else []
        products, late = cotangent_product(
            chain, grad, weight, rows, low_bits, False, 1, late
        )
        if q == 0:
            own = [[first] + terms[1:] for first, terms in zip(late, own)]
        plain = [v[0] if isinstance(v, list) else v for v in products]
        others.append(core_send(plain))

    ahead = [j for j in gathered if j and j < 1 << dp_bits and not j & 4]
    if low_bits > 2:
        own, pieces, message = split_send(own, 2, *[gathered[j] for j in ahead])
    else:
        message = jnp.concatenate([gathered[j] for j in ahead], axis=0)
        came = near(message, 2)
        pieces = [came[k * rows : (k + 1) * rows] for k in range(len(ahead))]
    gathered.update({j | 4: piece for j, piece in zip(ahead, pieces)})
    for p in range(3, low_bits):
        own, _, message = split_send(own, p)

    def gate_first(parts, after):
        held = list(chain.gate([terms[0] for part in parts for terms in part], after))
        return [[[held.pop(0)] + terms[1:] for terms in part] for part in parts]

    others = gate_first(others, [message])
    others = [split_send(part, 1)[0] for part in others]

    order = [
        t << low_bits | reversed_bits(r, low_bits - 2) << 2
        for t in range(tensor)
        for r in range(rest)
    ]
    here = [gathered[j] for j in order]
    core = [near(block, 0) for block in here]
    cut = width * 5 // 8
    ranges = [(0, cut), (cut, width - cut)]
    across_sent = [
        jnp.concatenate([block[:, start : start + size] for block in here], axis=0)
        for start, size in ranges
    ]
    others = gate_first(others, across_sent[:1])
    messages = []
    for p in range(2, low_bits):
        sent_parts = [split_send(part, p) for part in others]
        others = [part for part, _, _ in sent_parts]
        messages = [message for _, _, message in sent_parts]
    chain.follow(across_sent[0], *messages)
    grads = [ordered] + far
    arrived = [near(across_sent[0], 1)]

    some = exchange_order([add(*part[0]) for part in [own] + others], apart)
    for p in reversed(range(top_bits)):
        count = 1 << p
        pairs = [
            (some[j], swap(some[j + count].astype(BF16), "dp", count << low_bits))
            for j in range(count)
        ]
        some = [add(*pair) for pair in pairs]
    kept, came = pairs[0]
    arrived.append(near(across_sent[1], 1))
    arrived_core = [near(arrived[0], 0)]
    start, size = ranges[0]
    weight_grad, total, kept = product(
        chain, [here, core, [arrived[0]], [arrived_core[0]]], grads, weight, start, size, inner,
        grad=True, out=4, late=[kept],
    )
    (arrived[1],) = chain.gate(arrived[1:], [total])
    arrived_core.append(near(arrived[1], 0))
    rotated_grad = add(kept, came)
    final = exchange_last(rotated_grad)
    chain.follow(rotated_grad)
    start, size = ranges[1]
    result = product(
        chain, [here, core, [arrived[1]], [arrived_core[1]]], grads, weight, start, size, inner,
        before=total, out=4, last=True,
    )
    shares = [result[0]] + [swap(result[q], "tensor", q) for q in range(1, tensor)]
    (in_grad,) = rotate(chain, [final], top_bits, factor)
    (weight_grad,) = product(
        chain, [here, core, [arrived[1]], [arrived_core[1]]], grads, weight, start, size, inner,
        into=weight_grad, grad=True,
    )
    outputs = finish(chain, shares, rows, low_bits)
    return (outputs, in_grad, weight_grad)


def solution(mesh):
    return jax.shard_map(
        per_device,
        mesh=mesh,
        in_specs=(P("dp", "tensor"), P("tensor", "dp"), P("tensor", "dp")),
        out_specs=(P("tensor", "dp"), P("dp", "tensor"), P("tensor", "dp")),
        check_vma=False,
    )
```

time: 371 us -> 172 us (0.46)
  waiting for transfers between devices: 288 us -> 60.6 us
  Pallas kernels: 0 us -> 65.4 us
  matrix products: 55.4 us -> 0 us
  starting transfers between devices: 4.88 us -> 19.7 us
  between operations: 13.8 us -> 0.95 us
  other arithmetic: 5 us -> 15.1 us
  local copies, waits for them, and re-layouts: 3.79 us -> 9.9 us
    reduce_scatter x2 -> x0, waiting for transfers between devices: 193 us -> none  [the longest x1 166 us: per_device(): lax.psum_scatter(lax.dot_general(grad_all, weight, (((1,), (1,)), ((), ()...]
    pallas_call x0 -> x11, Pallas kernels: none -> 65.4 us  [the longest x8 65.4 us: __call__(): pl.pallas_call(kernel, grid=(steps,), in_specs=[pl.BlockSpec(memory_space...]
    all_gather x2 -> x0, waiting for transfers between devices: 60.1 us -> none  [the longest x1 60.1 us: per_device(): rows_all = lax.all_gather(rotated, 'dp', axis=0, tiled=True)]
    dot_general x7 -> x0, matrix products: 55.4 us -> none  [the longest x1 19.5 us: per_device(): lax.dot_general(rows_all, grad_all, (((0,), (0,)), ((), ())), preferred_e...]
    ppermute x2 -> x29, waiting for transfers between devices: 34.3 us -> 60.6 us  [swap(): lax.ppermute(values, axis, [(i, i ^ mask) for i in range(lax.axis_size(ax...]
    ppermute x2 -> x29, starting transfers between devices: 4.54 us -> 19.7 us  [swap(): lax.ppermute(values, axis, [(i, i ^ mask) for i in range(lax.axis_size(ax...]
    convert_element_type x3 -> x6, other arithmetic: 5 us -> 12.3 us  [the longest x4 6.42 us: split_send(): add(*t).astype(BF16)]
  transfers between devices with their start and end apart: 6 -> 29, of which waited for: 4 -> 12; matrix products, arithmetic and copies ran while one was open for 16% -> 11% of each run, Pallas kernels for 0% -> 34%
where the time goes in v2:
time: 172 us
  Pallas kernels  65.4 us (38%)
  waiting for transfers between devices  60.6 us (35%)
  starting transfers between devices  19.7 us (11%)
  other arithmetic  15.1 us (9%)
  local copies, waits for them, and re-layouts  9.9 us (6%)
    pallas_call x8, Pallas kernels, __call__(): pl.pallas_call(kernel, grid=(steps,), in_specs=[pl.BlockSpec(memory_space...  65.4 us
    ppermute x29, waiting for transfers between devices, swap(): lax.ppermute(values, axis, [(i, i ^ mask) for i in range(lax.axis_size(ax...  60.6 us
    ppermute x29, starting transfers between devices, swap(): lax.ppermute(values, axis, [(i, i ^ mask) for i in range(lax.axis_size(ax...  19.7 us
    unnamed x46, local copies, waits for them, and re-layouts  6.51 us
    convert_element_type x4, other arithmetic, split_send(): add(*t).astype(BF16)  6.42 us
    convert_element_type x1, other arithmetic, per_device(): some[j + count].astype(BF16)  3.54 us
  transfers between devices with their start and end apart: 29, of which 12 were waited for; matrix products, arithmetic and copies ran while one was open for 11% of the time, Pallas kernels for 34%

profile of v2, /device:TPU:0, one launch (start us, length us, event | category | flops | bytes accessed | tf_op | source)
XLA Modules:
  0.0 171.7 jit_solution(5267831349653178630)
XLA Ops:
  0.6 3.0 %collective-permute-start = (bf16[32,8192]{1,0:T(8,128)(2,1)}, bf16[32,8192]{1,0:T(8,128)(2,1)S(1)}, u32[]{:S(2)}, u32[]{:S(2)}) collective-permute-start(bf16[32,8192]{1,0:T(8,128)(2,1)} %refs_0_.3), channel_id=1, source_target_pairs={{0,1},{1,0},{2,3},{3,2},{4,5},{5,4},{6,7},{7,6},{8,9},{9,8},{10,11... | collective-permute-start | bytes 1572872 | tf_op jit(solution)/shard_map/ppermute | solution.py:19
  4.2 10.6 %shard_map.58 = (bf16[32,8192]{1,0:T(8,128)(2,1)}, bf16[32,8192]{1,0:T(8,128)(2,1)}, bf16[32,8192]{1,0:T(8,128)(2,1)}, bf16[32,8192]{1,0:T(8,128)(2,1)}, bf16[32...) custom-call(s32[3]{0:T(128)} %pad_add_fusion.place, ...), custom_call_target="tpu_custom_call" | custom-call | flops 4294967296 | bytes 22020096 | tf_op jit(solution)/shard_map/pallas_call | solution.py:71
  18.7 4.1 %shard_map.59 = (bf16[32,8192]{1,0:T(8,128)(2,1)}, bf16[32,8192]{1,0:T(8,128)(2,1)}, bf16[64,8192]{1,0:T(8,128)(2,1)}) custom-call(s32[3]{0:T(128)} %pad_add_fusion.place, bf16[32,8192]{1,0:T(8,128)(2,1)} %refs_0_.3, bf16[32,8192]{1,0:T(8,128)(2,1)} %copy-done.17, bf16[32,8192]{1,0:T(8,128)(2,1)} %get-tuple-element.38.refs_2_, bf16[32,4096]{1,0:T(8,128)(2,1)} %copy-done.18, ...), custom_call_target="tpu_custom_call" | custom-call | flops 201326592 | bytes 5242880 | tf_op jit(solution)/shard_map/pallas_call | solution.py:71
  22.8 1.5 collective-permute-start.9
  24.9 1.6 collective-permute-start.5
  26.5 2.6 %collective-permute-start.6 = (bf16[32,8192]{1,0:T(8,128)(2,1)}, bf16[32,8192]{1,0:T(8,128)(2,1)S(1)}, u32[]{:S(2)}, u32[]{:S(2)}) collective-permute-start(bf16[32,8192]{1,0:T(8,128)(2,1)} %get-tuple-element.46), channel_id=1, source_target_pairs={{0,16},{2,18},{4,20},{6,22},{8,24},{10,26},{12,28},{14,30},{16,0},... | collective-permute-start | bytes 1572872 | tf_op jit(solution)/shard_map/ppermute | solution.py:19
  29.0 9.0 %collective-permute-done.7.refs_0_.refs_11_ = bf16[256,1024]{1,0:T(8,128)(2,1)S(1)} collective-permute-done((bf16[256,1024]{1,0:T(8,128)(2,1)S(1)}, bf16[256,1024]{1,0:T(8,128)(2,1)S(1)}, u32[]{:S(2)}, u32[]{:S(2)}) %collective-permute-start.7) | collective-permute-done | bytes 524320 | tf_op jit(solution)/shard_map/ppermute | solution.py:19
  38.8 10.3 %shard_map.60 = (bf16[32,8192]{1,0:T(8,128)(2,1)}, bf16[32,8192]{1,0:T(8,128)(2,1)}, bf16[32,8192]{1,0:T(8,128)(2,1)}, bf16[32,8192]{1,0:T(8,128)(2,1)}, bf16[32...) custom-call(s32[3]{0:T(128)} %pad_add_fusion.place, ...), custom_call_target="tpu_custom_call", output_to_operand_aliasing={{8}: (3, {}), {9}: (4, {})} | custom-call | flops 4294967296 | bytes 21495808 | tf_op jit(solution)/shard_map/pallas_call | solution.py:71
  49.7 1.4 add_convert_fusion.3
  51.1 1.9 %collective-permute-done.6.refs_2_ = bf16[32,8192]{1,0:T(8,128)(2,1)S(1)} collective-permute-done((bf16[32,8192]{1,0:T(8,128)(2,1)}, bf16[32,8192]{1,0:T(8,128)(2,1)S(1)}, u32[]{:S(2)}, u32[]{:S(2)}) %collective-permute-start.6) | collective-permute-done | bytes 524320 | tf_op jit(solution)/shard_map/ppermute | solution.py:19
  54.1 1.3 add_convert_fusion.1
  55.4 1.4 add_convert_fusion.2
  59.1 17.5 %collective-permute-done.10 = bf16[64,8192]{1,0:T(8,128)(2,1)} collective-permute-done((bf16[64,8192]{1,0:T(8,128)(2,1)S(1)}, bf16[64,8192]{1,0:T(8,128)(2,1)}, u32[]{:S(2)}, u32[]{:S(2)}) %collective-permute-start.10) | collective-permute-done | bytes 1048608 | tf_op jit(solution)/shard_map/ppermute | solution.py:19
  78.8 5.4 %collective-permute-done.21 = bf16[64,8192]{1,0:T(8,128)(2,1)} collective-permute-done((bf16[64,8192]{1,0:T(8,128)(2,1)}, bf16[64,8192]{1,0:T(8,128)(2,1)}, u32[]{:S(2)}, u32[]{:S(2)}) %collective-permute-start.21) | collective-permute-done | bytes 1048608 | tf_op jit(solution)/shard_map/ppermute | solution.py:19
  84.2 2.3 %add_convert_fusion.refs_16_ = bf16[32,8192]{1,0:T(8,128)(2,1)} fusion(bf16[32,8192]{1,0:T(8,128)(2,1)} %collective-permute-done.22, bf16[32,8192]{1,0:T(8,128)(2,1)} %get-tuple-element.64, bf16[64,8192]{1,0:T(8,128)(2,1)} %collective-permute-done.21), kind=kLoop, calls=%fused_computation.7 | loop fusion | flops 1572864 | bytes 2097152 | tf_op jit(solution)/shard_map/convert_element_type | solution.py:437
  86.6 1.1 collective-permute-start.23
  87.7 1.2 slice.59.refs_3_
  88.9 1.1 slice.62
  91.6 4.9 %collective-permute-done.23 = bf16[32,8192]{1,0:T(8,128)(2,1)} collective-permute-done((bf16[32,8192]{1,0:T(8,128)(2,1)}, bf16[32,8192]{1,0:T(8,128)(2,1)}, u32[]{:S(2)}, u32[]{:S(2)}) %collective-permute-start.23) | collective-permute-done | bytes 524320 | tf_op jit(solution)/shard_map/ppermute | solution.py:19
  96.5 13.7 %collective-permute-done.16.refs_8_ = bf16[128,5120]{1,0:T(8,128)(2,1)} collective-permute-done((bf16[128,5120]{1,0:T(8,128)(2,1)S(1)}, bf16[128,5120]{1,0:T(8,128)(2,1)}, u32[]{:S(2)}, u32[]{:S(2)}) %collective-permute-start.16) | collective-permute-done | bytes 1310752 | tf_op jit(solution)/shard_map/ppermute | solution.py:19
  110.2 3.5 %select_convert_fusion = (bf16[32,8192]{1,0:T(8,128)(2,1)}, f32[32,8192]{1,0:T(8,128)}) fusion(pred[]{:T(512)S(6)} %eq.3, bf16[32,8192]{1,0:T(8,128)(2,1)} %collective-permute-done.23, bf16[64,8192]{1,0:T(8,128)(2,1)} %collective-permute-done.21, bf16[32,8192]{1,0:T(8,128)(2,1)} %collective-permute-done.18, bf16[32,8192]{1,0:T(8,128)(2,1)S(1)} %copy-done.5, ...), kind=kLoop, calls=%fused_computation.4 | loop fusion | flops 4456448 | bytes 5767169 | tf_op jit(solution)/shard_map/convert_element_type | solution.py:518
  114.3 2.3 %collective-permute-start.26 = (bf16[32,8192]{1,0:T(8,128)(2,1)}, bf16[32,8192]{1,0:T(8,128)(2,1)}, u32[]{:S(2)}, u32[]{:S(2)}) collective-permute-start(bf16[32,8192]{1,0:T(8,128)(2,1)} %get-tuple-element.75), channel_id=1, source_target_pairs={{0,16},{2,18},{4,20},{6,22},{8,24},{10,26},{12,28},{14,30},{16,0},... | collective-permute-start | bytes 1572872 | tf_op jit(solution)/shard_map/ppermute | solution.py:19
  117.6 1.1 copy-done.22
  118.7 17.4 %shard_map.63 = (f32[8192,1024]{1,0:T(8,128)}, f32[512,1024]{1,0:T(8,128)}, f32[32,8192]{1,0:T(8,128)}) custom-call(s32[3]{0:T(128)} %pad_add_fusion.place, bf16[32,8192]{1,0:T(8,128)(2,1)} %get-tuple-element.45.refs_0_, bf16[32,8192]{1,0:T(8,128)(2,1)} %copy-done.3, bf16[32,8192]{1,0:T(8,128)(2,1)} %copy-done, ...), custom_call_target="tpu_custom_call", output_to_operand_aliasing={{2}: (14, {})} | custom-call | flops 10737418240 | bytes 60293120 | tf_op jit(solution)/shard_map/pallas_call | solution.py:71
  136.2 4.6 %collective-permute-done.26 = bf16[32,8192]{1,0:T(8,128)(2,1)} collective-permute-done((bf16[32,8192]{1,0:T(8,128)(2,1)}, bf16[32,8192]{1,0:T(8,128)(2,1)}, u32[]{:S(2)}, u32[]{:S(2)}) %collective-permute-start.26) | collective-permute-done | bytes 524320 | tf_op jit(solution)/shard_map/ppermute | solution.py:19
  140.8 2.3 %fusion = (bf16[32,8192]{1,0:T(8,128)(2,1)}, f32[32,8192]{1,0:T(8,128)}) fusion(f32[32,8192]{1,0:T(8,128)S(1)} %copy-done.7, bf16[32,8192]{1,0:T(8,128)(2,1)} %collective-permute-done.26), kind=kLoop, calls=%fused_computation.14 | loop fusion | flops 786432 | bytes 3145728 | tf_op jit(solution)/shard_map/convert_element_type | solution.py:189
  143.1 1.5 collective-permute-start.28
  145.5 8.9 %shard_map.65 = (f32[256,1024]{1,0:T(8,128)}, bf16[256,1024]{1,0:T(8,128)(2,1)}) custom-call(s32[3]{0:T(128)} %pad_add_fusion.place, bf16[32,8192]{1,0:T(8,128)(2,1)} %get-tuple-element.45.refs_0_, bf16[32,8192]{1,0:T(8,128)(2,1)} %copy-done.3, bf16[32,8192]{1,0:T(8,128)(2,1)} %copy-done, bf16[32,8192]{1,0:T(8,128)(2,1)} %copy-done.4, ...), custom_call_target="tpu_custom_call" | custom-call | flops 3221225472 | bytes 26214400 | tf_op jit(solution)/shard_map/pallas_call | solution.py:71
  155.0 1.8 %collective-permute-done.28.refs_1_ = bf16[32,8192]{1,0:T(8,128)(2,1)} collective-permute-done((bf16[32,8192]{1,0:T(8,128)(2,1)}, bf16[32,8192]{1,0:T(8,128)(2,1)}, u32[]{:S(2)}, u32[]{:S(2)}) %collective-permute-start.28) | collective-permute-done | bytes 524320 | tf_op jit(solution)/shard_map/ppermute | solution.py:19
  156.8 3.0 %shard_map.66.refs_13_ = bf16[32,8192]{1,0:T(8,128)(2,1)} custom-call(s32[3]{0:T(128)} %pad_add_fusion.place, f32[32,8192]{1,0:T(8,128)} %get-tuple-element.74.refs_13_.refs_0_, bf16[32,8192]{1,0:T(8,128)(2,1)} %collective-permute-done.28.refs_1_, bf16[256,1024]{1,0:T(8,128)(2,1)} %get-tuple-element.71.refs_2_), custom_call_target="tpu_custom_call" | custom-call | flops 201326592 | bytes 2097152 | tf_op jit(solution)/shard_map/pallas_call | solution.py:71
  159.7 8.9 %shard_map.67.refs_2_ = f32[8192,1024]{1,0:T(8,128)} custom-call(s32[3]{0:T(128)} %pad_add_fusion.place, bf16[32,8192]{1,0:T(8,128)(2,1)} %get-tuple-element.45.refs_0_, bf16[32,8192]{1,0:T(8,128)(2,1)} %copy-done.3, bf16[32,8192]{1,0:T(8,128)(2,1)} %copy-done, bf16[32,8192]{1,0:T(8,128)(2,1)} %copy-done.4, ...), custom_call_target="tpu_custom_call", output_to_operand_aliasing={{}: (13, {})} | custom-call | flops 3221225472 | bytes 73924608 | tf_op jit(solution)/shard_map/pallas_call | solution.py:71
  169.4 2.2 %shard_map.68 = bf16[256,1024]{1,0:T(8,128)(2,1)} custom-call(s32[3]{0:T(128)} %pad_add_fusion.place, f32[256,1024]{1,0:T(8,128)} %get-tuple-element.70.refs_0_, bf16[256,1024]{1,0:T(8,128)(2,1)} %copy-done.16, f32[8192,1024]{1,0:T(8,128)} %shard_map.67.refs_2_), custom_call_target="tpu_custom_call" | custom-call | bytes 2097152 | tf_op jit(solution)/shard_map/pallas_call | solution.py:71
  (103 shorter events, 17.4 us)
Async XLA Ops:
  0.6 17.2 %collective-permute-start = (bf16[32,8192]{1,0:T(8,128)(2,1)}, bf16[32,8192]{1,0:T(8,128)(2,1)S(1)}, u32[]{:S(2)}, u32[]{:S(2)}) collective-permute-start(bf16[32,8192]{1,0:T(8,128)(2,1)} %refs_0_.3), channel_id=1, source_target_pairs={{0,1},{1,0},{2,3},{3,2},{4,5},{5,4},{6,7},{7,6},{8,9},{9,8},{10,11... | collective-permute-start | bytes 1572872 | tf_op jit(solution)/shard_map/ppermute | solution.py:19
  14.9 1.8 %collective-permute-start.1 = (bf16[32,4096]{1,0:T(8,128)(2,1)}, bf16[32,4096]{1,0:T(8,128)(2,1)S(1)}, u32[]{:S(2)}, u32[]{:S(2)}) collective-permute-start(bf16[32,4096]{1,0:T(8,128)(2,1)} %get-tuple-element.39), channel_id=1, source_target_pairs={{0,2},{2,0},{4,6},{6,4},{8,10},{10,8},{12,14},{14,12},{16,18},{18,... | collective-permute-start | bytes 786440 | tf_op jit(solution)/shard_map/ppermute | solution.py:19
  15.0 2.1 %collective-permute-start.2 = (bf16[32,4096]{1,0:T(8,128)(2,1)}, bf16[32,4096]{1,0:T(8,128)(2,1)S(1)}, u32[]{:S(2)}, u32[]{:S(2)}) collective-permute-start(bf16[32,4096]{1,0:T(8,128)(2,1)} %get-tuple-element.40), channel_id=1, source_target_pairs={{0,2},{2,0},{4,6},{6,4},{8,10},{10,8},{12,14},{14,12},{16,18},{18,... | collective-permute-start | bytes 786440 | tf_op jit(solution)/shard_map/ppermute | solution.py:19
  15.5 2.0 %collective-permute-start.3 = (bf16[32,4096]{1,0:T(8,128)(2,1)}, bf16[32,4096]{1,0:T(8,128)(2,1)S(1)}, u32[]{:S(2)}, u32[]{:S(2)}) collective-permute-start(bf16[32,4096]{1,0:T(8,128)(2,1)} %get-tuple-element.42), channel_id=1, source_target_pairs={{0,2},{2,0},{4,6},{6,4},{8,10},{10,8},{12,14},{14,12},{16,18},{18,... | collective-permute-start | bytes 786440 | tf_op jit(solution)/shard_map/ppermute | solution.py:19
  15.5 2.3 %collective-permute-start.4 = (bf16[32,4096]{1,0:T(8,128)(2,1)}, bf16[32,4096]{1,0:T(8,128)(2,1)S(1)}, u32[]{:S(2)}, u32[]{:S(2)}) collective-permute-start(bf16[32,4096]{1,0:T(8,128)(2,1)} %get-tuple-element.43), channel_id=1, source_target_pairs={{0,2},{2,0},{4,6},{6,4},{8,10},{10,8},{12,14},{14,12},{16,18},{18,... | collective-permute-start | bytes 786440 | tf_op jit(solution)/shard_map/ppermute | solution.py:19
  22.8 26.9 %collective-permute-start.9 = (bf16[64,8192]{1,0:T(8,128)(2,1)}, bf16[64,8192]{1,0:T(8,128)(2,1)}, u32[]{:S(2)}, u32[]{:S(2)}) collective-permute-start(bf16[64,8192]{1,0:T(8,128)(2,1)} %get-tuple-element.49.refs_4_), channel_id=1, source_target_pairs={{0,4},{2,6},{4,0},{6,2},{8,12},{10,14},{12,8},{14,10},{16,20},{18,... | collective-permute-start | bytes 3145736 | tf_op jit(solution)/shard_map/ppermute | solution.py:19
  24.3 13.7 %collective-permute-start.7 = (bf16[256,1024]{1,0:T(8,128)(2,1)S(1)}, bf16[256,1024]{1,0:T(8,128)(2,1)S(1)}, u32[]{:S(2)}, u32[]{:S(2)}) collective-permute-start(bf16[256,1024]{1,0:T(8,128)(2,1)S(1)} %copy-done.14), channel_id=1, source_target_pairs={{0,1},{1,0},{2,3},{3,2},{4,5},{5,4},{6,7},{7,6},{8,9},{9,8},{10,11... | collective-permute-start | bytes 1572872 | tf_op jit(solution)/shard_map/ppermute | solution.py:19
  24.9 24.3 %collective-permute-start.8 = (bf16[32,8192]{1,0:T(8,128)(2,1)}, bf16[32,8192]{1,0:T(8,128)(2,1)S(1)}, u32[]{:S(2)}, u32[]{:S(2)}) collective-permute-start(bf16[32,8192]{1,0:T(8,128)(2,1)} %get-tuple-element.51), channel_id=1, source_target_pairs={{0,2},{2,0},{4,6},{6,4},{8,10},{10,8},{12,14},{14,12},{16,18},{18,... | collective-permute-start | bytes 1572872 | tf_op jit(solution)/shard_map/ppermute | solution.py:19
  24.9 34.1 %collective-permute-start.5 = (bf16[32,8192]{1,0:T(8,128)(2,1)}, bf16[32,8192]{1,0:T(8,128)(2,1)S(1)}, u32[]{:S(2)}, u32[]{:S(2)}) collective-permute-start(bf16[32,8192]{1,0:T(8,128)(2,1)} %get-tuple-element.46), channel_id=1, source_target_pairs={{0,8},{2,10},{4,12},{6,14},{8,0},{10,2},{12,4},{14,6},{16,24},{18,... | collective-permute-start | bytes 1572872 | tf_op jit(solution)/shard_map/ppermute | solution.py:19
  26.5 26.5 %collective-permute-start.6 = (bf16[32,8192]{1,0:T(8,128)(2,1)}, bf16[32,8192]{1,0:T(8,128)(2,1)S(1)}, u32[]{:S(2)}, u32[]{:S(2)}) collective-permute-start(bf16[32,8192]{1,0:T(8,128)(2,1)} %get-tuple-element.46), channel_id=1, source_target_pairs={{0,16},{2,18},{4,20},{6,22},{8,24},{10,26},{12,28},{14,30},{16,0},... | collective-permute-start | bytes 1572872 | tf_op jit(solution)/shard_map/ppermute | solution.py:19
  49.1 4.9 %collective-permute-start.20 = (bf16[32,8192]{1,0:T(8,128)(2,1)}, bf16[32,8192]{1,0:T(8,128)(2,1)}, u32[]{:S(2)}, u32[]{:S(2)}) collective-permute-start(bf16[32,8192]{1,0:T(8,128)(2,1)} %get-tuple-element.63.refs_14_), channel_id=1, source_target_pairs={{0,2},{2,0},{4,6},{6,4},{8,10},{10,8},{12,14},{14,12},{16,18},{18,... | collective-permute-start | bytes 1572872 | tf_op jit(solution)/shard_map/ppermute | solution.py:19
  49.2 6.2 %collective-permute-start.19 = (bf16[32,8192]{1,0:T(8,128)(2,1)}, bf16[32,8192]{1,0:T(8,128)(2,1)}, u32[]{:S(2)}, u32[]{:S(2)}) collective-permute-start(bf16[32,8192]{1,0:T(8,128)(2,1)} %get-tuple-element.61), channel_id=1, source_target_pairs={{0,2},{2,0},{4,6},{6,4},{8,10},{10,8},{12,14},{14,12},{16,18},{18,... | collective-permute-start | bytes 1572872 | tf_op jit(solution)/shard_map/ppermute | solution.py:19
  52.9 38.6 %copy-start = (bf16[32,8192]{1,0:T(8,128)(2,1)}, bf16[32,8192]{1,0:T(8,128)(2,1)S(1)}, u32[]{:S(2)}) copy-start(bf16[32,8192]{1,0:T(8,128)(2,1)S(1)} %collective-permute-done.6.refs_2_) | copy-start | bytes 1572868
  53.0 23.6 %collective-permute-start.10 = (bf16[64,8192]{1,0:T(8,128)(2,1)S(1)}, bf16[64,8192]{1,0:T(8,128)(2,1)}, u32[]{:S(2)}, u32[]{:S(2)}) collective-permute-start(bf16[64,8192]{1,0:T(8,128)(2,1)S(1)} %pad_maximum_fusion.1.refs_4_), channel_id=1, source_target_pairs={{0,8},{2,10},{4,12},{6,14},{8,0},{10,2},{12,4},{14,6},{16,24},{18,... | collective-permute-start | bytes 3145736 | tf_op jit(solution)/shard_map/ppermute | solution.py:19
  57.8 26.4 %collective-permute-start.21 = (bf16[64,8192]{1,0:T(8,128)(2,1)}, bf16[64,8192]{1,0:T(8,128)(2,1)}, u32[]{:S(2)}, u32[]{:S(2)}) collective-permute-start(bf16[64,8192]{1,0:T(8,128)(2,1)} %pad_maximum_fusion.2), channel_id=1, source_target_pairs={{0,4},{2,6},{4,0},{6,2},{8,12},{10,14},{12,8},{14,10},{16,20},{18,... | collective-permute-start | bytes 3145736 | tf_op jit(solution)/shard_map/ppermute | solution.py:19
  58.3 32.7 %collective-permute-start.24 = (bf16[32,8192]{1,0:T(8,128)(2,1)}, bf16[32,8192]{1,0:T(8,128)(2,1)}, u32[]{:S(2)}, u32[]{:S(2)}) collective-permute-start(bf16[32,8192]{1,0:T(8,128)(2,1)} %get-tuple-element.67), channel_id=1, source_target_pairs={{0,2},{2,0},{4,6},{6,4},{8,10},{10,8},{12,14},{14,12},{16,18},{18,... | collective-permute-start | bytes 1572872 | tf_op jit(solution)/shard_map/ppermute | solution.py:19
  58.4 20.4 %collective-permute-start.22 = (bf16[32,8192]{1,0:T(8,128)(2,1)}, bf16[32,8192]{1,0:T(8,128)(2,1)}, u32[]{:S(2)}, u32[]{:S(2)}) collective-permute-start(bf16[32,8192]{1,0:T(8,128)(2,1)} %get-tuple-element.65), channel_id=1, source_target_pairs={{0,2},{2,0},{4,6},{6,4},{8,10},{10,8},{12,14},{14,12},{16,18},{18,... | collective-permute-start | bytes 1572872 | tf_op jit(solution)/shard_map/ppermute | solution.py:19
  59.0 32.1 %copy-start.3 = (bf16[32,8192]{1,0:T(8,128)(2,1)}, bf16[32,8192]{1,0:T(8,128)(2,1)S(1)}, u32[]{:S(2)}) copy-start(bf16[32,8192]{1,0:T(8,128)(2,1)S(1)} %collective-permute-done.5.refs_1_) | copy-start | bytes 1572868
  59.0 32.5 %collective-permute-start.18 = (bf16[32,8192]{1,0:T(8,128)(2,1)}, bf16[32,8192]{1,0:T(8,128)(2,1)}, u32[]{:S(2)}, u32[]{:S(2)}) collective-permute-start(bf16[32,8192]{1,0:T(8,128)(2,1)} %get-tuple-element.59), channel_id=1, source_target_pairs={{0,2},{2,0},{4,6},{6,4},{8,10},{10,8},{12,14},{14,12},{16,18},{18,... | collective-permute-start | bytes 1572872 | tf_op jit(solution)/shard_map/ppermute | solution.py:19
  77.7 32.4 %collective-permute-start.16 = (bf16[128,5120]{1,0:T(8,128)(2,1)S(1)}, bf16[128,5120]{1,0:T(8,128)(2,1)}, u32[]{:S(2)}, u32[]{:S(2)}) collective-permute-start(bf16[128,5120]{1,0:T(8,128)(2,1)S(1)} %pad_maximum_fusion.refs_2_.refs_15_), channel_id=1, source_target_pairs={{0,4},{2,6},{4,0},{6,2},{8,12},{10,14},{12,8},{14,10},{16,20},{18,... | collective-permute-start | bytes 3932168 | tf_op jit(solution)/shard_map/ppermute | solution.py:19
  86.6 9.9 %collective-permute-start.23 = (bf16[32,8192]{1,0:T(8,128)(2,1)}, bf16[32,8192]{1,0:T(8,128)(2,1)}, u32[]{:S(2)}, u32[]{:S(2)}) collective-permute-start(bf16[32,8192]{1,0:T(8,128)(2,1)} %add_convert_fusion.refs_16_), channel_id=1, source_target_pairs={{0,8},{2,10},{4,12},{6,14},{8,0},{10,2},{12,4},{14,6},{16,24},{18,... | collective-permute-start | bytes 1572872 | tf_op jit(solution)/shard_map/ppermute | solution.py:19
  87.6 26.1 %collective-permute-start.11 = (bf16[32,8192]{1,0:T(8,128)(2,1)S(1)}, bf16[32,8192]{1,0:T(8,128)(2,1)S(1)}, u32[]{:S(2)}, u32[]{:S(2)}) collective-permute-start(bf16[32,8192]{1,0:T(8,128)(2,1)S(1)} %copy-done.2), channel_id=1, source_target_pairs={{0,2},{2,0},{4,6},{6,4},{8,10},{10,8},{12,14},{14,12},{16,18},{18,... | collective-permute-start | bytes 1572872 | tf_op jit(solution)/shard_map/ppermute | solution.py:19
  88.9 24.9 %copy-start.4 = (bf16[32,8192]{1,0:T(8,128)(2,1)}, bf16[32,8192]{1,0:T(8,128)(2,1)S(1)}, u32[]{:S(2)}) copy-start(bf16[32,8192]{1,0:T(8,128)(2,1)S(1)} %slice.59.refs_3_) | copy-start | bytes 1572868
  91.0 23.3 %collective-permute-start.12 = (bf16[32,8192]{1,0:T(8,128)(2,1)S(1)}, bf16[32,8192]{1,0:T(8,128)(2,1)S(1)}, u32[]{:S(2)}, u32[]{:S(2)}) collective-permute-start(bf16[32,8192]{1,0:T(8,128)(2,1)S(1)} %collective-permute-done.5.refs_1_), channel_id=1, source_target_pairs={{0,2},{2,0},{4,6},{6,4},{8,10},{10,8},{12,14},{14,12},{16,18},{18,... | collective-permute-start | bytes 1572872 | tf_op jit(solution)/shard_map/ppermute | solution.py:19
  91.5 25.1 %collective-permute-start.13 = (bf16[32,8192]{1,0:T(8,128)(2,1)S(1)}, bf16[32,8192]{1,0:T(8,128)(2,1)S(1)}, u32[]{:S(2)}, u32[]{:S(2)}) collective-permute-start(bf16[32,8192]{1,0:T(8,128)(2,1)S(1)} %collective-permute-done.6.refs_2_), channel_id=1, source_target_pairs={{0,2},{2,0},{4,6},{6,4},{8,10},{10,8},{12,14},{14,12},{16,18},{18,... | collective-permute-start | bytes 1572872 | tf_op jit(solution)/shard_map/ppermute | solution.py:19
  96.5 20.2 %collective-permute-start.14 = (bf16[32,8192]{1,0:T(8,128)(2,1)S(1)}, bf16[32,8192]{1,0:T(8,128)(2,1)S(1)}, u32[]{:S(2)}, u32[]{:S(2)}) collective-permute-start(bf16[32,8192]{1,0:T(8,128)(2,1)S(1)} %slice.59.refs_3_), channel_id=1, source_target_pairs={{0,2},{2,0},{4,6},{6,4},{8,10},{10,8},{12,14},{14,12},{16,18},{18,... | collective-permute-start | bytes 1572872 | tf_op jit(solution)/shard_map/ppermute | solution.py:19
  110.1 6.5 %collective-permute-start.17 = (bf16[128,5120]{1,0:T(8,128)(2,1)}, bf16[128,5120]{1,0:T(8,128)(2,1)S(1)}, u32[]{:S(2)}, u32[]{:S(2)}) collective-permute-start(bf16[128,5120]{1,0:T(8,128)(2,1)} %collective-permute-done.16.refs_8_), channel_id=1, source_target_pairs={{0,2},{2,0},{4,6},{6,4},{8,10},{10,8},{12,14},{14,12},{16,18},{18,... | collective-permute-start | bytes 3932168 | tf_op jit(solution)/shard_map/ppermute | solution.py:19
  113.7 22.4 %collective-permute-start.15 = (bf16[128,3072]{1,0:T(8,128)(2,1)}, bf16[128,3072]{1,0:T(8,128)(2,1)}, u32[]{:S(2)}, u32[]{:S(2)}) collective-permute-start(bf16[128,3072]{1,0:T(8,128)(2,1)} %pad_maximum_fusion.3), channel_id=1, source_target_pairs={{0,4},{2,6},{4,0},{6,2},{8,12},{10,14},{12,8},{14,10},{16,20},{18,... | collective-permute-start | bytes 2359304 | tf_op jit(solution)/shard_map/ppermute | solution.py:19
  114.3 26.5 %collective-permute-start.26 = (bf16[32,8192]{1,0:T(8,128)(2,1)}, bf16[32,8192]{1,0:T(8,128)(2,1)}, u32[]{:S(2)}, u32[]{:S(2)}) collective-permute-start(bf16[32,8192]{1,0:T(8,128)(2,1)} %get-tuple-element.75), channel_id=1, source_target_pairs={{0,16},{2,18},{4,20},{6,22},{8,24},{10,26},{12,28},{14,30},{16,0},... | collective-permute-start | bytes 1572872 | tf_op jit(solution)/shard_map/ppermute | solution.py:19
  136.1 8.5 %collective-permute-start.25 = (bf16[128,3072]{1,0:T(8,128)(2,1)}, bf16[128,3072]{1,0:T(8,128)(2,1)S(1)}, u32[]{:S(2)}, u32[]{:S(2)}) collective-permute-start(bf16[128,3072]{1,0:T(8,128)(2,1)} %shard_map.64.refs_8_), channel_id=1, source_target_pairs={{0,2},{2,0},{4,6},{6,4},{8,10},{10,8},{12,14},{14,12},{16,18},{18,... | collective-permute-start | bytes 2359304 | tf_op jit(solution)/shard_map/ppermute | solution.py:19
  143.1 13.7 %collective-permute-start.28 = (bf16[32,8192]{1,0:T(8,128)(2,1)}, bf16[32,8192]{1,0:T(8,128)(2,1)}, u32[]{:S(2)}, u32[]{:S(2)}) collective-permute-start(bf16[32,8192]{1,0:T(8,128)(2,1)} %get-tuple-element.73), channel_id=1, source_target_pairs={{0,1},{1,0},{2,3},{3,2},{4,5},{5,4},{6,7},{7,6},{8,9},{9,8},{10,11... | collective-permute-start | bytes 1572872 | tf_op jit(solution)/shard_map/ppermute | solution.py:19
  154.4 14.2 %collective-permute-start.27 = (bf16[256,1024]{1,0:T(8,128)(2,1)}, bf16[256,1024]{1,0:T(8,128)(2,1)S(1)}, u32[]{:S(2)}, u32[]{:S(2)}) collective-permute-start(bf16[256,1024]{1,0:T(8,128)(2,1)} %get-tuple-element.71.refs_2_), channel_id=1, source_target_pairs={{0,1},{1,0},{2,3},{3,2},{4,5},{5,4},{6,7},{7,6},{8,9},{9,8},{10,11... | collective-permute-start | bytes 1572872 | tf_op jit(solution)/shard_map/ppermute | solution.py:19
  (20 other events, 79.2 us)

commit v3 on v2

--- a/solution.py
+++ b/solution.py
@@ -10,8 +10,7 @@
 
 BF16 = jnp.bfloat16
 F32 = jnp.float32
-VMEM_LIMIT = 60 * 1024 * 1024
-VMEM_MOST = 63 * 1024 * 1024
+VMEM_LIMIT = 67000000
 LANES = 128
 
 
@@ -50,7 +49,6 @@
         scratch=(),
         aliases=None,
         flops=0,
-        limit=VMEM_LIMIT,
         late=(),
     ):
         count, extra = len(inputs), len(self.last)
@@ -79,7 +77,7 @@
             out_shape=list(outs) + [jax.ShapeDtypeStruct(v.shape, v.dtype) for v in late],
             input_output_aliases={1 + k: v for k, v in (aliases or {}).items()}
             | {1 + count + k: made + k for k in range(len(late))},
-            compiler_params=pltpu.CompilerParams(vmem_limit_bytes=limit),
+            compiler_params=pltpu.CompilerParams(vmem_limit_bytes=VMEM_LIMIT),
             cost_estimate=pl.CostEstimate(flops=flops, bytes_accessed=moved, transcendentals=0),
         )(self.place, *inputs, *late, *self.last)
         self.last = [result[made - 1]]
@@ -194,7 +192,7 @@
     return values, other
 
 
-def rotate(chain, pairs, places, factor, copies=1, sums=()):
+def rotate(chain, pairs, places, factor, copies=1, sums=(), first=0):
     rows = pairs[0][0].shape[0]
     widths = [own.shape[1] for own, _ in pairs]
     width = sum(widths)
@@ -209,7 +207,7 @@
                 other = terms.pop(0)
                 there = slice(start, start + other.shape[1])
                 total = own[:, there].astype(F32) + other[...].astype(F32)
-                outs[-1][k * rows : (k + 1) * rows, there] = total.astype(BF16)
+                outs[copies][k * rows : (k + 1) * rows, there] = total.astype(BF16)
                 start += other.shape[1]
         upper = bit(place[2], places - 1)
         columns = []
@@ -246,10 +244,15 @@
                 outs[copy][:, block * LANES : (block + 1) * LANES] = result[
                     block * rows : (block + 1) * rows
                 ]
+            if block * LANES < first:
+                outs[-1][:, block * LANES : (block + 1) * LANES] = result[
+                    block * rows : (block + 1) * rows
+                ]
 
     flat = [v for pair in pairs for v in pair]
     flat += [v for own, others in sums for v in [own] + list(others)]
     shapes = [(rows, width)] * copies + [(len(sums) * rows, width)] * (len(sums) > 0)
+    shapes += [(rows, first)] * (first > 0)
     return chain(
         body,
         flat,
@@ -274,12 +277,15 @@
     out=0,
     last=False,
     late=(),
+    origin=None,
 ):
     features, columns = weight.shape
-    tile = min(1024, width)
+    origin = columns_from if origin is None else origin
+    tile = math.gcd(1024, math.gcd(columns_from - origin, math.gcd(columns_from, width)))
     steps = width // tile
     first = columns_from // tile
-    count = len(grads)
+    ahead = (columns_from - origin) // tile
+    count = lax.axis_size("tensor")
     held = count * inner
     groups = len(gathered)
     flat = [v for group in gathered for v in group]
@@ -287,9 +293,10 @@
     share = whole((out * inner, columns))
     inputs = list(flat)
     specs = [
-        across(v.shape[0], tile)
-        if v.shape[1] == width
-        else pl.BlockSpec((v.shape[0], tile), lambda i: (0, first + i))
+        pl.BlockSpec(
+            (v.shape[0], tile),
+            lambda i, skip=first if v.shape[1] == features else ahead: (0, skip + i),
+        )
         for v in flat
     ]
     outs, out_specs, scratch, aliases = [], [], [], {}
@@ -305,7 +312,7 @@
         specs.append(tall)
         if before is not None:
             inputs.append(before)
-            specs.append(square)
+            specs.append(whole(before.shape))
         if last:
             outs += [array(out * inner, columns, F32)] + [array(out * inner, columns)] * (count - 1)
             out_specs += [share] * count
@@ -353,10 +360,15 @@
 
             @pl.when(step == 0)
             def _():
-                total[...] = jnp.zeros_like(total) if earlier is None else earlier[...]
-
-            total[...] += jnp.dot(
-                rotated[(groups - out) * held :], weight[...], preferred_element_type=F32
+                filled = 0 if before is None else before.shape[0]
+                if filled:
+                    total[:filled, :] = earlier[...]
+                if filled < out * held:
+                    total[filled:, :] = jnp.zeros((out * held - filled, columns), F32)
+
+            mine = min(groups, out)
+            total[(out - mine) * held :, :] += jnp.dot(
+                rotated[(groups - mine) * held :], weight[...], preferred_element_type=F32
             )
             if last:
 
@@ -381,7 +393,6 @@
         scratch,
         aliases,
         flops=2 * width * columns * held * (groups * grad + out),
-        limit=VMEM_MOST,
         late=late,
     )
 
@@ -401,9 +412,11 @@
             target = place[0] ^ reversed_bits(position, low_bits)
             out[pl.ds(pl.multiple_of(target * rows, rows), rows), :] = total.astype(BF16)
 
-    shape = shares[0].shape
+    tokens, columns = shares[0].shape
+    tile = columns
+    block = across(tokens, tile)
     (out,) = chain(
-        body, shares, [whole(shape)] * len(shares), [array(*shape)], [whole(shape)]
+        body, shares, [block] * len(shares), [array(tokens, columns)], [block], columns // tile
     )
     return out
 
@@ -447,7 +460,11 @@
     own = core_send(own)
     far = [swap(ordered, "tensor", q) for q in range(1, tensor)]
     half = len(own) // 2
-    sent, rotated, message = rotate(chain, [rotation], top_bits, factor, 2, own[half:])
+    cut = width * 5 // 8
+    sent, rotated, message, leading = rotate(
+        chain, [rotation], top_bits, factor, 2, own[half:], cut
+    )
+    leading = near(leading, 1)
     came = near(message, 1)
     own = [terms + [came[k * rows : (k + 1) * rows]] for k, terms in enumerate(own[:half])]
 
@@ -485,7 +502,7 @@
         held = list(chain.gate([terms[0] for part in parts for terms in part], after))
         return [[[held.pop(0)] + terms[1:] for terms in part] for part in parts]
 
-    others = gate_first(others, [message])
+    others = gate_first(others, [message, leading])
     others = [split_send(part, 1)[0] for part in others]
 
     order = [
@@ -495,11 +512,10 @@
     ]
     here = [gathered[j] for j in order]
     core = [near(block, 0) for block in here]
-    cut = width * 5 // 8
     ranges = [(0, cut), (cut, width - cut)]
     across_sent = [
-        jnp.concatenate([block[:, start : start + size] for block in here], axis=0)
-        for start, size in ranges
+        jnp.concatenate([block[:, start : start + size] for block in blocks], axis=0)
+        for (start, size), blocks in zip(ranges, (here[1:], here))
     ]
     others = gate_first(others, across_sent[:1])
     messages = []
@@ -508,8 +524,10 @@
         others = [part for part, _, _ in sent_parts]
         messages = [message for _, _, message in sent_parts]
     chain.follow(across_sent[0], *messages)
+    start, size = ranges[1]
+    (total,) = product(chain, [here, core], [], weight, start, size, inner, out=2)
     grads = [ordered] + far
-    arrived = [near(across_sent[0], 1)]
+    arrived = list(chain.gate([near(across_sent[0], 1)], [total]))
 
     some = exchange_order([add(*part[0]) for part in [own] + others], apart)
     for p in reversed(range(top_bits)):
@@ -522,10 +540,11 @@
     kept, came = pairs[0]
     arrived.append(near(across_sent[1], 1))
     arrived_core = [near(arrived[0], 0)]
+    leading_core = near(leading, 0)
     start, size = ranges[0]
     weight_grad, total, kept = product(
-        chain, [here, core, [arrived[0]], [arrived_core[0]]], grads, weight, start, size, inner,
-        grad=True, out=4, late=[kept],
+        chain, [here, core, [leading, arrived[0]], [leading_core, arrived_core[0]]], grads, weight, start, size, inner,
+        before=total, grad=True, out=4, late=[kept],
     )
     (arrived[1],) = chain.gate(arrived[1:], [total])
     arrived_core.append(near(arrived[1], 0))
@@ -534,14 +553,19 @@
     chain.follow(rotated_grad)
     start, size = ranges[1]
     result = product(
-        chain, [here, core, [arrived[1]], [arrived_core[1]]], grads, weight, start, size, inner,
+        chain, [[arrived[1]], [arrived_core[1]]], grads, weight, start, size, inner,
         before=total, out=4, last=True,
     )
     shares = [result[0]] + [swap(result[q], "tensor", q) for q in range(1, tensor)]
+    held = [here, core, [arrived[1]], [arrived_core[1]]]
+    part = size * 2 // 3 // LANES * LANES
+    (weight_grad,) = product(
+        chain, held, grads, weight, start, part, inner, into=weight_grad, grad=True, origin=start
+    )
     (in_grad,) = rotate(chain, [final], top_bits, factor)
     (weight_grad,) = product(
-        chain, [here, core, [arrived[1]], [arrived_core[1]]], grads, weight, start, size, inner,
-        into=weight_grad, grad=True,
+        chain, held, grads, weight, start + part, size - part, inner, into=weight_grad, grad=True,
+        origin=start,
     )
     outputs = finish(chain, shares, rows, low_bits)
     return (outputs, in_grad, weight_grad)

time: 172 us -> 167 us (0.971)
  waiting for transfers between devices: 60.6 us -> 42.5 us
  Pallas kernels: 65.4 us -> 73.2 us
  starting transfers between devices: 19.7 us -> 25 us
  local copies, waits for them, and re-layouts: 9.9 us -> 7.73 us
  other arithmetic: 15.1 us -> 17 us
    ppermute x29 -> x31, waiting for transfers between devices: 60.6 us -> 42.5 us  [swap(): lax.ppermute(values, axis, [(i, i ^ mask) for i in range(lax.axis_size(ax...]
    pallas_call x8 -> x10, Pallas kernels: 65.4 us -> 73.2 us  [__call__(): pl.pallas_call(kernel, grid=(steps,), in_specs=[pl.BlockSpec(memory_space...]
    unnamed x46 -> x22, local copies, waits for them, and re-layouts: 6.51 us -> 0.84 us
    ppermute x29 -> x31, starting transfers between devices: 19.7 us -> 25 us  [swap(): lax.ppermute(values, axis, [(i, i ^ mask) for i in range(lax.axis_size(ax...]
    slice x8 -> x7, local copies, waits for them, and re-layouts: 2.23 us -> 5.82 us  [per_device(): block[:, start:start + size]]
  transfers between devices with their start and end apart: 29 -> 31, of which waited for: 12 -> 12; matrix products, arithmetic and copies ran while one was open for 11% -> 14% of each run, Pallas kernels for 34% -> 40%
where the time goes in v3:
time: 167 us; the launch traced here: 166 us
  Pallas kernels  73.2 us (44%)
  waiting for transfers between devices  42.5 us (25%)
  starting transfers between devices  25 us (15%)
  other arithmetic  17 us (10%)
  local copies, waits for them, and re-layouts  7.73 us (5%)
    pallas_call x10, Pallas kernels, __call__(): pl.pallas_call(kernel, grid=(steps,), in_specs=[pl.BlockSpec(memory_space...  73.2 us
    ppermute x31, waiting for transfers between devices, swap(): lax.ppermute(values, axis, [(i, i ^ mask) for i in range(lax.axis_size(ax...  42.5 us
    ppermute x31, starting transfers between devices, swap(): lax.ppermute(values, axis, [(i, i ^ mask) for i in range(lax.axis_size(ax...  25 us
    convert_element_type x4, other arithmetic, split_send(): add(*t).astype(BF16)  6.27 us
    slice x7, local copies, waits for them, and re-layouts, per_device(): block[:, start:start + size]  5.82 us
    convert_element_type x1, other arithmetic, per_device(): some[j + count].astype(BF16)  3.54 us
  transfers between devices with their start and end apart: 31, of which 12 were waited for; matrix products, arithmetic and copies ran while one was open for 14% of the time, Pallas kernels for 40%

profile of v3, /device:TPU:0, one launch (start us, length us, event | category | flops | bytes accessed | tf_op | source)
XLA Modules:
  0.0 166.4 jit_solution(17591084457408371736)
XLA Ops:
  0.6 3.0 %collective-permute-start = (bf16[32,8192]{1,0:T(8,128)(2,1)}, bf16[32,8192]{1,0:T(8,128)(2,1)}, u32[]{:S(2)}, u32[]{:S(2)}) collective-permute-start(bf16[32,8192]{1,0:T(8,128)(2,1)} %refs_0_.3), channel_id=1, source_target_pairs={{0,1},{1,0},{2,3},{3,2},{4,5},{5,4},{6,7},{7,6},{8,9},{9,8},{10,11... | collective-permute-start | bytes 1572872 | tf_op jit(solution)/shard_map/ppermute | solution.py:18
  4.3 10.6 %shard_map.58 = (bf16[32,8192]{1,0:T(8,128)(2,1)}, bf16[32,8192]{1,0:T(8,128)(2,1)}, bf16[32,8192]{1,0:T(8,128)(2,1)}, bf16[32,8192]{1,0:T(8,128)(2,1)}, bf16[32...) custom-call(s32[3]{0:T(128)} %pad_add_fusion.place, ...), custom_call_target="tpu_custom_call" | custom-call | flops 4294967296 | bytes 22020096 | tf_op jit(solution)/shard_map/pallas_call | solution.py:69
  18.0 4.2 %shard_map.59 = (bf16[32,8192]{1,0:T(8,128)(2,1)}, bf16[32,8192]{1,0:T(8,128)(2,1)}, bf16[64,8192]{1,0:T(8,128)(2,1)}, bf16[32,5120]{1,0:T(8,128)(2,1)}) custom-call(s32[3]{0:T(128)} %pad_add_fusion.place, bf16[32,8192]{1,0:T(8,128)(2,1)} %refs_0_.3, bf16[32,8192]{1,0:T(8,128)(2,1)} %collective-permute-done.refs_1_, ...), custom_call_target="tpu_custom_call" | custom-call | flops 201326592 | bytes 5570560 | tf_op jit(solution)/shard_map/pallas_call | solution.py:69
  22.2 1.5 collective-permute-start.9
  24.2 2.6 %collective-permute-start.6 = (bf16[32,8192]{1,0:T(8,128)(2,1)}, bf16[32,8192]{1,0:T(8,128)(2,1)}, u32[]{:S(2)}, u32[]{:S(2)}) collective-permute-start(bf16[32,8192]{1,0:T(8,128)(2,1)} %get-tuple-element.47), channel_id=1, source_target_pairs={{0,16},{2,18},{4,20},{6,22},{8,24},{10,26},{12,28},{14,30},{16,0},... | collective-permute-start | bytes 1572872 | tf_op jit(solution)/shard_map/ppermute | solution.py:18
  26.8 1.6 collective-permute-start.5
  28.4 9.3 %collective-permute-done.7.refs_0_.refs_13_.refs_11_ = bf16[256,1024]{1,0:T(8,128)(2,1)} collective-permute-done((bf16[256,1024]{1,0:T(8,128)(2,1)}, bf16[256,1024]{1,0:T(8,128)(2,1)}, u32[]{:S(2)}, u32[]{:S(2)}) %collective-permute-start.7) | collective-permute-done | bytes 524320 | tf_op jit(solution)/shard_map/ppermute | solution.py:18
  38.2 10.4 %shard_map.60 = (bf16[32,8192]{1,0:T(8,128)(2,1)}, bf16[32,8192]{1,0:T(8,128)(2,1)}, bf16[32,8192]{1,0:T(8,128)(2,1)}, bf16[32,8192]{1,0:T(8,128)(2,1)}, bf16[32...) custom-call(s32[3]{0:T(128)} %pad_add_fusion.place, ...), custom_call_target="tpu_custom_call", output_to_operand_aliasing={{8}: (3, {}), {9}: (4, {})} | custom-call | flops 4294967296 | bytes 21495808 | tf_op jit(solution)/shard_map/pallas_call | solution.py:69
  49.1 1.5 add_convert_fusion.3
  52.2 1.2 collective-permute-start.10
  53.5 1.2 collective-permute-done.16.refs_5_.refs_8_
  55.9 1.2 add_convert_fusion.1
  58.2 1.5 collective-permute-start.21
  62.3 14.9 %collective-permute-done.10 = bf16[64,8192]{1,0:T(8,128)(2,1)} collective-permute-done((bf16[64,8192]{1,0:T(8,128)(2,1)S(1)}, bf16[64,8192]{1,0:T(8,128)(2,1)}, u32[]{:S(2)}, u32[]{:S(2)}) %collective-permute-start.10) | collective-permute-done | bytes 1048608 | tf_op jit(solution)/shard_map/ppermute | solution.py:18
  80.3 1.6 collective-permute-start.17
  82.9 2.3 %add_convert_fusion.refs_11_ = bf16[32,8192]{1,0:T(8,128)(2,1)} fusion(bf16[32,8192]{1,0:T(8,128)(2,1)} %copy-done.10, bf16[32,8192]{1,0:T(8,128)(2,1)} %get-tuple-element.61, bf16[64,8192]{1,0:T(8,128)(2,1)} %collective-permute-done.21), kind=kLoop, calls=%fused_computation.6 | loop fusion | flops 1572864 | bytes 2097152 | tf_op jit(solution)/shard_map/convert_element_type | solution.py:450
  85.8 1.6 collective-permute-start.25
  92.3 6.3 %shard_map.63.refs_1_.refs_15_.refs_17_ = f32[256,1024]{1,0:T(8,128)} custom-call(s32[3]{0:T(128)} %pad_add_fusion.place, bf16[32,8192]{1,0:T(8,128)(2,1)} %get-tuple-element.46.refs_0_, bf16[32,8192]{1,0:T(8,128)(2,1)} %collective-permute-done.5.refs_1_, bf16[32,8192]{1,0:T(8,128)(2,1)} %collective-permute-done.6.refs_2_, bf16[32,8192]{1,0:T(8,128)(2,1)} %copy-done, ...), custom_call_target="tpu_custom_call" | custom-call | flops 1610612736 | bytes 22020096 | tf_op jit(solution)/shard_map/pallas_call | solution.py:69
  98.6 6.2 %collective-permute-done.17.refs_0_ = bf16[96,5120]{1,0:T(8,128)(2,1)} collective-permute-done((bf16[96,5120]{1,0:T(8,128)(2,1)}, bf16[96,5120]{1,0:T(8,128)(2,1)}, u32[]{:S(2)}, u32[]{:S(2)}) %collective-permute-start.17) | collective-permute-done | bytes 983072 | tf_op jit(solution)/shard_map/ppermute | solution.py:18
  104.9 1.5 collective-permute-start.11
  106.4 3.5 %select_convert_fusion = (bf16[32,8192]{1,0:T(8,128)(2,1)}, f32[32,8192]{1,0:T(8,128)}) fusion(pred[]{:T(512)S(6)} %eq.3, bf16[32,8192]{1,0:T(8,128)(2,1)} %collective-permute-done.25, bf16[64,8192]{1,0:T(8,128)(2,1)} %collective-permute-done.21, bf16[32,8192]{1,0:T(8,128)(2,1)} %collective-permute-done.24, bf16[32,8192]{1,0:T(8,128)(2,1)S(1)} %copy-done.6, ...), kind=kLoop, calls=%fused_computation.3 | loop fusion | flops 4456448 | bytes 5767169 | tf_op jit(solution)/shard_map/convert_element_type | solution.py:536
  110.0 2.6 %collective-permute-start.28 = (bf16[32,8192]{1,0:T(8,128)(2,1)}, bf16[32,8192]{1,0:T(8,128)(2,1)}, u32[]{:S(2)}, u32[]{:S(2)}) collective-permute-start(bf16[32,8192]{1,0:T(8,128)(2,1)} %get-tuple-element.77), channel_id=1, source_target_pairs={{0,16},{2,18},{4,20},{6,22},{8,24},{10,26},{12,28},{14,30},{16,0},... | collective-permute-start | bytes 1572872 | tf_op jit(solution)/shard_map/ppermute | solution.py:18
  112.6 17.7 %shard_map.65 = (f32[8192,1024]{1,0:T(8,128)}, f32[512,1024]{1,0:T(8,128)}, f32[32,8192]{1,0:T(8,128)}) custom-call(s32[3]{0:T(128)} %pad_add_fusion.place, bf16[32,8192]{1,0:T(8,128)(2,1)} %get-tuple-element.46.refs_0_, bf16[32,8192]{1,0:T(8,128)(2,1)} %collective-permute-done.5.refs_1_, ...), custom_call_target="tpu_custom_call", output_to_operand_aliasing={{2}: (17, {})} | custom-call | flops 10737418240 | bytes 61341696 | tf_op jit(solution)/shard_map/pallas_call | solution.py:69
  130.5 6.2 %collective-permute-done.28 = bf16[32,8192]{1,0:T(8,128)(2,1)} collective-permute-done((bf16[32,8192]{1,0:T(8,128)(2,1)}, bf16[32,8192]{1,0:T(8,128)(2,1)}, u32[]{:S(2)}, u32[]{:S(2)}) %collective-permute-start.28) | collective-permute-done | bytes 524320 | tf_op jit(solution)/shard_map/ppermute | solution.py:18
  136.7 2.3 %fusion = (bf16[32,8192]{1,0:T(8,128)(2,1)}, f32[32,8192]{1,0:T(8,128)}) fusion(f32[32,8192]{1,0:T(8,128)S(1)} %copy-done.8, bf16[32,8192]{1,0:T(8,128)(2,1)} %collective-permute-done.28), kind=kLoop, calls=%fused_computation.14 | loop fusion | flops 786432 | bytes 3145728 | tf_op jit(solution)/shard_map/convert_element_type | solution.py:187
  139.6 7.2 %shard_map.67 = (f32[256,1024]{1,0:T(8,128)}, bf16[256,1024]{1,0:T(8,128)(2,1)}) custom-call(s32[3]{0:T(128)} %pad_add_fusion.place, bf16[128,3072]{1,0:T(8,128)(2,1)} %shard_map.66.refs_0_.refs_8_, bf16[128,3072]{1,0:T(8,128)(2,1)} %collective-permute-done.27.refs_1_.refs_9_, bf16[8192,1024]{1,0:T(8,128)(2,1)} %refs_2_.1, ...), custom_call_target="tpu_custom_call" | custom-call | flops 3221225472 | bytes 22020096 | tf_op jit(solution)/shard_map/pallas_call | solution.py:69
  146.8 1.5 collective-permute-start.29
  148.2 6.8 %shard_map.68.refs_2_.refs_12_ = f32[8192,1024]{1,0:T(8,128)} custom-call(s32[3]{0:T(128)} %pad_add_fusion.place, bf16[32,8192]{1,0:T(8,128)(2,1)} %get-tuple-element.46.refs_0_, bf16[32,8192]{1,0:T(8,128)(2,1)} %collective-permute-done.5.refs_1_, bf16[32,8192]{1,0:T(8,128)(2,1)} %collective-permute-done.6.refs_2_, ...), custom_call_target="tpu_custom_call", output_to_operand_aliasing={{}: (13, {})} | custom-call | flops 2147483648 | bytes 73924608 | tf_op jit(solution)/shard_map/pallas_call | solution.py:69
  155.1 3.0 %shard_map.69.refs_13_ = bf16[32,8192]{1,0:T(8,128)(2,1)} custom-call(s32[3]{0:T(128)} %pad_add_fusion.place, f32[32,8192]{1,0:T(8,128)} %get-tuple-element.76.refs_5_.refs_0_, bf16[32,8192]{1,0:T(8,128)(2,1)} %collective-permute-done.30.refs_1_, f32[8192,1024]{1,0:T(8,128)} %shard_map.68.refs_2_.refs_12_), custom_call_target="tpu_custom_call" | custom-call | flops 201326592 | bytes 2097152 | tf_op jit(solution)/shard_map/pallas_call | solution.py:69
  158.0 4.9 %shard_map.70.refs_2_ = f32[8192,1024]{1,0:T(8,128)} custom-call(s32[3]{0:T(128)} %pad_add_fusion.place, bf16[32,8192]{1,0:T(8,128)(2,1)} %get-tuple-element.46.refs_0_, bf16[32,8192]{1,0:T(8,128)(2,1)} %collective-permute-done.5.refs_1_, bf16[32,8192]{1,0:T(8,128)(2,1)} %collective-permute-done.6.refs_2_, ...), custom_call_target="tpu_custom_call", output_to_operand_aliasing={{}: (13, {})} | custom-call | flops 1073741824 | bytes 73924608 | tf_op jit(solution)/shard_map/pallas_call | solution.py:69
  162.9 1.2 collective-permute-done.29.refs_1_
  164.1 2.2 %shard_map.71 = bf16[256,1024]{1,0:T(8,128)(2,1)} custom-call(s32[3]{0:T(128)} %pad_add_fusion.place, f32[256,1024]{1,0:T(8,128)} %get-tuple-element.72.refs_0_, bf16[256,1024]{1,0:T(8,128)(2,1)} %collective-permute-done.29.refs_1_, f32[8192,1024]{1,0:T(8,128)} %shard_map.70.refs_2_), custom_call_target="tpu_custom_call" | custom-call | bytes 2097152 | tf_op jit(solution)/shard_map/pallas_call | solution.py:69
  (85 shorter events, 22.0 us)
Async XLA Ops:
  0.6 17.4 %collective-permute-start = (bf16[32,8192]{1,0:T(8,128)(2,1)}, bf16[32,8192]{1,0:T(8,128)(2,1)}, u32[]{:S(2)}, u32[]{:S(2)}) collective-permute-start(bf16[32,8192]{1,0:T(8,128)(2,1)} %refs_0_.3), channel_id=1, source_target_pairs={{0,1},{1,0},{2,3},{3,2},{4,5},{5,4},{6,7},{7,6},{8,9},{9,8},{10,11... | collective-permute-start | bytes 1572872 | tf_op jit(solution)/shard_map/ppermute | solution.py:18
  14.9 1.9 %collective-permute-start.1 = (bf16[32,4096]{1,0:T(8,128)(2,1)}, bf16[32,4096]{1,0:T(8,128)(2,1)}, u32[]{:S(2)}, u32[]{:S(2)}) collective-permute-start(bf16[32,4096]{1,0:T(8,128)(2,1)} %get-tuple-element.40), channel_id=1, source_target_pairs={{0,2},{2,0},{4,6},{6,4},{8,10},{10,8},{12,14},{14,12},{16,18},{18,... | collective-permute-start | bytes 786440 | tf_op jit(solution)/shard_map/ppermute | solution.py:18
  15.0 2.2 %collective-permute-start.2 = (bf16[32,4096]{1,0:T(8,128)(2,1)}, bf16[32,4096]{1,0:T(8,128)(2,1)}, u32[]{:S(2)}, u32[]{:S(2)}) collective-permute-start(bf16[32,4096]{1,0:T(8,128)(2,1)} %get-tuple-element.41), channel_id=1, source_target_pairs={{0,2},{2,0},{4,6},{6,4},{8,10},{10,8},{12,14},{14,12},{16,18},{18,... | collective-permute-start | bytes 786440 | tf_op jit(solution)/shard_map/ppermute | solution.py:18
  15.5 2.1 %collective-permute-start.3 = (bf16[32,4096]{1,0:T(8,128)(2,1)}, bf16[32,4096]{1,0:T(8,128)(2,1)}, u32[]{:S(2)}, u32[]{:S(2)}) collective-permute-start(bf16[32,4096]{1,0:T(8,128)(2,1)} %get-tuple-element.43), channel_id=1, source_target_pairs={{0,2},{2,0},{4,6},{6,4},{8,10},{10,8},{12,14},{14,12},{16,18},{18,... | collective-permute-start | bytes 786440 | tf_op jit(solution)/shard_map/ppermute | solution.py:18
  15.6 2.4 %collective-permute-start.4 = (bf16[32,4096]{1,0:T(8,128)(2,1)}, bf16[32,4096]{1,0:T(8,128)(2,1)}, u32[]{:S(2)}, u32[]{:S(2)}) collective-permute-start(bf16[32,4096]{1,0:T(8,128)(2,1)} %get-tuple-element.44), channel_id=1, source_target_pairs={{0,2},{2,0},{4,6},{6,4},{8,10},{10,8},{12,14},{14,12},{16,18},{18,... | collective-permute-start | bytes 786440 | tf_op jit(solution)/shard_map/ppermute | solution.py:18
  22.2 26.5 %collective-permute-start.9 = (bf16[64,8192]{1,0:T(8,128)(2,1)}, bf16[64,8192]{1,0:T(8,128)(2,1)}, u32[]{:S(2)}, u32[]{:S(2)}) collective-permute-start(bf16[64,8192]{1,0:T(8,128)(2,1)} %get-tuple-element.53), channel_id=1, source_target_pairs={{0,4},{2,6},{4,0},{6,2},{8,12},{10,14},{12,8},{14,10},{16,20},{18,... | collective-permute-start | bytes 3145736 | tf_op jit(solution)/shard_map/ppermute | solution.py:18
  23.7 14.0 %collective-permute-start.7 = (bf16[256,1024]{1,0:T(8,128)(2,1)}, bf16[256,1024]{1,0:T(8,128)(2,1)}, u32[]{:S(2)}, u32[]{:S(2)}) collective-permute-start(bf16[256,1024]{1,0:T(8,128)(2,1)} %get-tuple-element.45.refs_8_.refs_12_.refs_10_), channel_id=1, source_target_pairs={{0,1},{1,0},{2,3},{3,2},{4,5},{5,4},{6,7},{7,6},{8,9},{9,8},{10,11... | collective-permute-start | bytes 1572872 | tf_op jit(solution)/shard_map/ppermute | solution.py:18
  24.2 24.3 %collective-permute-start.8 = (bf16[32,8192]{1,0:T(8,128)(2,1)}, bf16[32,8192]{1,0:T(8,128)(2,1)}, u32[]{:S(2)}, u32[]{:S(2)}) collective-permute-start(bf16[32,8192]{1,0:T(8,128)(2,1)} %get-tuple-element.52), channel_id=1, source_target_pairs={{0,2},{2,0},{4,6},{6,4},{8,10},{10,8},{12,14},{14,12},{16,18},{18,... | collective-permute-start | bytes 1572872 | tf_op jit(solution)/shard_map/ppermute | solution.py:18
  24.2 26.9 %collective-permute-start.6 = (bf16[32,8192]{1,0:T(8,128)(2,1)}, bf16[32,8192]{1,0:T(8,128)(2,1)}, u32[]{:S(2)}, u32[]{:S(2)}) collective-permute-start(bf16[32,8192]{1,0:T(8,128)(2,1)} %get-tuple-element.47), channel_id=1, source_target_pairs={{0,16},{2,18},{4,20},{6,22},{8,24},{10,26},{12,28},{14,30},{16,0},... | collective-permute-start | bytes 1572872 | tf_op jit(solution)/shard_map/ppermute | solution.py:18
  26.8 34.4 %collective-permute-start.5 = (bf16[32,8192]{1,0:T(8,128)(2,1)}, bf16[32,8192]{1,0:T(8,128)(2,1)}, u32[]{:S(2)}, u32[]{:S(2)}) collective-permute-start(bf16[32,8192]{1,0:T(8,128)(2,1)} %get-tuple-element.47), channel_id=1, source_target_pairs={{0,8},{2,10},{4,12},{6,14},{8,0},{10,2},{12,4},{14,6},{16,24},{18,... | collective-permute-start | bytes 1572872 | tf_op jit(solution)/shard_map/ppermute | solution.py:18
  37.7 17.0 %collective-permute-start.16 = (bf16[32,5120]{1,0:T(8,128)(2,1)}, bf16[32,5120]{1,0:T(8,128)(2,1)}, u32[]{:S(2)}, u32[]{:S(2)}) collective-permute-start(bf16[32,5120]{1,0:T(8,128)(2,1)} %get-tuple-element.50.refs_4_), channel_id=1, source_target_pairs={{0,4},{2,6},{4,0},{6,2},{8,12},{10,14},{12,8},{14,10},{16,20},{18,... | collective-permute-start | bytes 983048 | tf_op jit(solution)/shard_map/ppermute | solution.py:18
  48.6 6.1 %collective-permute-start.19 = (bf16[32,8192]{1,0:T(8,128)(2,1)}, bf16[32,8192]{1,0:T(8,128)(2,1)S(1)}, u32[]{:S(2)}, u32[]{:S(2)}) collective-permute-start(bf16[32,8192]{1,0:T(8,128)(2,1)} %get-tuple-element.64), channel_id=1, source_target_pairs={{0,2},{2,0},{4,6},{6,4},{8,10},{10,8},{12,14},{14,12},{16,18},{18,... | collective-permute-start | bytes 1572872 | tf_op jit(solution)/shard_map/ppermute | solution.py:18
  48.7 7.2 %collective-permute-start.20 = (bf16[32,8192]{1,0:T(8,128)(2,1)}, bf16[32,8192]{1,0:T(8,128)(2,1)S(1)}, u32[]{:S(2)}, u32[]{:S(2)}) collective-permute-start(bf16[32,8192]{1,0:T(8,128)(2,1)} %get-tuple-element.54.refs_9_), channel_id=1, source_target_pairs={{0,2},{2,0},{4,6},{6,4},{8,10},{10,8},{12,14},{14,12},{16,18},{18,... | collective-permute-start | bytes 1572872 | tf_op jit(solution)/shard_map/ppermute | solution.py:18
  52.2 24.9 %collective-permute-start.10 = (bf16[64,8192]{1,0:T(8,128)(2,1)S(1)}, bf16[64,8192]{1,0:T(8,128)(2,1)}, u32[]{:S(2)}, u32[]{:S(2)}) collective-permute-start(bf16[64,8192]{1,0:T(8,128)(2,1)S(1)} %pad_maximum_fusion.refs_4_), channel_id=1, source_target_pairs={{0,8},{2,10},{4,12},{6,14},{8,0},{10,2},{12,4},{14,6},{16,24},{18,... | collective-permute-start | bytes 3145736 | tf_op jit(solution)/shard_map/ppermute | solution.py:18
  58.2 24.7 %collective-permute-start.21 = (bf16[64,8192]{1,0:T(8,128)(2,1)}, bf16[64,8192]{1,0:T(8,128)(2,1)}, u32[]{:S(2)}, u32[]{:S(2)}) collective-permute-start(bf16[64,8192]{1,0:T(8,128)(2,1)} %pad_maximum_fusion.1), channel_id=1, source_target_pairs={{0,4},{2,6},{4,0},{6,2},{8,12},{10,14},{12,8},{14,10},{16,20},{18,... | collective-permute-start | bytes 3145736 | tf_op jit(solution)/shard_map/ppermute | solution.py:18
  59.7 25.5 %collective-permute-start.12 = (bf16[32,8192]{1,0:T(8,128)(2,1)S(1)}, bf16[32,8192]{1,0:T(8,128)(2,1)S(1)}, u32[]{:S(2)}, u32[]{:S(2)}) collective-permute-start(bf16[32,8192]{1,0:T(8,128)(2,1)S(1)} %copy-done.1), channel_id=1, source_target_pairs={{0,2},{2,0},{4,6},{6,4},{8,10},{10,8},{12,14},{14,12},{16,18},{18,... | collective-permute-start | bytes 1572872 | tf_op jit(solution)/shard_map/ppermute | solution.py:18
  59.7 20.6 %collective-permute-start.18 = (bf16[32,8192]{1,0:T(8,128)(2,1)}, bf16[32,8192]{1,0:T(8,128)(2,1)S(1)}, u32[]{:S(2)}, u32[]{:S(2)}) collective-permute-start(bf16[32,8192]{1,0:T(8,128)(2,1)} %get-tuple-element.62), channel_id=1, source_target_pairs={{0,2},{2,0},{4,6},{6,4},{8,10},{10,8},{12,14},{14,12},{16,18},{18,... | collective-permute-start | bytes 1572872 | tf_op jit(solution)/shard_map/ppermute | solution.py:18
  61.2 24.5 %collective-permute-start.14 = (bf16[32,8192]{1,0:T(8,128)(2,1)}, bf16[32,8192]{1,0:T(8,128)(2,1)S(1)}, u32[]{:S(2)}, u32[]{:S(2)}) collective-permute-start(bf16[32,8192]{1,0:T(8,128)(2,1)} %collective-permute-done.6.refs_2_), channel_id=1, source_target_pairs={{0,2},{2,0},{4,6},{6,4},{8,10},{10,8},{12,14},{14,12},{16,18},{18,... | collective-permute-start | bytes 1572872 | tf_op jit(solution)/shard_map/ppermute | solution.py:18
  77.1 8.7 %collective-permute-start.13 = (bf16[32,8192]{1,0:T(8,128)(2,1)}, bf16[32,8192]{1,0:T(8,128)(2,1)S(1)}, u32[]{:S(2)}, u32[]{:S(2)}) collective-permute-start(bf16[32,8192]{1,0:T(8,128)(2,1)} %collective-permute-done.5.refs_1_), channel_id=1, source_target_pairs={{0,2},{2,0},{4,6},{6,4},{8,10},{10,8},{12,14},{14,12},{16,18},{18,... | collective-permute-start | bytes 1572872 | tf_op jit(solution)/shard_map/ppermute | solution.py:18
  80.3 11.0 %copy-start = (bf16[32,8192]{1,0:T(8,128)(2,1)}, bf16[32,8192]{1,0:T(8,128)(2,1)S(1)}, u32[]{:S(2)}) copy-start(bf16[32,8192]{1,0:T(8,128)(2,1)S(1)} %slice.58.refs_3_) | copy-start | bytes 1572868
  80.3 24.5 %collective-permute-start.17 = (bf16[96,5120]{1,0:T(8,128)(2,1)}, bf16[96,5120]{1,0:T(8,128)(2,1)}, u32[]{:S(2)}, u32[]{:S(2)}) collective-permute-start(bf16[96,5120]{1,0:T(8,128)(2,1)} %pad_maximum_fusion.2.refs_2_.refs_10_), channel_id=1, source_target_pairs={{0,4},{2,6},{4,0},{6,2},{8,12},{10,14},{12,8},{14,10},{16,20},{18,... | collective-permute-start | bytes 2949128 | tf_op jit(solution)/shard_map/ppermute | solution.py:18
  82.9 8.4 %collective-permute-start.15 = (bf16[32,8192]{1,0:T(8,128)(2,1)S(1)}, bf16[32,8192]{1,0:T(8,128)(2,1)S(1)}, u32[]{:S(2)}, u32[]{:S(2)}) collective-permute-start(bf16[32,8192]{1,0:T(8,128)(2,1)S(1)} %slice.58.refs_3_), channel_id=1, source_target_pairs={{0,2},{2,0},{4,6},{6,4},{8,10},{10,8},{12,14},{14,12},{16,18},{18,... | collective-permute-start | bytes 1572872 | tf_op jit(solution)/shard_map/ppermute | solution.py:18
  85.2 21.2 %collective-permute-start.26 = (bf16[32,8192]{1,0:T(8,128)(2,1)}, bf16[32,8192]{1,0:T(8,128)(2,1)}, u32[]{:S(2)}, u32[]{:S(2)}) collective-permute-start(bf16[32,8192]{1,0:T(8,128)(2,1)} %get-tuple-element.69), channel_id=1, source_target_pairs={{0,2},{2,0},{4,6},{6,4},{8,10},{10,8},{12,14},{14,12},{16,18},{18,... | collective-permute-start | bytes 1572872 | tf_op jit(solution)/shard_map/ppermute | solution.py:18
  85.7 20.7 %collective-permute-start.24 = (bf16[32,8192]{1,0:T(8,128)(2,1)}, bf16[32,8192]{1,0:T(8,128)(2,1)}, u32[]{:S(2)}, u32[]{:S(2)}) collective-permute-start(bf16[32,8192]{1,0:T(8,128)(2,1)} %get-tuple-element.67), channel_id=1, source_target_pairs={{0,2},{2,0},{4,6},{6,4},{8,10},{10,8},{12,14},{14,12},{16,18},{18,... | collective-permute-start | bytes 1572872 | tf_op jit(solution)/shard_map/ppermute | solution.py:18
  85.8 20.6 %collective-permute-start.25 = (bf16[32,8192]{1,0:T(8,128)(2,1)}, bf16[32,8192]{1,0:T(8,128)(2,1)}, u32[]{:S(2)}, u32[]{:S(2)}) collective-permute-start(bf16[32,8192]{1,0:T(8,128)(2,1)} %add_convert_fusion.refs_11_), channel_id=1, source_target_pairs={{0,8},{2,10},{4,12},{6,14},{8,0},{10,2},{12,4},{14,6},{16,24},{18,... | collective-permute-start | bytes 1572872 | tf_op jit(solution)/shard_map/ppermute | solution.py:18
  92.1 20.4 %collective-permute-start.22 = (bf16[32,5120]{1,0:T(8,128)(2,1)}, bf16[32,5120]{1,0:T(8,128)(2,1)}, u32[]{:S(2)}, u32[]{:S(2)}) collective-permute-start(bf16[32,5120]{1,0:T(8,128)(2,1)} %collective-permute-done.16.refs_5_.refs_8_), channel_id=1, source_target_pairs={{0,2},{2,0},{4,6},{6,4},{8,10},{10,8},{12,14},{14,12},{16,18},{18,... | collective-permute-start | bytes 983048 | tf_op jit(solution)/shard_map/ppermute | solution.py:18
  104.9 25.4 %collective-permute-start.11 = (bf16[128,3072]{1,0:T(8,128)(2,1)}, bf16[128,3072]{1,0:T(8,128)(2,1)}, u32[]{:S(2)}, u32[]{:S(2)}) collective-permute-start(bf16[128,3072]{1,0:T(8,128)(2,1)} %pad_maximum_fusion.3), channel_id=1, source_target_pairs={{0,4},{2,6},{4,0},{6,2},{8,12},{10,14},{12,8},{14,10},{16,20},{18,... | collective-permute-start | bytes 2359304 | tf_op jit(solution)/shard_map/ppermute | solution.py:18
  106.4 6.2 %collective-permute-start.23 = (bf16[96,5120]{1,0:T(8,128)(2,1)}, bf16[96,5120]{1,0:T(8,128)(2,1)}, u32[]{:S(2)}, u32[]{:S(2)}) collective-permute-start(bf16[96,5120]{1,0:T(8,128)(2,1)} %shard_map.64.refs_9_), channel_id=1, source_target_pairs={{0,2},{2,0},{4,6},{6,4},{8,10},{10,8},{12,14},{14,12},{16,18},{18,... | collective-permute-start | bytes 2949128 | tf_op jit(solution)/shard_map/ppermute | solution.py:18
  110.0 26.8 %collective-permute-start.28 = (bf16[32,8192]{1,0:T(8,128)(2,1)}, bf16[32,8192]{1,0:T(8,128)(2,1)}, u32[]{:S(2)}, u32[]{:S(2)}) collective-permute-start(bf16[32,8192]{1,0:T(8,128)(2,1)} %get-tuple-element.77), channel_id=1, source_target_pairs={{0,16},{2,18},{4,20},{6,22},{8,24},{10,26},{12,28},{14,30},{16,0},... | collective-permute-start | bytes 1572872 | tf_op jit(solution)/shard_map/ppermute | solution.py:18
  130.2 9.3 %collective-permute-start.27 = (bf16[128,3072]{1,0:T(8,128)(2,1)}, bf16[128,3072]{1,0:T(8,128)(2,1)}, u32[]{:S(2)}, u32[]{:S(2)}) collective-permute-start(bf16[128,3072]{1,0:T(8,128)(2,1)} %shard_map.66.refs_0_.refs_8_), channel_id=1, source_target_pairs={{0,2},{2,0},{4,6},{6,4},{8,10},{10,8},{12,14},{14,12},{16,18},{18,... | collective-permute-start | bytes 2359304 | tf_op jit(solution)/shard_map/ppermute | solution.py:18
  139.0 16.0 %collective-permute-start.30 = (bf16[32,8192]{1,0:T(8,128)(2,1)}, bf16[32,8192]{1,0:T(8,128)(2,1)}, u32[]{:S(2)}, u32[]{:S(2)}) collective-permute-start(bf16[32,8192]{1,0:T(8,128)(2,1)} %get-tuple-element.75), channel_id=1, source_target_pairs={{0,1},{1,0},{2,3},{3,2},{4,5},{5,4},{6,7},{7,6},{8,9},{9,8},{10,11... | collective-permute-start | bytes 1572872 | tf_op jit(solution)/shard_map/ppermute | solution.py:18
  146.8 17.4 %collective-permute-start.29 = (bf16[256,1024]{1,0:T(8,128)(2,1)}, bf16[256,1024]{1,0:T(8,128)(2,1)}, u32[]{:S(2)}, u32[]{:S(2)}) collective-permute-start(bf16[256,1024]{1,0:T(8,128)(2,1)} %get-tuple-element.73.refs_13_), channel_id=1, source_target_pairs={{0,1},{1,0},{2,3},{3,2},{4,5},{5,4},{6,7},{7,6},{8,9},{9,8},{10,11... | collective-permute-start | bytes 1572872 | tf_op jit(solution)/shard_map/ppermute | solution.py:18
  (10 other events, 48.0 us)

commit v4 on v3

--- a/solution.py
+++ b/solution.py
@@ -397,27 +397,25 @@
     )
 
 
-def finish(chain, shares, rows, low_bits):
+def finish(chain, parts, rows, low_bits):
+    each = len(parts[0])
     rest = 1 << (low_bits - 2)
 
     def body(place, *refs):
         *shares, out = refs
         for position in range(1 << low_bits):
             side, middle = position // (2 * rest), position // rest % 2
-            start = ((middle * 2 + side) * rest + position % rest) * rows
+            start = (side * rest + position % rest) * rows
             here = slice(start, start + rows)
-            total = shares[0][here, :]
-            for other in shares[1:]:
+            total = shares[middle * each][here, :]
+            for other in shares[middle * each + 1 : (middle + 1) * each]:
                 total = total + other[here, :].astype(F32)
             target = place[0] ^ reversed_bits(position, low_bits)
             out[pl.ds(pl.multiple_of(target * rows, rows), rows), :] = total.astype(BF16)
 
-    tokens, columns = shares[0].shape
-    tile = columns
-    block = across(tokens, tile)
-    (out,) = chain(
-        body, shares, [block] * len(shares), [array(tokens, columns)], [block], columns // tile
-    )
+    flat = [v for part in parts for v in part]
+    shape = (rows << low_bits, flat[0].shape[1])
+    (out,) = chain(body, flat, [whole(v.shape) for v in flat], [array(*shape)], [whole(shape)])
     return out
 
 
@@ -524,8 +522,8 @@
         others = [part for part, _, _ in sent_parts]
         messages = [message for _, _, message in sent_parts]
     chain.follow(across_sent[0], *messages)
-    start, size = ranges[1]
-    (total,) = product(chain, [here, core], [], weight, start, size, inner, out=2)
+    total, *early = product(chain, [here, core], [], weight, 0, width, inner, out=2, last=True)
+    early = [total] + [swap(early[q - 1], "tensor", q) for q in range(1, tensor)]
     grads = [ordered] + far
     arrived = list(chain.gate([near(across_sent[0], 1)], [total]))
 
@@ -544,17 +542,17 @@
     start, size = ranges[0]
     weight_grad, total, kept = product(
         chain, [here, core, [leading, arrived[0]], [leading_core, arrived_core[0]]], grads, weight, start, size, inner,
-        before=total, grad=True, out=4, late=[kept],
+        grad=True, out=2, late=[kept],
     )
     (arrived[1],) = chain.gate(arrived[1:], [total])
     arrived_core.append(near(arrived[1], 0))
     rotated_grad = add(kept, came)
     final = exchange_last(rotated_grad)
-    chain.follow(rotated_grad)
+    chain.follow(rotated_grad, *early[1:])
     start, size = ranges[1]
     result = product(
         chain, [[arrived[1]], [arrived_core[1]]], grads, weight, start, size, inner,
-        before=total, out=4, last=True,
+        before=total, out=2, last=True,
     )
     shares = [result[0]] + [swap(result[q], "tensor", q) for q in range(1, tensor)]
     held = [here, core, [arrived[1]], [arrived_core[1]]]
@@ -567,7 +565,7 @@
         chain, held, grads, weight, start + part, size - part, inner, into=weight_grad, grad=True,
         origin=start,
     )
-    outputs = finish(chain, shares, rows, low_bits)
+    outputs = finish(chain, [early, shares], rows, low_bits)
     return (outputs, in_grad, weight_grad)
 
 

time: 167 us -> 166 us (level)
  waiting for transfers between devices: 42.5 us -> 34.9 us
  Pallas kernels: 73.2 us -> 78.9 us
    ppermute x31 -> x32, waiting for transfers between devices: 42.5 us -> 34.9 us  [swap(): lax.ppermute(values, axis, [(i, i ^ mask) for i in range(lax.axis_size(ax...]
    pallas_call x10, Pallas kernels: 73.2 us -> 78.9 us  [__call__(): pl.pallas_call(kernel, grid=(steps,), in_specs=[pl.BlockSpec(memory_space...]
    ppermute x31 -> x32, starting transfers between devices: 25 us -> 25.6 us  [swap(): lax.ppermute(values, axis, [(i, i ^ mask) for i in range(lax.axis_size(ax...]
  transfers between devices with their start and end apart: 31 -> 32, of which waited for: 12 -> 11; matrix products, arithmetic and copies ran while one was open for 14% -> 14% of each run, Pallas kernels for 40% -> 44%
where the time goes in v4:
time: 166 us; the launch traced here: 165 us
  Pallas kernels  78.9 us (48%)
  waiting for transfers between devices  34.9 us (21%)
  starting transfers between devices  25.6 us (15%)
  other arithmetic  16.9 us (10%)
  local copies, waits for them, and re-layouts  7.74 us (5%)
    pallas_call x10, Pallas kernels, __call__(): pl.pallas_call(kernel, grid=(steps,), in_specs=[pl.BlockSpec(memory_space...  78.9 us
    ppermute x32, waiting for transfers between devices, swap(): lax.ppermute(values, axis, [(i, i ^ mask) for i in range(lax.axis_size(ax...  34.9 us
    ppermute x32, starting transfers between devices, swap(): lax.ppermute(values, axis, [(i, i ^ mask) for i in range(lax.axis_size(ax...  25.6 us
    convert_element_type x4, other arithmetic, split_send(): add(*t).astype(BF16)  6.27 us
    slice x7, local copies, waits for them, and re-layouts, per_device(): block[:, start:start + size]  5.82 us
    convert_element_type x1, other arithmetic, per_device(): some[j + count].astype(BF16)  3.54 us
  transfers between devices with their start and end apart: 32, of which 11 were waited for; matrix products, arithmetic and copies ran while one was open for 14% of the time, Pallas kernels for 44%

profile of v4, /device:TPU:0, one launch (start us, length us, event | category | flops | bytes accessed | tf_op | source)
XLA Modules:
  0.0 164.9 jit_solution(8843935562113749801)
XLA Ops:
  0.6 3.0 %collective-permute-start = (bf16[32,8192]{1,0:T(8,128)(2,1)}, bf16[32,8192]{1,0:T(8,128)(2,1)}, u32[]{:S(2)}, u32[]{:S(2)}) collective-permute-start(bf16[32,8192]{1,0:T(8,128)(2,1)} %refs_0_.3), channel_id=1, source_target_pairs={{0,1},{1,0},{2,3},{3,2},{4,5},{5,4},{6,7},{7,6},{8,9},{9,8},{10,11... | collective-permute-start | bytes 1572872 | tf_op jit(solution)/shard_map/ppermute | solution.py:18
  4.3 10.7 %shard_map.58 = (bf16[32,8192]{1,0:T(8,128)(2,1)}, bf16[32,8192]{1,0:T(8,128)(2,1)}, bf16[32,8192]{1,0:T(8,128)(2,1)}, bf16[32,8192]{1,0:T(8,128)(2,1)}, bf16[32...) custom-call(s32[3]{0:T(128)} %pad_add_fusion.place, ...), custom_call_target="tpu_custom_call" | custom-call | flops 4294967296 | bytes 22020096 | tf_op jit(solution)/shard_map/pallas_call | solution.py:69
  18.0 4.2 %shard_map.59 = (bf16[32,8192]{1,0:T(8,128)(2,1)}, bf16[32,8192]{1,0:T(8,128)(2,1)}, bf16[64,8192]{1,0:T(8,128)(2,1)}, bf16[32,5120]{1,0:T(8,128)(2,1)}) custom-call(s32[3]{0:T(128)} %pad_add_fusion.place, bf16[32,8192]{1,0:T(8,128)(2,1)} %refs_0_.3, bf16[32,8192]{1,0:T(8,128)(2,1)} %collective-permute-done.refs_1_, ...), custom_call_target="tpu_custom_call" | custom-call | flops 201326592 | bytes 5570560 | tf_op jit(solution)/shard_map/pallas_call | solution.py:69
  22.2 1.5 collective-permute-start.9
  24.3 2.6 %collective-permute-start.6 = (bf16[32,8192]{1,0:T(8,128)(2,1)}, bf16[32,8192]{1,0:T(8,128)(2,1)}, u32[]{:S(2)}, u32[]{:S(2)}) collective-permute-start(bf16[32,8192]{1,0:T(8,128)(2,1)} %get-tuple-element.49), channel_id=1, source_target_pairs={{0,16},{2,18},{4,20},{6,22},{8,24},{10,26},{12,28},{14,30},{16,0},... | collective-permute-start | bytes 1572872 | tf_op jit(solution)/shard_map/ppermute | solution.py:18
  26.8 1.6 collective-permute-start.5
  28.4 9.3 %collective-permute-done.7.refs_0_.refs_13_.refs_11_ = bf16[256,1024]{1,0:T(8,128)(2,1)} collective-permute-done((bf16[256,1024]{1,0:T(8,128)(2,1)}, bf16[256,1024]{1,0:T(8,128)(2,1)}, u32[]{:S(2)}, u32[]{:S(2)}) %collective-permute-start.7) | collective-permute-done | bytes 524320 | tf_op jit(solution)/shard_map/ppermute | solution.py:18
  38.2 10.3 %shard_map.60 = (bf16[32,8192]{1,0:T(8,128)(2,1)}, bf16[32,8192]{1,0:T(8,128)(2,1)}, bf16[32,8192]{1,0:T(8,128)(2,1)}, bf16[32,8192]{1,0:T(8,128)(2,1)}, bf16[32...) custom-call(s32[3]{0:T(128)} %pad_add_fusion.place, ...), custom_call_target="tpu_custom_call", output_to_operand_aliasing={{8}: (3, {}), {9}: (4, {})} | custom-call | flops 4294967296 | bytes 21495808 | tf_op jit(solution)/shard_map/pallas_call | solution.py:69
  49.1 1.5 add_convert_fusion.3
  52.3 1.1 collective-permute-start.10
  53.4 1.3 collective-permute-done.15.refs_5_.refs_8_
  54.7 1.2 add_convert_fusion.2
  55.9 1.2 add_convert_fusion.1
  58.2 1.5 collective-permute-start.19
  64.3 12.8 %collective-permute-done.10 = bf16[64,8192]{1,0:T(8,128)(2,1)} collective-permute-done((bf16[64,8192]{1,0:T(8,128)(2,1)S(1)}, bf16[64,8192]{1,0:T(8,128)(2,1)}, u32[]{:S(2)}, u32[]{:S(2)}) %collective-permute-start.10) | collective-permute-done | bytes 1048608 | tf_op jit(solution)/shard_map/ppermute | solution.py:18
  80.3 1.5 collective-permute-start.22
  82.9 2.3 %add_convert_fusion.refs_11_ = bf16[32,8192]{1,0:T(8,128)(2,1)} fusion(bf16[32,8192]{1,0:T(8,128)(2,1)} %collective-permute-done.16, bf16[32,8192]{1,0:T(8,128)(2,1)} %get-tuple-element.63, bf16[64,8192]{1,0:T(8,128)(2,1)} %collective-permute-done.19), kind=kLoop, calls=%fused_computation.6 | loop fusion | flops 1572864 | bytes 2097152 | tf_op jit(solution)/shard_map/convert_element_type | solution.py:448
  86.9 1.6 collective-permute-start.26
  90.4 12.6 %shard_map.63 = (f32[128,1024]{1,0:T(8,128)}, bf16[128,1024]{1,0:T(8,128)(2,1)}) custom-call(s32[3]{0:T(128)} %pad_add_fusion.place, bf16[32,8192]{1,0:T(8,128)(2,1)} %get-tuple-element.48.refs_0_, bf16[32,8192]{1,0:T(8,128)(2,1)} %collective-permute-done.5.refs_1_, bf16[32,8192]{1,0:T(8,128)(2,1)} %collective-permute-done.6.refs_2_, ...), custom_call_target="tpu_custom_call" | custom-call | flops 4294967296 | bytes 21757952 | tf_op jit(solution)/shard_map/pallas_call | solution.py:69
  103.0 1.8 %collective-permute-done.22.refs_0_ = bf16[96,5120]{1,0:T(8,128)(2,1)} collective-permute-done((bf16[96,5120]{1,0:T(8,128)(2,1)}, bf16[96,5120]{1,0:T(8,128)(2,1)}, u32[]{:S(2)}, u32[]{:S(2)}) %collective-permute-start.22) | collective-permute-done | bytes 983072 | tf_op jit(solution)/shard_map/ppermute | solution.py:18
  104.9 1.4 collective-permute-start.21
  106.9 3.5 %select_convert_fusion = (bf16[32,8192]{1,0:T(8,128)(2,1)}, f32[32,8192]{1,0:T(8,128)}) fusion(pred[]{:T(512)S(6)} %eq.3, bf16[32,8192]{1,0:T(8,128)(2,1)} %collective-permute-done.26, bf16[64,8192]{1,0:T(8,128)(2,1)} %collective-permute-done.19, bf16[32,8192]{1,0:T(8,128)(2,1)} %collective-permute-done.25, bf16[32,8192]{1,0:T(8,128)(2,1)S(1)} %copy-done.6, ...), kind=kLoop, calls=%fused_computation.3 | loop fusion | flops 4456448 | bytes 5767169 | tf_op jit(solution)/shard_map/convert_element_type | solution.py:534
  110.4 2.6 %collective-permute-start.29 = (bf16[32,8192]{1,0:T(8,128)(2,1)}, bf16[32,8192]{1,0:T(8,128)(2,1)}, u32[]{:S(2)}, u32[]{:S(2)}) collective-permute-start(bf16[32,8192]{1,0:T(8,128)(2,1)} %get-tuple-element.81), channel_id=1, source_target_pairs={{0,16},{2,18},{4,20},{6,22},{8,24},{10,26},{12,28},{14,30},{16,0},... | collective-permute-start | bytes 1572872 | tf_op jit(solution)/shard_map/ppermute | solution.py:18
  113.1 17.8 %shard_map.65 = (f32[8192,1024]{1,0:T(8,128)}, f32[256,1024]{1,0:T(8,128)}, f32[32,8192]{1,0:T(8,128)}) custom-call(s32[3]{0:T(128)} %pad_add_fusion.place, bf16[32,8192]{1,0:T(8,128)(2,1)} %get-tuple-element.48.refs_0_, bf16[32,8192]{1,0:T(8,128)(2,1)} %collective-permute-done.5.refs_1_, ...), custom_call_target="tpu_custom_call", output_to_operand_aliasing={{2}: (16, {})} | custom-call | flops 8053063680 | bytes 59244544 | tf_op jit(solution)/shard_map/pallas_call | solution.py:69
  131.2 6.0 %collective-permute-done.29 = bf16[32,8192]{1,0:T(8,128)(2,1)} collective-permute-done((bf16[32,8192]{1,0:T(8,128)(2,1)}, bf16[32,8192]{1,0:T(8,128)(2,1)}, u32[]{:S(2)}, u32[]{:S(2)}) %collective-permute-start.29) | collective-permute-done | bytes 524320 | tf_op jit(solution)/shard_map/ppermute | solution.py:18
  137.2 2.3 %fusion = (bf16[32,8192]{1,0:T(8,128)(2,1)}, f32[32,8192]{1,0:T(8,128)}) fusion(f32[32,8192]{1,0:T(8,128)S(1)} %copy-done.8, bf16[32,8192]{1,0:T(8,128)(2,1)} %collective-permute-done.29), kind=kLoop, calls=%fused_computation.14 | loop fusion | flops 786432 | bytes 3145728 | tf_op jit(solution)/shard_map/convert_element_type | solution.py:187
  139.5 1.5 collective-permute-start.31
  141.0 6.4 %shard_map.67 = (f32[128,1024]{1,0:T(8,128)}, bf16[128,1024]{1,0:T(8,128)(2,1)}) custom-call(s32[3]{0:T(128)} %pad_add_fusion.place, bf16[128,3072]{1,0:T(8,128)(2,1)} %shard_map.66.refs_0_.refs_8_, bf16[128,3072]{1,0:T(8,128)(2,1)} %collective-permute-done.28.refs_1_.refs_9_, bf16[8192,1024]{1,0:T(8,128)(2,1)} %refs_2_.1, ...), custom_call_target="tpu_custom_call" | custom-call | flops 1610612736 | bytes 20185088 | tf_op jit(solution)/shard_map/pallas_call | solution.py:69
  148.0 6.8 %shard_map.68.refs_2_.refs_12_ = f32[8192,1024]{1,0:T(8,128)} custom-call(s32[3]{0:T(128)} %pad_add_fusion.place, bf16[32,8192]{1,0:T(8,128)(2,1)} %get-tuple-element.48.refs_0_, bf16[32,8192]{1,0:T(8,128)(2,1)} %collective-permute-done.5.refs_1_, bf16[32,8192]{1,0:T(8,128)(2,1)} %collective-permute-done.6.refs_2_, ...), custom_call_target="tpu_custom_call", output_to_operand_aliasing={{}: (13, {})} | custom-call | flops 2147483648 | bytes 73924608 | tf_op jit(solution)/shard_map/pallas_call | solution.py:69
  154.8 3.0 %shard_map.69.refs_13_ = bf16[32,8192]{1,0:T(8,128)(2,1)} custom-call(s32[3]{0:T(128)} %pad_add_fusion.place, f32[32,8192]{1,0:T(8,128)} %get-tuple-element.80.refs_5_.refs_0_, bf16[32,8192]{1,0:T(8,128)(2,1)} %collective-permute-done.31.refs_1_, f32[8192,1024]{1,0:T(8,128)} %shard_map.68.refs_2_.refs_12_), custom_call_target="tpu_custom_call" | custom-call | flops 201326592 | bytes 2097152 | tf_op jit(solution)/shard_map/pallas_call | solution.py:69
  157.7 4.9 %shard_map.70.refs_4_ = f32[8192,1024]{1,0:T(8,128)} custom-call(s32[3]{0:T(128)} %pad_add_fusion.place, bf16[32,8192]{1,0:T(8,128)(2,1)} %get-tuple-element.48.refs_0_, bf16[32,8192]{1,0:T(8,128)(2,1)} %collective-permute-done.5.refs_1_, bf16[32,8192]{1,0:T(8,128)(2,1)} %collective-permute-done.6.refs_2_, ...), custom_call_target="tpu_custom_call", output_to_operand_aliasing={{}: (13, {})} | custom-call | flops 1073741824 | bytes 73924608 | tf_op jit(solution)/shard_map/pallas_call | solution.py:69
  162.7 2.2 %shard_map.71 = bf16[256,1024]{1,0:T(8,128)(2,1)} custom-call(s32[3]{0:T(128)} %pad_add_fusion.place, f32[128,1024]{1,0:T(8,128)} %get-tuple-element.68.refs_1_.refs_0_, bf16[128,1024]{1,0:T(8,128)(2,1)} %collective-permute-done.20.refs_6_.refs_1_, f32[128,1024]{1,0:T(8,128)} %get-tuple-element.76.refs_2_, ...), custom_call_target="tpu_custom_call" | custom-call | bytes 2097152 | tf_op jit(solution)/shard_map/pallas_call | solution.py:69
  (85 shorter events, 21.7 us)
Async XLA Ops:
  0.6 17.4 %collective-permute-start = (bf16[32,8192]{1,0:T(8,128)(2,1)}, bf16[32,8192]{1,0:T(8,128)(2,1)}, u32[]{:S(2)}, u32[]{:S(2)}) collective-permute-start(bf16[32,8192]{1,0:T(8,128)(2,1)} %refs_0_.3), channel_id=1, source_target_pairs={{0,1},{1,0},{2,3},{3,2},{4,5},{5,4},{6,7},{7,6},{8,9},{9,8},{10,11... | collective-permute-start | bytes 1572872 | tf_op jit(solution)/shard_map/ppermute | solution.py:18
  15.0 1.9 %collective-permute-start.1 = (bf16[32,4096]{1,0:T(8,128)(2,1)}, bf16[32,4096]{1,0:T(8,128)(2,1)}, u32[]{:S(2)}, u32[]{:S(2)}) collective-permute-start(bf16[32,4096]{1,0:T(8,128)(2,1)} %get-tuple-element.42), channel_id=1, source_target_pairs={{0,2},{2,0},{4,6},{6,4},{8,10},{10,8},{12,14},{14,12},{16,18},{18,... | collective-permute-start | bytes 786440 | tf_op jit(solution)/shard_map/ppermute | solution.py:18
  15.0 2.2 %collective-permute-start.2 = (bf16[32,4096]{1,0:T(8,128)(2,1)}, bf16[32,4096]{1,0:T(8,128)(2,1)}, u32[]{:S(2)}, u32[]{:S(2)}) collective-permute-start(bf16[32,4096]{1,0:T(8,128)(2,1)} %get-tuple-element.43), channel_id=1, source_target_pairs={{0,2},{2,0},{4,6},{6,4},{8,10},{10,8},{12,14},{14,12},{16,18},{18,... | collective-permute-start | bytes 786440 | tf_op jit(solution)/shard_map/ppermute | solution.py:18
  15.5 2.1 %collective-permute-start.3 = (bf16[32,4096]{1,0:T(8,128)(2,1)}, bf16[32,4096]{1,0:T(8,128)(2,1)}, u32[]{:S(2)}, u32[]{:S(2)}) collective-permute-start(bf16[32,4096]{1,0:T(8,128)(2,1)} %get-tuple-element.45), channel_id=1, source_target_pairs={{0,2},{2,0},{4,6},{6,4},{8,10},{10,8},{12,14},{14,12},{16,18},{18,... | collective-permute-start | bytes 786440 | tf_op jit(solution)/shard_map/ppermute | solution.py:18
  15.6 2.4 %collective-permute-start.4 = (bf16[32,4096]{1,0:T(8,128)(2,1)}, bf16[32,4096]{1,0:T(8,128)(2,1)}, u32[]{:S(2)}, u32[]{:S(2)}) collective-permute-start(bf16[32,4096]{1,0:T(8,128)(2,1)} %get-tuple-element.46), channel_id=1, source_target_pairs={{0,2},{2,0},{4,6},{6,4},{8,10},{10,8},{12,14},{14,12},{16,18},{18,... | collective-permute-start | bytes 786440 | tf_op jit(solution)/shard_map/ppermute | solution.py:18
  22.2 26.4 %collective-permute-start.9 = (bf16[64,8192]{1,0:T(8,128)(2,1)}, bf16[64,8192]{1,0:T(8,128)(2,1)}, u32[]{:S(2)}, u32[]{:S(2)}) collective-permute-start(bf16[64,8192]{1,0:T(8,128)(2,1)} %get-tuple-element.55), channel_id=1, source_target_pairs={{0,4},{2,6},{4,0},{6,2},{8,12},{10,14},{12,8},{14,10},{16,20},{18,... | collective-permute-start | bytes 3145736 | tf_op jit(solution)/shard_map/ppermute | solution.py:18
  23.7 14.0 %collective-permute-start.7 = (bf16[256,1024]{1,0:T(8,128)(2,1)}, bf16[256,1024]{1,0:T(8,128)(2,1)}, u32[]{:S(2)}, u32[]{:S(2)}) collective-permute-start(bf16[256,1024]{1,0:T(8,128)(2,1)} %get-tuple-element.47.refs_8_.refs_12_.refs_10_), channel_id=1, source_target_pairs={{0,1},{1,0},{2,3},{3,2},{4,5},{5,4},{6,7},{7,6},{8,9},{9,8},{10,11... | collective-permute-start | bytes 1572872 | tf_op jit(solution)/shard_map/ppermute | solution.py:18
  24.3 24.3 %collective-permute-start.8 = (bf16[32,8192]{1,0:T(8,128)(2,1)}, bf16[32,8192]{1,0:T(8,128)(2,1)}, u32[]{:S(2)}, u32[]{:S(2)}) collective-permute-start(bf16[32,8192]{1,0:T(8,128)(2,1)} %get-tuple-element.54), channel_id=1, source_target_pairs={{0,2},{2,0},{4,6},{6,4},{8,10},{10,8},{12,14},{14,12},{16,18},{18,... | collective-permute-start | bytes 1572872 | tf_op jit(solution)/shard_map/ppermute | solution.py:18
  24.3 26.9 %collective-permute-start.6 = (bf16[32,8192]{1,0:T(8,128)(2,1)}, bf16[32,8192]{1,0:T(8,128)(2,1)}, u32[]{:S(2)}, u32[]{:S(2)}) collective-permute-start(bf16[32,8192]{1,0:T(8,128)(2,1)} %get-tuple-element.49), channel_id=1, source_target_pairs={{0,16},{2,18},{4,20},{6,22},{8,24},{10,26},{12,28},{14,30},{16,0},... | collective-permute-start | bytes 1572872 | tf_op jit(solution)/shard_map/ppermute | solution.py:18
  26.8 35.4 %collective-permute-start.5 = (bf16[32,8192]{1,0:T(8,128)(2,1)}, bf16[32,8192]{1,0:T(8,128)(2,1)}, u32[]{:S(2)}, u32[]{:S(2)}) collective-permute-start(bf16[32,8192]{1,0:T(8,128)(2,1)} %get-tuple-element.49), channel_id=1, source_target_pairs={{0,8},{2,10},{4,12},{6,14},{8,0},{10,2},{12,4},{14,6},{16,24},{18,... | collective-permute-start | bytes 1572872 | tf_op jit(solution)/shard_map/ppermute | solution.py:18
  37.7 17.0 %collective-permute-start.15 = (bf16[32,5120]{1,0:T(8,128)(2,1)}, bf16[32,5120]{1,0:T(8,128)(2,1)}, u32[]{:S(2)}, u32[]{:S(2)}) collective-permute-start(bf16[32,5120]{1,0:T(8,128)(2,1)} %get-tuple-element.52.refs_4_), channel_id=1, source_target_pairs={{0,4},{2,6},{4,0},{6,2},{8,12},{10,14},{12,8},{14,10},{16,20},{18,... | collective-permute-start | bytes 983048 | tf_op jit(solution)/shard_map/ppermute | solution.py:18
  48.5 6.2 %collective-permute-start.17 = (bf16[32,8192]{1,0:T(8,128)(2,1)}, bf16[32,8192]{1,0:T(8,128)(2,1)S(1)}, u32[]{:S(2)}, u32[]{:S(2)}) collective-permute-start(bf16[32,8192]{1,0:T(8,128)(2,1)} %get-tuple-element.66), channel_id=1, source_target_pairs={{0,2},{2,0},{4,6},{6,4},{8,10},{10,8},{12,14},{14,12},{16,18},{18,... | collective-permute-start | bytes 1572872 | tf_op jit(solution)/shard_map/ppermute | solution.py:18
  48.6 7.3 %collective-permute-start.18 = (bf16[32,8192]{1,0:T(8,128)(2,1)}, bf16[32,8192]{1,0:T(8,128)(2,1)S(1)}, u32[]{:S(2)}, u32[]{:S(2)}) collective-permute-start(bf16[32,8192]{1,0:T(8,128)(2,1)} %get-tuple-element.56.refs_9_), channel_id=1, source_target_pairs={{0,2},{2,0},{4,6},{6,4},{8,10},{10,8},{12,14},{14,12},{16,18},{18,... | collective-permute-start | bytes 1572872 | tf_op jit(solution)/shard_map/ppermute | solution.py:18
  52.3 24.9 %collective-permute-start.10 = (bf16[64,8192]{1,0:T(8,128)(2,1)S(1)}, bf16[64,8192]{1,0:T(8,128)(2,1)}, u32[]{:S(2)}, u32[]{:S(2)}) collective-permute-start(bf16[64,8192]{1,0:T(8,128)(2,1)S(1)} %pad_maximum_fusion.refs_4_), channel_id=1, source_target_pairs={{0,8},{2,10},{4,12},{6,14},{8,0},{10,2},{12,4},{14,6},{16,24},{18,... | collective-permute-start | bytes 3145736 | tf_op jit(solution)/shard_map/ppermute | solution.py:18
  58.2 24.7 %collective-permute-start.19 = (bf16[64,8192]{1,0:T(8,128)(2,1)}, bf16[64,8192]{1,0:T(8,128)(2,1)}, u32[]{:S(2)}, u32[]{:S(2)}) collective-permute-start(bf16[64,8192]{1,0:T(8,128)(2,1)} %pad_maximum_fusion.1), channel_id=1, source_target_pairs={{0,4},{2,6},{4,0},{6,2},{8,12},{10,14},{12,8},{14,10},{16,20},{18,... | collective-permute-start | bytes 3145736 | tf_op jit(solution)/shard_map/ppermute | solution.py:18
  59.7 26.4 %collective-permute-start.11 = (bf16[32,8192]{1,0:T(8,128)(2,1)S(1)}, bf16[32,8192]{1,0:T(8,128)(2,1)S(1)}, u32[]{:S(2)}, u32[]{:S(2)}) collective-permute-start(bf16[32,8192]{1,0:T(8,128)(2,1)S(1)} %copy-done.1), channel_id=1, source_target_pairs={{0,2},{2,0},{4,6},{6,4},{8,10},{10,8},{12,14},{14,12},{16,18},{18,... | collective-permute-start | bytes 1572872 | tf_op jit(solution)/shard_map/ppermute | solution.py:18
  59.8 20.5 %collective-permute-start.16 = (bf16[32,8192]{1,0:T(8,128)(2,1)}, bf16[32,8192]{1,0:T(8,128)(2,1)}, u32[]{:S(2)}, u32[]{:S(2)}) collective-permute-start(bf16[32,8192]{1,0:T(8,128)(2,1)} %get-tuple-element.64), channel_id=1, source_target_pairs={{0,2},{2,0},{4,6},{6,4},{8,10},{10,8},{12,14},{14,12},{16,18},{18,... | collective-permute-start | bytes 1572872 | tf_op jit(solution)/shard_map/ppermute | solution.py:18
  62.3 24.5 %collective-permute-start.13 = (bf16[32,8192]{1,0:T(8,128)(2,1)}, bf16[32,8192]{1,0:T(8,128)(2,1)S(1)}, u32[]{:S(2)}, u32[]{:S(2)}) collective-permute-start(bf16[32,8192]{1,0:T(8,128)(2,1)} %collective-permute-done.6.refs_2_), channel_id=1, source_target_pairs={{0,2},{2,0},{4,6},{6,4},{8,10},{10,8},{12,14},{14,12},{16,18},{18,... | collective-permute-start | bytes 1572872 | tf_op jit(solution)/shard_map/ppermute | solution.py:18
  77.2 9.7 %collective-permute-start.12 = (bf16[32,8192]{1,0:T(8,128)(2,1)}, bf16[32,8192]{1,0:T(8,128)(2,1)S(1)}, u32[]{:S(2)}, u32[]{:S(2)}) collective-permute-start(bf16[32,8192]{1,0:T(8,128)(2,1)} %collective-permute-done.5.refs_1_), channel_id=1, source_target_pairs={{0,2},{2,0},{4,6},{6,4},{8,10},{10,8},{12,14},{14,12},{16,18},{18,... | collective-permute-start | bytes 1572872 | tf_op jit(solution)/shard_map/ppermute | solution.py:18
  80.3 24.5 %collective-permute-start.22 = (bf16[96,5120]{1,0:T(8,128)(2,1)}, bf16[96,5120]{1,0:T(8,128)(2,1)}, u32[]{:S(2)}, u32[]{:S(2)}) collective-permute-start(bf16[96,5120]{1,0:T(8,128)(2,1)} %pad_maximum_fusion.2.refs_2_.refs_10_), channel_id=1, source_target_pairs={{0,4},{2,6},{4,0},{6,2},{8,12},{10,14},{12,8},{14,10},{16,20},{18,... | collective-permute-start | bytes 2949128 | tf_op jit(solution)/shard_map/ppermute | solution.py:18
  82.9 6.5 %collective-permute-start.14 = (bf16[32,8192]{1,0:T(8,128)(2,1)S(1)}, bf16[32,8192]{1,0:T(8,128)(2,1)S(1)}, u32[]{:S(2)}, u32[]{:S(2)}) collective-permute-start(bf16[32,8192]{1,0:T(8,128)(2,1)S(1)} %slice.55.refs_3_), channel_id=1, source_target_pairs={{0,2},{2,0},{4,6},{6,4},{8,10},{10,8},{12,14},{14,12},{16,18},{18,... | collective-permute-start | bytes 1572872 | tf_op jit(solution)/shard_map/ppermute | solution.py:18
  86.2 20.1 %collective-permute-start.27 = (bf16[32,8192]{1,0:T(8,128)(2,1)}, bf16[32,8192]{1,0:T(8,128)(2,1)}, u32[]{:S(2)}, u32[]{:S(2)}) collective-permute-start(bf16[32,8192]{1,0:T(8,128)(2,1)} %get-tuple-element.73), channel_id=1, source_target_pairs={{0,2},{2,0},{4,6},{6,4},{8,10},{10,8},{12,14},{14,12},{16,18},{18,... | collective-permute-start | bytes 1572872 | tf_op jit(solution)/shard_map/ppermute | solution.py:18
  86.8 20.1 %collective-permute-start.25 = (bf16[32,8192]{1,0:T(8,128)(2,1)}, bf16[32,8192]{1,0:T(8,128)(2,1)}, u32[]{:S(2)}, u32[]{:S(2)}) collective-permute-start(bf16[32,8192]{1,0:T(8,128)(2,1)} %get-tuple-element.71), channel_id=1, source_target_pairs={{0,2},{2,0},{4,6},{6,4},{8,10},{10,8},{12,14},{14,12},{16,18},{18,... | collective-permute-start | bytes 1572872 | tf_op jit(solution)/shard_map/ppermute | solution.py:18
  86.9 20.0 %collective-permute-start.26 = (bf16[32,8192]{1,0:T(8,128)(2,1)}, bf16[32,8192]{1,0:T(8,128)(2,1)}, u32[]{:S(2)}, u32[]{:S(2)}) collective-permute-start(bf16[32,8192]{1,0:T(8,128)(2,1)} %add_convert_fusion.refs_11_), channel_id=1, source_target_pairs={{0,8},{2,10},{4,12},{6,14},{8,0},{10,2},{12,4},{14,6},{16,24},{18,... | collective-permute-start | bytes 1572872 | tf_op jit(solution)/shard_map/ppermute | solution.py:18
  90.2 22.8 %collective-permute-start.23 = (bf16[32,5120]{1,0:T(8,128)(2,1)}, bf16[32,5120]{1,0:T(8,128)(2,1)}, u32[]{:S(2)}, u32[]{:S(2)}) collective-permute-start(bf16[32,5120]{1,0:T(8,128)(2,1)} %collective-permute-done.15.refs_5_.refs_8_), channel_id=1, source_target_pairs={{0,2},{2,0},{4,6},{6,4},{8,10},{10,8},{12,14},{14,12},{16,18},{18,... | collective-permute-start | bytes 983048 | tf_op jit(solution)/shard_map/ppermute | solution.py:18
  104.9 26.1 %collective-permute-start.21 = (bf16[128,3072]{1,0:T(8,128)(2,1)}, bf16[128,3072]{1,0:T(8,128)(2,1)}, u32[]{:S(2)}, u32[]{:S(2)}) collective-permute-start(bf16[128,3072]{1,0:T(8,128)(2,1)} %pad_maximum_fusion.3), channel_id=1, source_target_pairs={{0,4},{2,6},{4,0},{6,2},{8,12},{10,14},{12,8},{14,10},{16,20},{18,... | collective-permute-start | bytes 2359304 | tf_op jit(solution)/shard_map/ppermute | solution.py:18
  106.3 34.7 %collective-permute-start.20 = (bf16[128,1024]{1,0:T(8,128)(2,1)}, bf16[128,1024]{1,0:T(8,128)(2,1)}, u32[]{:S(2)}, u32[]{:S(2)}) collective-permute-start(bf16[128,1024]{1,0:T(8,128)(2,1)} %get-tuple-element.69.refs_16_), channel_id=1, source_target_pairs={{0,1},{1,0},{2,3},{3,2},{4,5},{5,4},{6,7},{7,6},{8,9},{9,8},{10,11... | collective-permute-start | bytes 786440 | tf_op jit(solution)/shard_map/ppermute | solution.py:18
  106.9 6.2 %collective-permute-start.24 = (bf16[96,5120]{1,0:T(8,128)(2,1)}, bf16[96,5120]{1,0:T(8,128)(2,1)}, u32[]{:S(2)}, u32[]{:S(2)}) collective-permute-start(bf16[96,5120]{1,0:T(8,128)(2,1)} %shard_map.64.refs_9_), channel_id=1, source_target_pairs={{0,2},{2,0},{4,6},{6,4},{8,10},{10,8},{12,14},{14,12},{16,18},{18,... | collective-permute-start | bytes 2949128 | tf_op jit(solution)/shard_map/ppermute | solution.py:18
  110.4 26.8 %collective-permute-start.29 = (bf16[32,8192]{1,0:T(8,128)(2,1)}, bf16[32,8192]{1,0:T(8,128)(2,1)}, u32[]{:S(2)}, u32[]{:S(2)}) collective-permute-start(bf16[32,8192]{1,0:T(8,128)(2,1)} %get-tuple-element.81), channel_id=1, source_target_pairs={{0,16},{2,18},{4,20},{6,22},{8,24},{10,26},{12,28},{14,30},{16,0},... | collective-permute-start | bytes 1572872 | tf_op jit(solution)/shard_map/ppermute | solution.py:18
  130.9 10.1 %collective-permute-start.28 = (bf16[128,3072]{1,0:T(8,128)(2,1)}, bf16[128,3072]{1,0:T(8,128)(2,1)}, u32[]{:S(2)}, u32[]{:S(2)}) collective-permute-start(bf16[128,3072]{1,0:T(8,128)(2,1)} %shard_map.66.refs_0_.refs_8_), channel_id=1, source_target_pairs={{0,2},{2,0},{4,6},{6,4},{8,10},{10,8},{12,14},{14,12},{16,18},{18,... | collective-permute-start | bytes 2359304 | tf_op jit(solution)/shard_map/ppermute | solution.py:18
  139.5 15.3 %collective-permute-start.31 = (bf16[32,8192]{1,0:T(8,128)(2,1)}, bf16[32,8192]{1,0:T(8,128)(2,1)}, u32[]{:S(2)}, u32[]{:S(2)}) collective-permute-start(bf16[32,8192]{1,0:T(8,128)(2,1)} %get-tuple-element.79), channel_id=1, source_target_pairs={{0,1},{1,0},{2,3},{3,2},{4,5},{5,4},{6,7},{7,6},{8,9},{9,8},{10,11... | collective-permute-start | bytes 1572872 | tf_op jit(solution)/shard_map/ppermute | solution.py:18
  147.4 15.2 %collective-permute-start.30 = (bf16[128,1024]{1,0:T(8,128)(2,1)}, bf16[128,1024]{1,0:T(8,128)(2,1)}, u32[]{:S(2)}, u32[]{:S(2)}) collective-permute-start(bf16[128,1024]{1,0:T(8,128)(2,1)} %get-tuple-element.77.refs_13_), channel_id=1, source_target_pairs={{0,1},{1,0},{2,3},{3,2},{4,5},{5,4},{6,7},{7,6},{8,9},{9,8},{10,11... | collective-permute-start | bytes 786440 | tf_op jit(solution)/shard_map/ppermute | solution.py:18
  (10 other events, 38.6 us)

commit v5 on v4

--- a/solution.py
+++ b/solution.py
@@ -556,15 +556,10 @@
     )
     shares = [result[0]] + [swap(result[q], "tensor", q) for q in range(1, tensor)]
     held = [here, core, [arrived[1]], [arrived_core[1]]]
-    part = size * 2 // 3 // LANES * LANES
     (weight_grad,) = product(
-        chain, held, grads, weight, start, part, inner, into=weight_grad, grad=True, origin=start
+        chain, held, grads, weight, start, size, inner, into=weight_grad, grad=True
     )
     (in_grad,) = rotate(chain, [final], top_bits, factor)
-    (weight_grad,) = product(
-        chain, held, grads, weight, start + part, size - part, inner, into=weight_grad, grad=True,
-        origin=start,
-    )
     outputs = finish(chain, [early, shares], rows, low_bits)
     return (outputs, in_grad, weight_grad)
 

time: 166 us -> 162 us (0.976)
  Pallas kernels: 78.9 us -> 76.1 us
  local copies, waits for them, and re-layouts: 7.74 us -> 5.51 us
    pallas_call x10 -> x9, Pallas kernels: 78.9 us -> 76.1 us  [__call__(): pl.pallas_call(kernel, grid=(steps,), in_specs=[pl.BlockSpec(memory_space...]
  transfers between devices with their start and end apart: 32 -> 32, of which waited for: 11 -> 11; matrix products, arithmetic and copies ran while one was open for 14% -> 13% of each run, Pallas kernels for 44% -> 43%
where the time goes in v5:
time: 162 us; the launch traced here: 161 us
  Pallas kernels  76.1 us (47%)
  waiting for transfers between devices  35.9 us (22%)
  starting transfers between devices  25.7 us (16%)
  other arithmetic  16.9 us (10%)
  local copies, waits for them, and re-layouts  5.51 us (3%)
    pallas_call x9, Pallas kernels, __call__(): pl.pallas_call(kernel, grid=(steps,), in_specs=[pl.BlockSpec(memory_space...  76.1 us
    ppermute x32, waiting for transfers between devices, swap(): lax.ppermute(values, axis, [(i, i ^ mask) for i in range(lax.axis_size(ax...  35.9 us
    ppermute x32, starting transfers between devices, swap(): lax.ppermute(values, axis, [(i, i ^ mask) for i in range(lax.axis_size(ax...  25.7 us
    convert_element_type x4, other arithmetic, split_send(): add(*t).astype(BF16)  6.43 us
    slice x7, local copies, waits for them, and re-layouts, per_device(): block[:, start:start + size]  4.59 us
    convert_element_type x1, other arithmetic, per_device(): some[j + count].astype(BF16)  3.38 us
  transfers between devices with their start and end apart: 32, of which 11 were waited for; matrix products, arithmetic and copies ran while one was open for 13% of the time, Pallas kernels for 43%

profile of v5, /device:TPU:0, one launch (start us, length us, event | category | flops | bytes accessed | tf_op | source)
XLA Modules:
  0.0 161.1 jit_solution(13028541348741790411)
XLA Ops:
  0.6 3.0 %collective-permute-start = (bf16[32,8192]{1,0:T(8,128)(2,1)}, bf16[32,8192]{1,0:T(8,128)(2,1)}, u32[]{:S(2)}, u32[]{:S(2)}) collective-permute-start(bf16[32,8192]{1,0:T(8,128)(2,1)} %refs_0_.3), channel_id=1, source_target_pairs={{0,1},{1,0},{2,3},{3,2},{4,5},{5,4},{6,7},{7,6},{8,9},{9,8},{10,11... | collective-permute-start | bytes 1572872 | tf_op jit(solution)/shard_map/ppermute | solution.py:18
  4.2 10.6 %shard_map.58 = (bf16[32,8192]{1,0:T(8,128)(2,1)}, bf16[32,8192]{1,0:T(8,128)(2,1)}, bf16[32,8192]{1,0:T(8,128)(2,1)}, bf16[32,8192]{1,0:T(8,128)(2,1)}, bf16[32...) custom-call(s32[3]{0:T(128)} %pad_add_fusion.place, ...), custom_call_target="tpu_custom_call" | custom-call | flops 4294967296 | bytes 22020096 | tf_op jit(solution)/shard_map/pallas_call | solution.py:69
  17.9 4.2 %shard_map.59 = (bf16[32,8192]{1,0:T(8,128)(2,1)}, bf16[32,8192]{1,0:T(8,128)(2,1)}, bf16[64,8192]{1,0:T(8,128)(2,1)}, bf16[32,5120]{1,0:T(8,128)(2,1)}) custom-call(s32[3]{0:T(128)} %pad_add_fusion.place, bf16[32,8192]{1,0:T(8,128)(2,1)} %refs_0_.3, bf16[32,8192]{1,0:T(8,128)(2,1)} %collective-permute-done.refs_1_, ...), custom_call_target="tpu_custom_call" | custom-call | flops 201326592 | bytes 5570560 | tf_op jit(solution)/shard_map/pallas_call | solution.py:69
  22.1 1.5 collective-permute-start.9
  24.1 2.6 %collective-permute-start.6 = (bf16[32,8192]{1,0:T(8,128)(2,1)}, bf16[32,8192]{1,0:T(8,128)(2,1)}, u32[]{:S(2)}, u32[]{:S(2)}) collective-permute-start(bf16[32,8192]{1,0:T(8,128)(2,1)} %get-tuple-element.49), channel_id=1, source_target_pairs={{0,16},{2,18},{4,20},{6,22},{8,24},{10,26},{12,28},{14,30},{16,0},... | collective-permute-start | bytes 1572872 | tf_op jit(solution)/shard_map/ppermute | solution.py:18
  26.7 1.6 collective-permute-start.5
  28.3 9.3 %collective-permute-done.7.refs_0_.refs_13_.refs_11_ = bf16[256,1024]{1,0:T(8,128)(2,1)} collective-permute-done((bf16[256,1024]{1,0:T(8,128)(2,1)}, bf16[256,1024]{1,0:T(8,128)(2,1)}, u32[]{:S(2)}, u32[]{:S(2)}) %collective-permute-start.7) | collective-permute-done | bytes 524320 | tf_op jit(solution)/shard_map/ppermute | solution.py:18
  38.1 10.3 %shard_map.60 = (bf16[32,8192]{1,0:T(8,128)(2,1)}, bf16[32,8192]{1,0:T(8,128)(2,1)}, bf16[32,8192]{1,0:T(8,128)(2,1)}, bf16[32,8192]{1,0:T(8,128)(2,1)}, bf16[32...) custom-call(s32[3]{0:T(128)} %pad_add_fusion.place, ...), custom_call_target="tpu_custom_call", output_to_operand_aliasing={{8}: (3, {}), {9}: (4, {})} | custom-call | flops 4294967296 | bytes 21495808 | tf_op jit(solution)/shard_map/pallas_call | solution.py:69
  49.0 1.5 add_convert_fusion.3
  52.2 1.2 collective-permute-start.10
  53.4 1.3 collective-permute-done.15.refs_5_.refs_8_
  54.6 1.2 add_convert_fusion.2
  55.8 1.4 add_convert_fusion.1
  58.3 1.5 collective-permute-start.19
  62.5 1.6 slice.60
  65.1 11.9 %collective-permute-done.10 = bf16[64,8192]{1,0:T(8,128)(2,1)S(1)} collective-permute-done((bf16[64,8192]{1,0:T(8,128)(2,1)S(1)}, bf16[64,8192]{1,0:T(8,128)(2,1)S(1)}, u32[]{:S(2)}, u32[]{:S(2)}) %collective-permute-start.10) | collective-permute-done | bytes 1048608 | tf_op jit(solution)/shard_map/ppermute | solution.py:18
  78.2 1.6 collective-permute-start.22
  79.7 4.5 %collective-permute-done.19 = bf16[64,8192]{1,0:T(8,128)(2,1)} collective-permute-done((bf16[64,8192]{1,0:T(8,128)(2,1)}, bf16[64,8192]{1,0:T(8,128)(2,1)}, u32[]{:S(2)}, u32[]{:S(2)}) %collective-permute-start.19) | collective-permute-done | bytes 1048608 | tf_op jit(solution)/shard_map/ppermute | solution.py:18
  84.2 2.3 %add_convert_fusion.refs_11_ = bf16[32,8192]{1,0:T(8,128)(2,1)} fusion(bf16[32,8192]{1,0:T(8,128)(2,1)} %collective-permute-done.16, bf16[32,8192]{1,0:T(8,128)(2,1)} %get-tuple-element.63, bf16[64,8192]{1,0:T(8,128)(2,1)} %collective-permute-done.19), kind=kLoop, calls=%fused_computation.6 | loop fusion | flops 1572864 | bytes 2097152 | tf_op jit(solution)/shard_map/convert_element_type | solution.py:448
  87.3 1.6 collective-permute-start.26
  90.9 12.6 %shard_map.63 = (f32[128,1024]{1,0:T(8,128)}, bf16[128,1024]{1,0:T(8,128)(2,1)}) custom-call(s32[3]{0:T(128)} %pad_add_fusion.place, bf16[32,8192]{1,0:T(8,128)(2,1)} %get-tuple-element.48.refs_0_, bf16[32,8192]{1,0:T(8,128)(2,1)} %collective-permute-done.5.refs_1_, bf16[32,8192]{1,0:T(8,128)(2,1)} %collective-permute-done.6.refs_2_, ...), custom_call_target="tpu_custom_call" | custom-call | flops 4294967296 | bytes 21757952 | tf_op jit(solution)/shard_map/pallas_call | solution.py:69
  104.0 1.5 collective-permute-start.21
  106.1 3.4 %select_convert_fusion = (bf16[32,8192]{1,0:T(8,128)(2,1)}, f32[32,8192]{1,0:T(8,128)}) fusion(pred[]{:T(512)S(6)} %eq.3, bf16[32,8192]{1,0:T(8,128)(2,1)} %collective-permute-done.26, bf16[64,8192]{1,0:T(8,128)(2,1)} %collective-permute-done.19, bf16[32,8192]{1,0:T(8,128)(2,1)} %collective-permute-done.25, bf16[32,8192]{1,0:T(8,128)(2,1)S(1)} %copy-done.1, ...), kind=kLoop, calls=%fused_computation.3 | loop fusion | flops 4456448 | bytes 5767169 | tf_op jit(solution)/shard_map/convert_element_type | solution.py:534
  109.5 2.6 %collective-permute-start.29 = (bf16[32,8192]{1,0:T(8,128)(2,1)}, bf16[32,8192]{1,0:T(8,128)(2,1)}, u32[]{:S(2)}, u32[]{:S(2)}) collective-permute-start(bf16[32,8192]{1,0:T(8,128)(2,1)} %get-tuple-element.81), channel_id=1, source_target_pairs={{0,16},{2,18},{4,20},{6,22},{8,24},{10,26},{12,28},{14,30},{16,0},... | collective-permute-start | bytes 1572872 | tf_op jit(solution)/shard_map/ppermute | solution.py:18
  112.1 17.8 %shard_map.65 = (f32[8192,1024]{1,0:T(8,128)}, f32[256,1024]{1,0:T(8,128)}, f32[32,8192]{1,0:T(8,128)}) custom-call(s32[3]{0:T(128)} %pad_add_fusion.place, bf16[32,8192]{1,0:T(8,128)(2,1)} %get-tuple-element.48.refs_0_, bf16[32,8192]{1,0:T(8,128)(2,1)} %collective-permute-done.5.refs_1_, ...), custom_call_target="tpu_custom_call", output_to_operand_aliasing={{2}: (16, {})} | custom-call | flops 8053063680 | bytes 59244544 | tf_op jit(solution)/shard_map/pallas_call | solution.py:69
  130.2 6.0 %collective-permute-done.29 = bf16[32,8192]{1,0:T(8,128)(2,1)} collective-permute-done((bf16[32,8192]{1,0:T(8,128)(2,1)}, bf16[32,8192]{1,0:T(8,128)(2,1)}, u32[]{:S(2)}, u32[]{:S(2)}) %collective-permute-start.29) | collective-permute-done | bytes 524320 | tf_op jit(solution)/shard_map/ppermute | solution.py:18
  136.3 2.3 %fusion = (bf16[32,8192]{1,0:T(8,128)(2,1)}, f32[32,8192]{1,0:T(8,128)}) fusion(f32[32,8192]{1,0:T(8,128)S(1)} %copy-done.3, bf16[32,8192]{1,0:T(8,128)(2,1)} %collective-permute-done.29), kind=kLoop, calls=%fused_computation.14 | loop fusion | flops 786432 | bytes 3145728 | tf_op jit(solution)/shard_map/convert_element_type | solution.py:187
  138.6 1.5 collective-permute-start.31
  140.1 6.5 %shard_map.67 = (f32[128,1024]{1,0:T(8,128)}, bf16[128,1024]{1,0:T(8,128)(2,1)}) custom-call(s32[3]{0:T(128)} %pad_add_fusion.place, bf16[128,3072]{1,0:T(8,128)(2,1)} %shard_map.66.refs_0_.refs_8_, bf16[128,3072]{1,0:T(8,128)(2,1)} %collective-permute-done.28.refs_1_.refs_9_, bf16[8192,1024]{1,0:T(8,128)(2,1)} %refs_2_.1, ...), custom_call_target="tpu_custom_call" | custom-call | flops 1610612736 | bytes 20185088 | tf_op jit(solution)/shard_map/pallas_call | solution.py:69
  147.1 8.9 %shard_map.68.refs_2_ = f32[8192,1024]{1,0:T(8,128)} custom-call(s32[3]{0:T(128)} %pad_add_fusion.place, bf16[32,8192]{1,0:T(8,128)(2,1)} %get-tuple-element.48.refs_0_, bf16[32,8192]{1,0:T(8,128)(2,1)} %collective-permute-done.5.refs_1_, bf16[32,8192]{1,0:T(8,128)(2,1)} %collective-permute-done.6.refs_2_, ...), custom_call_target="tpu_custom_call", output_to_operand_aliasing={{}: (13, {})} | custom-call | flops 3221225472 | bytes 73924608 | tf_op jit(solution)/shard_map/pallas_call | solution.py:69
  155.9 3.0 %shard_map.69.refs_4_ = bf16[32,8192]{1,0:T(8,128)(2,1)} custom-call(s32[3]{0:T(128)} %pad_add_fusion.place, f32[32,8192]{1,0:T(8,128)} %get-tuple-element.80.refs_5_.refs_0_, bf16[32,8192]{1,0:T(8,128)(2,1)} %collective-permute-done.31.refs_1_, f32[8192,1024]{1,0:T(8,128)} %shard_map.68.refs_2_), custom_call_target="tpu_custom_call" | custom-call | flops 201326592 | bytes 2097152 | tf_op jit(solution)/shard_map/pallas_call | solution.py:69
  158.9 2.2 %shard_map.70 = bf16[256,1024]{1,0:T(8,128)(2,1)} custom-call(s32[3]{0:T(128)} %pad_add_fusion.place, f32[128,1024]{1,0:T(8,128)} %get-tuple-element.68.refs_1_.refs_0_, bf16[128,1024]{1,0:T(8,128)(2,1)} %collective-permute-done.20.refs_6_.refs_1_, f32[128,1024]{1,0:T(8,128)} %get-tuple-element.76.refs_2_, ...), custom_call_target="tpu_custom_call" | custom-call | bytes 2097152 | tf_op jit(solution)/shard_map/pallas_call | solution.py:69
  (88 shorter events, 17.3 us)
Async XLA Ops:
  0.6 17.3 %collective-permute-start = (bf16[32,8192]{1,0:T(8,128)(2,1)}, bf16[32,8192]{1,0:T(8,128)(2,1)}, u32[]{:S(2)}, u32[]{:S(2)}) collective-permute-start(bf16[32,8192]{1,0:T(8,128)(2,1)} %refs_0_.3), channel_id=1, source_target_pairs={{0,1},{1,0},{2,3},{3,2},{4,5},{5,4},{6,7},{7,6},{8,9},{9,8},{10,11... | collective-permute-start | bytes 1572872 | tf_op jit(solution)/shard_map/ppermute | solution.py:18
  14.9 1.9 %collective-permute-start.1 = (bf16[32,4096]{1,0:T(8,128)(2,1)}, bf16[32,4096]{1,0:T(8,128)(2,1)}, u32[]{:S(2)}, u32[]{:S(2)}) collective-permute-start(bf16[32,4096]{1,0:T(8,128)(2,1)} %get-tuple-element.42), channel_id=1, source_target_pairs={{0,2},{2,0},{4,6},{6,4},{8,10},{10,8},{12,14},{14,12},{16,18},{18,... | collective-permute-start | bytes 786440 | tf_op jit(solution)/shard_map/ppermute | solution.py:18
  14.9 2.2 %collective-permute-start.2 = (bf16[32,4096]{1,0:T(8,128)(2,1)}, bf16[32,4096]{1,0:T(8,128)(2,1)}, u32[]{:S(2)}, u32[]{:S(2)}) collective-permute-start(bf16[32,4096]{1,0:T(8,128)(2,1)} %get-tuple-element.43), channel_id=1, source_target_pairs={{0,2},{2,0},{4,6},{6,4},{8,10},{10,8},{12,14},{14,12},{16,18},{18,... | collective-permute-start | bytes 786440 | tf_op jit(solution)/shard_map/ppermute | solution.py:18
  15.4 2.1 %collective-permute-start.3 = (bf16[32,4096]{1,0:T(8,128)(2,1)}, bf16[32,4096]{1,0:T(8,128)(2,1)}, u32[]{:S(2)}, u32[]{:S(2)}) collective-permute-start(bf16[32,4096]{1,0:T(8,128)(2,1)} %get-tuple-element.45), channel_id=1, source_target_pairs={{0,2},{2,0},{4,6},{6,4},{8,10},{10,8},{12,14},{14,12},{16,18},{18,... | collective-permute-start | bytes 786440 | tf_op jit(solution)/shard_map/ppermute | solution.py:18
  15.5 2.4 %collective-permute-start.4 = (bf16[32,4096]{1,0:T(8,128)(2,1)}, bf16[32,4096]{1,0:T(8,128)(2,1)}, u32[]{:S(2)}, u32[]{:S(2)}) collective-permute-start(bf16[32,4096]{1,0:T(8,128)(2,1)} %get-tuple-element.46), channel_id=1, source_target_pairs={{0,2},{2,0},{4,6},{6,4},{8,10},{10,8},{12,14},{14,12},{16,18},{18,... | collective-permute-start | bytes 786440 | tf_op jit(solution)/shard_map/ppermute | solution.py:18
  22.1 26.4 %collective-permute-start.9 = (bf16[64,8192]{1,0:T(8,128)(2,1)}, bf16[64,8192]{1,0:T(8,128)(2,1)}, u32[]{:S(2)}, u32[]{:S(2)}) collective-permute-start(bf16[64,8192]{1,0:T(8,128)(2,1)} %get-tuple-element.55), channel_id=1, source_target_pairs={{0,4},{2,6},{4,0},{6,2},{8,12},{10,14},{12,8},{14,10},{16,20},{18,... | collective-permute-start | bytes 3145736 | tf_op jit(solution)/shard_map/ppermute | solution.py:18
  23.6 14.0 %collective-permute-start.7 = (bf16[256,1024]{1,0:T(8,128)(2,1)}, bf16[256,1024]{1,0:T(8,128)(2,1)}, u32[]{:S(2)}, u32[]{:S(2)}) collective-permute-start(bf16[256,1024]{1,0:T(8,128)(2,1)} %get-tuple-element.47.refs_8_.refs_12_.refs_10_), channel_id=1, source_target_pairs={{0,1},{1,0},{2,3},{3,2},{4,5},{5,4},{6,7},{7,6},{8,9},{9,8},{10,11... | collective-permute-start | bytes 1572872 | tf_op jit(solution)/shard_map/ppermute | solution.py:18
  24.1 24.3 %collective-permute-start.8 = (bf16[32,8192]{1,0:T(8,128)(2,1)}, bf16[32,8192]{1,0:T(8,128)(2,1)}, u32[]{:S(2)}, u32[]{:S(2)}) collective-permute-start(bf16[32,8192]{1,0:T(8,128)(2,1)} %get-tuple-element.54), channel_id=1, source_target_pairs={{0,2},{2,0},{4,6},{6,4},{8,10},{10,8},{12,14},{14,12},{16,18},{18,... | collective-permute-start | bytes 1572872 | tf_op jit(solution)/shard_map/ppermute | solution.py:18
  24.1 26.9 %collective-permute-start.6 = (bf16[32,8192]{1,0:T(8,128)(2,1)}, bf16[32,8192]{1,0:T(8,128)(2,1)}, u32[]{:S(2)}, u32[]{:S(2)}) collective-permute-start(bf16[32,8192]{1,0:T(8,128)(2,1)} %get-tuple-element.49), channel_id=1, source_target_pairs={{0,16},{2,18},{4,20},{6,22},{8,24},{10,26},{12,28},{14,30},{16,0},... | collective-permute-start | bytes 1572872 | tf_op jit(solution)/shard_map/ppermute | solution.py:18
  26.7 35.6 %collective-permute-start.5 = (bf16[32,8192]{1,0:T(8,128)(2,1)}, bf16[32,8192]{1,0:T(8,128)(2,1)}, u32[]{:S(2)}, u32[]{:S(2)}) collective-permute-start(bf16[32,8192]{1,0:T(8,128)(2,1)} %get-tuple-element.49), channel_id=1, source_target_pairs={{0,8},{2,10},{4,12},{6,14},{8,0},{10,2},{12,4},{14,6},{16,24},{18,... | collective-permute-start | bytes 1572872 | tf_op jit(solution)/shard_map/ppermute | solution.py:18
  37.6 17.0 %collective-permute-start.15 = (bf16[32,5120]{1,0:T(8,128)(2,1)}, bf16[32,5120]{1,0:T(8,128)(2,1)}, u32[]{:S(2)}, u32[]{:S(2)}) collective-permute-start(bf16[32,5120]{1,0:T(8,128)(2,1)} %get-tuple-element.52.refs_4_), channel_id=1, source_target_pairs={{0,4},{2,6},{4,0},{6,2},{8,12},{10,14},{12,8},{14,10},{16,20},{18,... | collective-permute-start | bytes 983048 | tf_op jit(solution)/shard_map/ppermute | solution.py:18
  48.5 6.2 %collective-permute-start.17 = (bf16[32,8192]{1,0:T(8,128)(2,1)}, bf16[32,8192]{1,0:T(8,128)(2,1)S(1)}, u32[]{:S(2)}, u32[]{:S(2)}) collective-permute-start(bf16[32,8192]{1,0:T(8,128)(2,1)} %get-tuple-element.66), channel_id=1, source_target_pairs={{0,2},{2,0},{4,6},{6,4},{8,10},{10,8},{12,14},{14,12},{16,18},{18,... | collective-permute-start | bytes 1572872 | tf_op jit(solution)/shard_map/ppermute | solution.py:18
  48.6 7.3 %collective-permute-start.18 = (bf16[32,8192]{1,0:T(8,128)(2,1)}, bf16[32,8192]{1,0:T(8,128)(2,1)}, u32[]{:S(2)}, u32[]{:S(2)}) collective-permute-start(bf16[32,8192]{1,0:T(8,128)(2,1)} %get-tuple-element.56.refs_9_), channel_id=1, source_target_pairs={{0,2},{2,0},{4,6},{6,4},{8,10},{10,8},{12,14},{14,12},{16,18},{18,... | collective-permute-start | bytes 1572872 | tf_op jit(solution)/shard_map/ppermute | solution.py:18
  52.2 24.8 %collective-permute-start.10 = (bf16[64,8192]{1,0:T(8,128)(2,1)S(1)}, bf16[64,8192]{1,0:T(8,128)(2,1)S(1)}, u32[]{:S(2)}, u32[]{:S(2)}) collective-permute-start(bf16[64,8192]{1,0:T(8,128)(2,1)S(1)} %pad_maximum_fusion.refs_4_), channel_id=1, source_target_pairs={{0,8},{2,10},{4,12},{6,14},{8,0},{10,2},{12,4},{14,6},{16,24},{18,... | collective-permute-start | bytes 3145736 | tf_op jit(solution)/shard_map/ppermute | solution.py:18
  58.3 26.0 %collective-permute-start.19 = (bf16[64,8192]{1,0:T(8,128)(2,1)}, bf16[64,8192]{1,0:T(8,128)(2,1)}, u32[]{:S(2)}, u32[]{:S(2)}) collective-permute-start(bf16[64,8192]{1,0:T(8,128)(2,1)} %pad_maximum_fusion.1), channel_id=1, source_target_pairs={{0,4},{2,6},{4,0},{6,2},{8,12},{10,14},{12,8},{14,10},{16,20},{18,... | collective-permute-start | bytes 3145736 | tf_op jit(solution)/shard_map/ppermute | solution.py:18
  59.8 26.8 %collective-permute-start.11 = (bf16[32,8192]{1,0:T(8,128)(2,1)S(1)}, bf16[32,8192]{1,0:T(8,128)(2,1)S(1)}, u32[]{:S(2)}, u32[]{:S(2)}) collective-permute-start(bf16[32,8192]{1,0:T(8,128)(2,1)S(1)} %copy-done.4), channel_id=1, source_target_pairs={{0,2},{2,0},{4,6},{6,4},{8,10},{10,8},{12,14},{14,12},{16,18},{18,... | collective-permute-start | bytes 1572872 | tf_op jit(solution)/shard_map/ppermute | solution.py:18
  59.9 18.3 %collective-permute-start.16 = (bf16[32,8192]{1,0:T(8,128)(2,1)}, bf16[32,8192]{1,0:T(8,128)(2,1)}, u32[]{:S(2)}, u32[]{:S(2)}) collective-permute-start(bf16[32,8192]{1,0:T(8,128)(2,1)} %get-tuple-element.64), channel_id=1, source_target_pairs={{0,2},{2,0},{4,6},{6,4},{8,10},{10,8},{12,14},{14,12},{16,18},{18,... | collective-permute-start | bytes 1572872 | tf_op jit(solution)/shard_map/ppermute | solution.py:18
  62.3 24.9 %collective-permute-start.13 = (bf16[32,8192]{1,0:T(8,128)(2,1)}, bf16[32,8192]{1,0:T(8,128)(2,1)}, u32[]{:S(2)}, u32[]{:S(2)}) collective-permute-start(bf16[32,8192]{1,0:T(8,128)(2,1)} %collective-permute-done.6.refs_2_), channel_id=1, source_target_pairs={{0,2},{2,0},{4,6},{6,4},{8,10},{10,8},{12,14},{14,12},{16,18},{18,... | collective-permute-start | bytes 1572872 | tf_op jit(solution)/shard_map/ppermute | solution.py:18
  77.0 10.3 %collective-permute-start.12 = (bf16[32,8192]{1,0:T(8,128)(2,1)}, bf16[32,8192]{1,0:T(8,128)(2,1)S(1)}, u32[]{:S(2)}, u32[]{:S(2)}) collective-permute-start(bf16[32,8192]{1,0:T(8,128)(2,1)} %collective-permute-done.5.refs_1_), channel_id=1, source_target_pairs={{0,2},{2,0},{4,6},{6,4},{8,10},{10,8},{12,14},{14,12},{16,18},{18,... | collective-permute-start | bytes 1572872 | tf_op jit(solution)/shard_map/ppermute | solution.py:18
  78.2 25.8 %collective-permute-start.22 = (bf16[96,5120]{1,0:T(8,128)(2,1)}, bf16[96,5120]{1,0:T(8,128)(2,1)}, u32[]{:S(2)}, u32[]{:S(2)}) collective-permute-start(bf16[96,5120]{1,0:T(8,128)(2,1)} %pad_maximum_fusion.2.refs_2_.refs_10_), channel_id=1, source_target_pairs={{0,4},{2,6},{4,0},{6,2},{8,12},{10,14},{12,8},{14,10},{16,20},{18,... | collective-permute-start | bytes 2949128 | tf_op jit(solution)/shard_map/ppermute | solution.py:18
  84.2 5.6 %collective-permute-start.14 = (bf16[32,8192]{1,0:T(8,128)(2,1)S(1)}, bf16[32,8192]{1,0:T(8,128)(2,1)S(1)}, u32[]{:S(2)}, u32[]{:S(2)}) collective-permute-start(bf16[32,8192]{1,0:T(8,128)(2,1)S(1)} %slice.55.refs_3_), channel_id=1, source_target_pairs={{0,2},{2,0},{4,6},{6,4},{8,10},{10,8},{12,14},{14,12},{16,18},{18,... | collective-permute-start | bytes 1572872 | tf_op jit(solution)/shard_map/ppermute | solution.py:18
  86.6 18.9 %collective-permute-start.27 = (bf16[32,8192]{1,0:T(8,128)(2,1)}, bf16[32,8192]{1,0:T(8,128)(2,1)}, u32[]{:S(2)}, u32[]{:S(2)}) collective-permute-start(bf16[32,8192]{1,0:T(8,128)(2,1)} %get-tuple-element.73), channel_id=1, source_target_pairs={{0,2},{2,0},{4,6},{6,4},{8,10},{10,8},{12,14},{14,12},{16,18},{18,... | collective-permute-start | bytes 1572872 | tf_op jit(solution)/shard_map/ppermute | solution.py:18
  87.2 18.9 %collective-permute-start.25 = (bf16[32,8192]{1,0:T(8,128)(2,1)}, bf16[32,8192]{1,0:T(8,128)(2,1)}, u32[]{:S(2)}, u32[]{:S(2)}) collective-permute-start(bf16[32,8192]{1,0:T(8,128)(2,1)} %get-tuple-element.71), channel_id=1, source_target_pairs={{0,2},{2,0},{4,6},{6,4},{8,10},{10,8},{12,14},{14,12},{16,18},{18,... | collective-permute-start | bytes 1572872 | tf_op jit(solution)/shard_map/ppermute | solution.py:18
  87.3 18.8 %collective-permute-start.26 = (bf16[32,8192]{1,0:T(8,128)(2,1)}, bf16[32,8192]{1,0:T(8,128)(2,1)}, u32[]{:S(2)}, u32[]{:S(2)}) collective-permute-start(bf16[32,8192]{1,0:T(8,128)(2,1)} %add_convert_fusion.refs_11_), channel_id=1, source_target_pairs={{0,8},{2,10},{4,12},{6,14},{8,0},{10,2},{12,4},{14,6},{16,24},{18,... | collective-permute-start | bytes 1572872 | tf_op jit(solution)/shard_map/ppermute | solution.py:18
  90.7 21.4 %collective-permute-start.23 = (bf16[32,5120]{1,0:T(8,128)(2,1)}, bf16[32,5120]{1,0:T(8,128)(2,1)}, u32[]{:S(2)}, u32[]{:S(2)}) collective-permute-start(bf16[32,5120]{1,0:T(8,128)(2,1)} %collective-permute-done.15.refs_5_.refs_8_), channel_id=1, source_target_pairs={{0,2},{2,0},{4,6},{6,4},{8,10},{10,8},{12,14},{14,12},{16,18},{18,... | collective-permute-start | bytes 983048 | tf_op jit(solution)/shard_map/ppermute | solution.py:18
  104.0 25.9 %collective-permute-start.21 = (bf16[128,3072]{1,0:T(8,128)(2,1)}, bf16[128,3072]{1,0:T(8,128)(2,1)}, u32[]{:S(2)}, u32[]{:S(2)}) collective-permute-start(bf16[128,3072]{1,0:T(8,128)(2,1)} %pad_maximum_fusion.3), channel_id=1, source_target_pairs={{0,4},{2,6},{4,0},{6,2},{8,12},{10,14},{12,8},{14,10},{16,20},{18,... | collective-permute-start | bytes 2359304 | tf_op jit(solution)/shard_map/ppermute | solution.py:18
  105.5 34.5 %collective-permute-start.20 = (bf16[128,1024]{1,0:T(8,128)(2,1)}, bf16[128,1024]{1,0:T(8,128)(2,1)}, u32[]{:S(2)}, u32[]{:S(2)}) collective-permute-start(bf16[128,1024]{1,0:T(8,128)(2,1)} %get-tuple-element.69.refs_16_), channel_id=1, source_target_pairs={{0,1},{1,0},{2,3},{3,2},{4,5},{5,4},{6,7},{7,6},{8,9},{9,8},{10,11... | collective-permute-start | bytes 786440 | tf_op jit(solution)/shard_map/ppermute | solution.py:18
  106.1 6.0 %collective-permute-start.24 = (bf16[96,5120]{1,0:T(8,128)(2,1)}, bf16[96,5120]{1,0:T(8,128)(2,1)}, u32[]{:S(2)}, u32[]{:S(2)}) collective-permute-start(bf16[96,5120]{1,0:T(8,128)(2,1)} %shard_map.64.refs_9_), channel_id=1, source_target_pairs={{0,2},{2,0},{4,6},{6,4},{8,10},{10,8},{12,14},{14,12},{16,18},{18,... | collective-permute-start | bytes 2949128 | tf_op jit(solution)/shard_map/ppermute | solution.py:18
  109.5 26.8 %collective-permute-start.29 = (bf16[32,8192]{1,0:T(8,128)(2,1)}, bf16[32,8192]{1,0:T(8,128)(2,1)}, u32[]{:S(2)}, u32[]{:S(2)}) collective-permute-start(bf16[32,8192]{1,0:T(8,128)(2,1)} %get-tuple-element.81), channel_id=1, source_target_pairs={{0,16},{2,18},{4,20},{6,22},{8,24},{10,26},{12,28},{14,30},{16,0},... | collective-permute-start | bytes 1572872 | tf_op jit(solution)/shard_map/ppermute | solution.py:18
  130.0 10.1 %collective-permute-start.28 = (bf16[128,3072]{1,0:T(8,128)(2,1)}, bf16[128,3072]{1,0:T(8,128)(2,1)}, u32[]{:S(2)}, u32[]{:S(2)}) collective-permute-start(bf16[128,3072]{1,0:T(8,128)(2,1)} %shard_map.66.refs_0_.refs_8_), channel_id=1, source_target_pairs={{0,2},{2,0},{4,6},{6,4},{8,10},{10,8},{12,14},{14,12},{16,18},{18,... | collective-permute-start | bytes 2359304 | tf_op jit(solution)/shard_map/ppermute | solution.py:18
  138.6 17.4 %collective-permute-start.31 = (bf16[32,8192]{1,0:T(8,128)(2,1)}, bf16[32,8192]{1,0:T(8,128)(2,1)}, u32[]{:S(2)}, u32[]{:S(2)}) collective-permute-start(bf16[32,8192]{1,0:T(8,128)(2,1)} %get-tuple-element.79), channel_id=1, source_target_pairs={{0,1},{1,0},{2,3},{3,2},{4,5},{5,4},{6,7},{7,6},{8,9},{9,8},{10,11... | collective-permute-start | bytes 1572872 | tf_op jit(solution)/shard_map/ppermute | solution.py:18
  146.5 12.4 %collective-permute-start.30 = (bf16[128,1024]{1,0:T(8,128)(2,1)}, bf16[128,1024]{1,0:T(8,128)(2,1)}, u32[]{:S(2)}, u32[]{:S(2)}) collective-permute-start(bf16[128,1024]{1,0:T(8,128)(2,1)} %get-tuple-element.77.refs_13_), channel_id=1, source_target_pairs={{0,1},{1,0},{2,3},{3,2},{4,5},{5,4},{6,7},{7,6},{8,9},{9,8},{10,11... | collective-permute-start | bytes 786440 | tf_op jit(solution)/shard_map/ppermute | solution.py:18
  (12 other events, 59.3 us)
